TPU v7x, 32 devices: a whole 2x2x4 slice. The times are simulated.
32 devices in a mesh: groups: 2 (over y), gx: 4 (over z), gy: 2 (over x), sa: 2 (over core).
Axes of the slice: x: 2, y: 2, z: 4, core: 2. Of those that a mesh axis runs over, the one named last changes fastest.
Arguments:
- initial: float32 [16, 4, 128, 256], P(('groups', 'sa'), None, 'gx', 'gy'), parts along dimension 0, may hold values from -6 to 6
- retard: float32 [16, 4, 128, 256], P(('groups', 'sa'), None, 'gx', 'gy'), parts along dimension 0, may hold values from 0.2 to 0.4
- velx: float32 [16, 4, 128, 256], P(('groups', 'sa'), None, 'gx', 'gy'), parts along dimension 0, may hold values from 0.2 to 1
- vely: float32 [16, 4, 128, 256], P(('groups', 'sa'), None, 'gx', 'gy'), parts along dimension 0, may hold values from 0.2 to 1
- monitor: float32 [8, 128, 256], P('groups', 'gx', 'gy'), parts along dimension 0, may hold values from 0.2 to 1
- controls: float32 [8192], P('groups'), parts along dimension 0, may hold values from -6 to 6
- profile: float32 [8192, 128], P('groups'), parts along dimension 0, may hold values from -4 to 4
- wells: int32 [8192], P('groups'), parts along dimension 0, may hold values from 0 to 1023
- ranking: int32 [16], P(('groups', 'sa')), parts along dimension 0, may hold values from 0 to 7, as said below
Outputs:
- final: float32 [16, 4, 128, 256], P(('groups', 'sa'), None, 'gx', 'gy'), parts along dimension 0
- gradient: float32 [8192], P('groups'), parts along dimension 0
- objective: float32 [2], P('groups'), parts along dimension 0
There are 2 independent parts, one for each index of `groups`. A program takes and returns all parts, laid end to end along the dimension named above; each array names one. Nothing has to cross between parts.
Inputs may be any that keep to these rules, and one draw needn't show every extreme that they name: ranking holds each number from 0 to 7 once.
All inputs are finite; a program needn't handle non-finite values.
Results may differ from a plain program's by a relative error of at most 0.00009.
Values sent between devices are 32-bit elements; how exact they have to be, the bound alone decides.
No kernel may reach another device: no remote copies, remote signals or barrier semaphores. Data moves between devices by JAX's collectives and lax.ppermute only.
A program may use at most 64 MiB of HBM per device.

v0:
```python
import jax
import jax.numpy as jnp
from jax import lax
from jax.sharding import PartitionSpec as P

ITERS = 16


KAPPA = 0.1
VERT = 0.05


def extended(cells, sides, width):
    for axis, dim in sides:
        count = lax.axis_size(axis)
        ends = count - 1
        head = lax.slice_in_dim(cells, 0, width, axis=dim)
        tail = lax.slice_in_dim(cells, cells.shape[dim] - width, cells.shape[dim], axis=dim)
        cells = jnp.concatenate(
            [
                lax.ppermute(tail, axis, [(i, (i + 1) % count) for i in range(ends)]),
                cells,
                lax.ppermute(head, axis, [((i + 1) % count, i) for i in range(ends)]),
            ],
            axis=dim,
        )
    return cells


def vertical(field):
    padded = jnp.pad(field, ((0, 0), (1, 1), (0, 0), (0, 0)))
    return (padded[:, :-2], padded[:, 2:])


def local(initial, retard, velx, vely, monitor, controls, profile, wells, ranking):
    samples, layers, width_x, width_y = initial.shape
    depth = 1
    x_index = lax.axis_index("gx")
    y_index = lax.axis_index("gy")
    global_x = width_x * lax.axis_size("gx")
    global_y = width_y * lax.axis_size("gy")
    blocks = width_y // 128
    all_blocks = global_y // 128
    pad_x = width_x + 2 * depth
    pad_b = blocks + 2
    layer_ids = lax.broadcasted_iota(jnp.int32, (layers, pad_x, pad_b), 0)
    x_ids = lax.broadcasted_iota(jnp.int32, (layers, pad_x, pad_b), 1) + x_index * width_x - depth
    block_ids = lax.broadcasted_iota(jnp.int32, (layers, pad_x, pad_b), 2) + y_index * blocks - 1
    inside = (x_ids >= 0) & (x_ids < global_x) & (block_ids >= 0) & (block_ids < all_blocks)
    row_ids = jnp.where(
        inside, (layer_ids * global_x + x_ids) * all_blocks + block_ids, -1
    ).reshape(-1)
    onehot = (wells[:, None] == row_ids[None, :]).astype(jnp.float32)
    weighted = controls[:, None] * profile
    src_rows = lax.dot_general(
        onehot,
        weighted,
        (((0,), (0,)), ((), ())),
        precision=lax.Precision.HIGHEST,
        preferred_element_type=jnp.float32,
    )
    srcpad = src_rows.reshape(layers, pad_x, pad_b * 128)[:, :, 128 - depth : 128 + width_y + depth]
    controls_count = controls.shape[0]
    inner_hot = onehot.reshape(controls_count, layers, pad_x, pad_b)[
        :, :, depth : depth + width_x, 1 : 1 + blocks
    ]
    inner_hot = inner_hot.reshape(controls_count, -1)
    stacked = jnp.stack([retard, velx, vely])
    coefpad = extended(stacked, (("gx", 3), ("gy", 4)), depth)

    def crop(field, margin):
        offset = depth - margin
        return field[..., offset : field.shape[-2] - offset, offset : field.shape[-1] - offset]

    def forward_local(padded, margin):
        coefs = crop(coefpad, margin)
        centre = padded[..., 1:-1, 1:-1]
        x_low = padded[..., :-2, 1:-1]
        x_high = padded[..., 2:, 1:-1]
        y_low = padded[..., 1:-1, :-2]
        y_high = padded[..., 1:-1, 2:]
        z_low, z_high = vertical(centre)
        flux = (
            coefs[1] * (x_low - centre)
            + coefs[2] * (y_low - centre)
            + KAPPA * (x_high + x_low + y_high + y_low - 4.0 * centre)
            + VERT * (z_high + z_low - 2.0 * centre)
        )
        return centre + coefs[0] * flux

    def adjoint_local(padded, margin):
        outer = crop(coefpad, margin + 1)
        inner = crop(coefpad, margin)
        scaled = outer[0] * padded
        moved_x = outer[1] * scaled
        moved_y = outer[2] * scaled
        centre = scaled[..., 1:-1, 1:-1]
        z_low, z_high = vertical(centre)
        neighbour_sum = (
            scaled[..., 2:, 1:-1]
            + scaled[..., :-2, 1:-1]
            + scaled[..., 1:-1, 2:]
            + scaled[..., 1:-1, :-2]
        )
        return (
            padded[..., 1:-1, 1:-1]
            - (inner[1] + inner[2] + 4.0 * KAPPA + 2.0 * VERT) * centre
            + moved_x[..., 2:, 1:-1]
            + moved_y[..., 1:-1, 2:]
            + KAPPA * neighbour_sum
            + VERT * (z_high + z_low)
        )

    own_source = crop(srcpad, 0)

    def forward_round(step, state):
        loaded = state + own_source[None]
        padded = extended(loaded, (("gx", 2), ("gy", 3)), depth)
        margin = depth - 1
        padded = forward_local(padded, margin)
        return padded

    final = lax.fori_loop(0, ITERS // depth, forward_round, initial)
    total_samples = samples * lax.axis_size("sa")
    tail_count = total_samples // 2
    tail = (ranking < tail_count).astype(jnp.float32)[:, None, None, None]
    objective_part = jnp.sum(tail * 0.5 * monitor[None] * final * final) / (
        tail_count * layers * global_x * global_y
    )
    start = tail * monitor[None] * final / (tail_count * ITERS)

    def adjoint_round(step, carry):
        adjoint, total = carry
        padded = extended(adjoint, (("gx", 2), ("gy", 3)), depth)
        margin = depth - 1
        padded = adjoint_local(padded, margin)
        total = total + padded
        return (padded, total)

    adjoint, total = lax.fori_loop(0, ITERS // depth, adjoint_round, (start, jnp.zeros_like(start)))
    sensitivity = jnp.sum(total, axis=0).reshape(-1, 128)
    collected = jnp.dot(
        inner_hot, sensitivity, precision=lax.Precision.HIGHEST, preferred_element_type=jnp.float32
    )
    gradient_part = jnp.sum(collected * profile, axis=1)
    objective_part = objective_part.reshape(1)
    gradient, objective = lax.psum((gradient_part, objective_part), ("gx", "gy", "sa"))
    return (final, gradient, objective)


def solution(mesh):
    in_specs = (
        P(("groups", "sa"), None, "gx", "gy"),
        P(("groups", "sa"), None, "gx", "gy"),
        P(("groups", "sa"), None, "gx", "gy"),
        P(("groups", "sa"), None, "gx", "gy"),
        P("groups", "gx", "gy"),
        P("groups"),
        P("groups", None),
        P("groups"),
        P(("groups", "sa")),
    )
    out_specs = (P(("groups", "sa"), None, "gx", "gy"), P("groups"), P("groups"))
    return jax.shard_map(local, mesh=mesh, in_specs=in_specs, out_specs=out_specs, check_vma=False)
```

profile of v0, /device:TPU:0, one launch (start us, length us, event | category | flops | bytes accessed | tf_op | source)
XLA Modules:
  0.0 891.2 jit_solution(4956184509490144373)
XLA Ops:
  35.6 382.1 %while.27 = (s32[]{:T(128)}, f32[4,4,32,128]{3,2,1,0:T(8,128)}, f32[4,32,128]{2,1,0:T(8,128)S(1)}, f32[4,4,32,128]{3,2,1,0:T(8,128)}, f32[4,4,32,128]{3,2,1,0:T(8,128)}, /*index=5*/f32[4,4,32,128]{3,2,1,0:T(8,128)}, s32[]{:T(128)}) while((s32[]{:T(128)}, f32[4,4,32,128]{3,2,1,0:T(8,128)}, f32[4,32,128]{2,1,0:T(8,128)S(1)}, ...), condition=%wide.region_1.2_spmd, body=%wide.region_0.1_spmd.sunk | while | flops 1974274 | bytes 2602989 | solution.py:123
  46.8 6.6 collective-permute-start.3
  70.8 6.0 collective-permute-start.3
  94.2 6.0 collective-permute-start.3
  117.5 6.0 collective-permute-start.3
  140.9 6.0 collective-permute-start.3
  164.2 6.0 collective-permute-start.3
  187.6 6.0 collective-permute-start.3
  210.9 6.0 collective-permute-start.3
  235.0 6.0 collective-permute-start.3
  261.4 6.0 collective-permute-start.3
  286.6 6.0 collective-permute-start.3
  310.0 6.0 collective-permute-start.3
  333.3 6.0 collective-permute-start.3
  356.7 6.0 collective-permute-start.3
  380.0 6.0 collective-permute-start.3
  403.4 6.0 collective-permute-start.3
  424.9 6.5 pad_maximum_fusion.10
  435.3 391.1 %while.28 = (s32[]{:T(128)}, f32[4,4,32,128]{3,2,1,0:T(8,128)S(1)}, f32[4,4,32,128]{3,2,1,0:T(8,128)}, f32[4,4,32,128]{3,2,1,0:T(8,128)}, f32[3,4,4,34,130]{4,3,2,1,0:T(8,128)S(1)}, /*index=5*/s32[]{:T(128)}, s32[]{:T(128)}) while((s32[]{:T(128)}, f32[4,4,32,128]{3,2,1,0:T(8,128)S(1)}, f32[4,4,32,128]{3,2,1,0:T(8,128)}, ...), condition=%wide.region_3.4_spmd.clone, body=%wide.region_2.3_spmd.clone.sunk | while | flops 1606979 | bytes 6331895 | solution.py:140
  445.3 6.0 collective-permute-start.7
  469.0 6.0 collective-permute-start.7
  494.1 6.0 collective-permute-start.7
  521.5 6.0 collective-permute-start.7
  546.6 6.0 collective-permute-start.7
  570.3 6.0 collective-permute-start.7
  594.0 6.0 collective-permute-start.7
  617.8 6.0 collective-permute-start.7
  641.5 6.0 collective-permute-start.7
  665.2 6.0 collective-permute-start.7
  712.7 6.0 collective-permute-start.7
  812.4 6.0 collective-permute-start.7
  830.2 61.0 %all-reduce.2 = (f32[4096]{0:T(1024)}, f32[1]{0:T(128)}) all-reduce(f32[4096]{0:T(1024)S(1)} %fusion.30, f32[1]{0:T(128)} %bitcast.5), channel_id=1, replica_groups=mesh['groups'=2,'gx'=4,'gy'=2,'sa'=2] {'gx','gy','sa'}, use_global_device_ids=true, to_apply=%region_6.7 | all-reduce | flops 4097 | bytes 32776 | tf_op jit(solution)/shard_map/psum | solution.py:147
  (469 shorter events, 650.8 us)
Async XLA Ops:
  5.2 18.1 %collective-permute-start.8 = (f32[3,4,4,1,128]{4,2,3,1,0:T(4,128)}, f32[3,4,4,1,128]{4,2,3,1,0:T(4,128)S(1)}, u32[]{:S(2)}, u32[]{:S(2)}) collective-permute-start(f32[3,4,4,1,128]{4,2,3,1,0:T(4,128)} %bitcast.9), channel_id=1, source_target_pairs={{0,4},{4,8},{8,12},{1,5},{5,9},{9,13},{2,6},{6,10},{10,14},{3,7},{... | collective-permute-start | bytes 73736 | tf_op jit(solution)/shard_map/ppermute | solution.py:21
  10.1 16.0 %collective-permute-start.9 = (f32[3,4,4,1,128]{4,2,3,1,0:T(4,128)S(1)}, f32[3,4,4,1,128]{4,2,3,1,0:T(4,128)S(1)}, u32[]{:S(2)}, u32[]{:S(2)}) collective-permute-start(f32[3,4,4,1,128]{4,2,3,1,0:T(4,128)S(1)} %bitcast.25), channel_id=1, source_target_pairs={{4,0},{8,4},{12,8},{5,1},{9,5},{13,9},{6,2},{10,6},{14,10},{7,3},{... | collective-permute-start | bytes 73736 | tf_op jit(solution)/shard_map/ppermute | solution.py:23
  30.3 394.6 %collective-permute-start.10 = (f32[3,4,4,34,1]{3,2,4,1,0:T(4,128)}, f32[3,4,4,34,1]{3,2,4,1,0:T(4,128)}, u32[]{:S(2)}, u32[]{:S(2)}) collective-permute-start(f32[3,4,4,34,1]{3,2,4,1,0:T(4,128)} %get-tuple-element.228), channel_id=1, source_target_pairs={{0,2},{1,3},{4,6},{5,7},{8,10},{9,11},{12,14},{13,15},{16,18},{17,... | collective-permute-start | bytes 19592 | tf_op jit(solution)/shard_map/ppermute | solution.py:21
  34.3 390.6 %collective-permute-start.11 = (f32[3,4,4,34,1]{3,2,4,1,0:T(4,128)}, f32[3,4,4,34,1]{3,2,4,1,0:T(4,128)}, u32[]{:S(2)}, u32[]{:S(2)}) collective-permute-start(f32[3,4,4,34,1]{3,2,4,1,0:T(4,128)} %get-tuple-element.229), channel_id=1, source_target_pairs={{2,0},{3,1},{6,4},{7,5},{10,8},{11,9},{14,12},{15,13},{18,16},{19,... | collective-permute-start | bytes 19592 | tf_op jit(solution)/shard_map/ppermute | solution.py:23
  45.5 10.5 %collective-permute-start.2 = (f32[4,4,34,1]{3,2,1,0:T(8,128)}, f32[4,4,34,1]{3,2,1,0:T(8,128)}, u32[]{:S(2)}, u32[]{:S(2)}) collective-permute-start(f32[4,4,34,1]{3,2,1,0:T(8,128)} %get-tuple-element.313), channel_id=1, source_target_pairs={{2,0},{3,1},{6,4},{7,5},{10,8},{11,9},{14,12},{15,13},{18,16},{19,... | collective-permute-start | bytes 6536 | tf_op jit(solution)/shard_map/while/body/eval_jaxpr/ppermute | solution.py:23
  46.8 11.2 %collective-permute-start.3 = (f32[4,4,34,1]{3,2,1,0:T(8,128)}, f32[4,4,34,1]{3,2,1,0:T(8,128)}, u32[]{:S(2)}, u32[]{:S(2)}) collective-permute-start(f32[4,4,34,1]{3,2,1,0:T(8,128)} %get-tuple-element.314), channel_id=1, source_target_pairs={{0,2},{1,3},{4,6},{5,7},{8,10},{9,11},{12,14},{13,15},{16,18},{17,... | collective-permute-start | bytes 6536 | tf_op jit(solution)/shard_map/while/body/eval_jaxpr/ppermute | solution.py:21
  70.8 10.2 %collective-permute-start.3 = (f32[4,4,34,1]{3,2,1,0:T(8,128)}, f32[4,4,34,1]{3,2,1,0:T(8,128)}, u32[]{:S(2)}, u32[]{:S(2)}) collective-permute-start(f32[4,4,34,1]{3,2,1,0:T(8,128)} %get-tuple-element.314), channel_id=1, source_target_pairs={{0,2},{1,3},{4,6},{5,7},{8,10},{9,11},{12,14},{13,15},{16,18},{17,... | collective-permute-start | bytes 6536 | tf_op jit(solution)/shard_map/while/body/eval_jaxpr/ppermute | solution.py:21
  94.2 10.2 %collective-permute-start.3 = (f32[4,4,34,1]{3,2,1,0:T(8,128)}, f32[4,4,34,1]{3,2,1,0:T(8,128)}, u32[]{:S(2)}, u32[]{:S(2)}) collective-permute-start(f32[4,4,34,1]{3,2,1,0:T(8,128)} %get-tuple-element.314), channel_id=1, source_target_pairs={{0,2},{1,3},{4,6},{5,7},{8,10},{9,11},{12,14},{13,15},{16,18},{17,... | collective-permute-start | bytes 6536 | tf_op jit(solution)/shard_map/while/body/eval_jaxpr/ppermute | solution.py:21
  117.5 10.2 %collective-permute-start.3 = (f32[4,4,34,1]{3,2,1,0:T(8,128)}, f32[4,4,34,1]{3,2,1,0:T(8,128)}, u32[]{:S(2)}, u32[]{:S(2)}) collective-permute-start(f32[4,4,34,1]{3,2,1,0:T(8,128)} %get-tuple-element.314), channel_id=1, source_target_pairs={{0,2},{1,3},{4,6},{5,7},{8,10},{9,11},{12,14},{13,15},{16,18},{17,... | collective-permute-start | bytes 6536 | tf_op jit(solution)/shard_map/while/body/eval_jaxpr/ppermute | solution.py:21
  140.9 10.2 %collective-permute-start.3 = (f32[4,4,34,1]{3,2,1,0:T(8,128)}, f32[4,4,34,1]{3,2,1,0:T(8,128)}, u32[]{:S(2)}, u32[]{:S(2)}) collective-permute-start(f32[4,4,34,1]{3,2,1,0:T(8,128)} %get-tuple-element.314), channel_id=1, source_target_pairs={{0,2},{1,3},{4,6},{5,7},{8,10},{9,11},{12,14},{13,15},{16,18},{17,... | collective-permute-start | bytes 6536 | tf_op jit(solution)/shard_map/while/body/eval_jaxpr/ppermute | solution.py:21
  164.2 10.2 %collective-permute-start.3 = (f32[4,4,34,1]{3,2,1,0:T(8,128)}, f32[4,4,34,1]{3,2,1,0:T(8,128)}, u32[]{:S(2)}, u32[]{:S(2)}) collective-permute-start(f32[4,4,34,1]{3,2,1,0:T(8,128)} %get-tuple-element.314), channel_id=1, source_target_pairs={{0,2},{1,3},{4,6},{5,7},{8,10},{9,11},{12,14},{13,15},{16,18},{17,... | collective-permute-start | bytes 6536 | tf_op jit(solution)/shard_map/while/body/eval_jaxpr/ppermute | solution.py:21
  187.6 10.2 %collective-permute-start.3 = (f32[4,4,34,1]{3,2,1,0:T(8,128)}, f32[4,4,34,1]{3,2,1,0:T(8,128)}, u32[]{:S(2)}, u32[]{:S(2)}) collective-permute-start(f32[4,4,34,1]{3,2,1,0:T(8,128)} %get-tuple-element.314), channel_id=1, source_target_pairs={{0,2},{1,3},{4,6},{5,7},{8,10},{9,11},{12,14},{13,15},{16,18},{17,... | collective-permute-start | bytes 6536 | tf_op jit(solution)/shard_map/while/body/eval_jaxpr/ppermute | solution.py:21
  210.9 10.6 %collective-permute-start.3 = (f32[4,4,34,1]{3,2,1,0:T(8,128)}, f32[4,4,34,1]{3,2,1,0:T(8,128)}, u32[]{:S(2)}, u32[]{:S(2)}) collective-permute-start(f32[4,4,34,1]{3,2,1,0:T(8,128)} %get-tuple-element.314), channel_id=1, source_target_pairs={{0,2},{1,3},{4,6},{5,7},{8,10},{9,11},{12,14},{13,15},{16,18},{17,... | collective-permute-start | bytes 6536 | tf_op jit(solution)/shard_map/while/body/eval_jaxpr/ppermute | solution.py:21
  233.7 11.7 %collective-permute-start.2 = (f32[4,4,34,1]{3,2,1,0:T(8,128)}, f32[4,4,34,1]{3,2,1,0:T(8,128)}, u32[]{:S(2)}, u32[]{:S(2)}) collective-permute-start(f32[4,4,34,1]{3,2,1,0:T(8,128)} %get-tuple-element.313), channel_id=1, source_target_pairs={{2,0},{3,1},{6,4},{7,5},{10,8},{11,9},{14,12},{15,13},{18,16},{19,... | collective-permute-start | bytes 6536 | tf_op jit(solution)/shard_map/while/body/eval_jaxpr/ppermute | solution.py:23
  235.0 13.0 %collective-permute-start.3 = (f32[4,4,34,1]{3,2,1,0:T(8,128)}, f32[4,4,34,1]{3,2,1,0:T(8,128)}, u32[]{:S(2)}, u32[]{:S(2)}) collective-permute-start(f32[4,4,34,1]{3,2,1,0:T(8,128)} %get-tuple-element.314), channel_id=1, source_target_pairs={{0,2},{1,3},{4,6},{5,7},{8,10},{9,11},{12,14},{13,15},{16,18},{17,... | collective-permute-start | bytes 6536 | tf_op jit(solution)/shard_map/while/body/eval_jaxpr/ppermute | solution.py:21
  260.1 11.5 %collective-permute-start.2 = (f32[4,4,34,1]{3,2,1,0:T(8,128)}, f32[4,4,34,1]{3,2,1,0:T(8,128)}, u32[]{:S(2)}, u32[]{:S(2)}) collective-permute-start(f32[4,4,34,1]{3,2,1,0:T(8,128)} %get-tuple-element.313), channel_id=1, source_target_pairs={{2,0},{3,1},{6,4},{7,5},{10,8},{11,9},{14,12},{15,13},{18,16},{19,... | collective-permute-start | bytes 6536 | tf_op jit(solution)/shard_map/while/body/eval_jaxpr/ppermute | solution.py:23
  261.4 12.1 %collective-permute-start.3 = (f32[4,4,34,1]{3,2,1,0:T(8,128)}, f32[4,4,34,1]{3,2,1,0:T(8,128)}, u32[]{:S(2)}, u32[]{:S(2)}) collective-permute-start(f32[4,4,34,1]{3,2,1,0:T(8,128)} %get-tuple-element.314), channel_id=1, source_target_pairs={{0,2},{1,3},{4,6},{5,7},{8,10},{9,11},{12,14},{13,15},{16,18},{17,... | collective-permute-start | bytes 6536 | tf_op jit(solution)/shard_map/while/body/eval_jaxpr/ppermute | solution.py:21
  286.6 10.2 %collective-permute-start.3 = (f32[4,4,34,1]{3,2,1,0:T(8,128)}, f32[4,4,34,1]{3,2,1,0:T(8,128)}, u32[]{:S(2)}, u32[]{:S(2)}) collective-permute-start(f32[4,4,34,1]{3,2,1,0:T(8,128)} %get-tuple-element.314), channel_id=1, source_target_pairs={{0,2},{1,3},{4,6},{5,7},{8,10},{9,11},{12,14},{13,15},{16,18},{17,... | collective-permute-start | bytes 6536 | tf_op jit(solution)/shard_map/while/body/eval_jaxpr/ppermute | solution.py:21
  310.0 10.2 %collective-permute-start.3 = (f32[4,4,34,1]{3,2,1,0:T(8,128)}, f32[4,4,34,1]{3,2,1,0:T(8,128)}, u32[]{:S(2)}, u32[]{:S(2)}) collective-permute-start(f32[4,4,34,1]{3,2,1,0:T(8,128)} %get-tuple-element.314), channel_id=1, source_target_pairs={{0,2},{1,3},{4,6},{5,7},{8,10},{9,11},{12,14},{13,15},{16,18},{17,... | collective-permute-start | bytes 6536 | tf_op jit(solution)/shard_map/while/body/eval_jaxpr/ppermute | solution.py:21
  333.3 10.2 %collective-permute-start.3 = (f32[4,4,34,1]{3,2,1,0:T(8,128)}, f32[4,4,34,1]{3,2,1,0:T(8,128)}, u32[]{:S(2)}, u32[]{:S(2)}) collective-permute-start(f32[4,4,34,1]{3,2,1,0:T(8,128)} %get-tuple-element.314), channel_id=1, source_target_pairs={{0,2},{1,3},{4,6},{5,7},{8,10},{9,11},{12,14},{13,15},{16,18},{17,... | collective-permute-start | bytes 6536 | tf_op jit(solution)/shard_map/while/body/eval_jaxpr/ppermute | solution.py:21
  356.7 10.2 %collective-permute-start.3 = (f32[4,4,34,1]{3,2,1,0:T(8,128)}, f32[4,4,34,1]{3,2,1,0:T(8,128)}, u32[]{:S(2)}, u32[]{:S(2)}) collective-permute-start(f32[4,4,34,1]{3,2,1,0:T(8,128)} %get-tuple-element.314), channel_id=1, source_target_pairs={{0,2},{1,3},{4,6},{5,7},{8,10},{9,11},{12,14},{13,15},{16,18},{17,... | collective-permute-start | bytes 6536 | tf_op jit(solution)/shard_map/while/body/eval_jaxpr/ppermute | solution.py:21
  380.0 10.2 %collective-permute-start.3 = (f32[4,4,34,1]{3,2,1,0:T(8,128)}, f32[4,4,34,1]{3,2,1,0:T(8,128)}, u32[]{:S(2)}, u32[]{:S(2)}) collective-permute-start(f32[4,4,34,1]{3,2,1,0:T(8,128)} %get-tuple-element.314), channel_id=1, source_target_pairs={{0,2},{1,3},{4,6},{5,7},{8,10},{9,11},{12,14},{13,15},{16,18},{17,... | collective-permute-start | bytes 6536 | tf_op jit(solution)/shard_map/while/body/eval_jaxpr/ppermute | solution.py:21
  402.1 10.8 %collective-permute-start.2 = (f32[4,4,34,1]{3,2,1,0:T(8,128)}, f32[4,4,34,1]{3,2,1,0:T(8,128)}, u32[]{:S(2)}, u32[]{:S(2)}) collective-permute-start(f32[4,4,34,1]{3,2,1,0:T(8,128)} %get-tuple-element.313), channel_id=1, source_target_pairs={{2,0},{3,1},{6,4},{7,5},{10,8},{11,9},{14,12},{15,13},{18,16},{19,... | collective-permute-start | bytes 6536 | tf_op jit(solution)/shard_map/while/body/eval_jaxpr/ppermute | solution.py:23
  403.4 12.0 %collective-permute-start.3 = (f32[4,4,34,1]{3,2,1,0:T(8,128)}, f32[4,4,34,1]{3,2,1,0:T(8,128)}, u32[]{:S(2)}, u32[]{:S(2)}) collective-permute-start(f32[4,4,34,1]{3,2,1,0:T(8,128)} %get-tuple-element.314), channel_id=1, source_target_pairs={{0,2},{1,3},{4,6},{5,7},{8,10},{9,11},{12,14},{13,15},{16,18},{17,... | collective-permute-start | bytes 6536 | tf_op jit(solution)/shard_map/while/body/eval_jaxpr/ppermute | solution.py:21
  469.0 11.2 %collective-permute-start.7 = (f32[4,4,34,1]{3,2,1,0:T(8,128)}, f32[4,4,34,1]{3,2,1,0:T(8,128)}, u32[]{:S(2)}, u32[]{:S(2)}) collective-permute-start(f32[4,4,34,1]{3,2,1,0:T(8,128)} %get-tuple-element.323), channel_id=1, source_target_pairs={{0,2},{1,3},{4,6},{5,7},{8,10},{9,11},{12,14},{13,15},{16,18},{17,... | collective-permute-start | bytes 6536 | tf_op jit(solution)/shard_map/while/body/eval_jaxpr/ppermute | solution.py:21
  492.8 12.4 %collective-permute-start.6 = (f32[4,4,34,1]{3,2,1,0:T(8,128)}, f32[4,4,34,1]{3,2,1,0:T(8,128)}, u32[]{:S(2)}, u32[]{:S(2)}) collective-permute-start(f32[4,4,34,1]{3,2,1,0:T(8,128)} %get-tuple-element.322), channel_id=1, source_target_pairs={{2,0},{3,1},{6,4},{7,5},{10,8},{11,9},{14,12},{15,13},{18,16},{19,... | collective-permute-start | bytes 6536 | tf_op jit(solution)/shard_map/while/body/eval_jaxpr/ppermute | solution.py:23
  494.1 13.5 %collective-permute-start.7 = (f32[4,4,34,1]{3,2,1,0:T(8,128)}, f32[4,4,34,1]{3,2,1,0:T(8,128)}, u32[]{:S(2)}, u32[]{:S(2)}) collective-permute-start(f32[4,4,34,1]{3,2,1,0:T(8,128)} %get-tuple-element.323), channel_id=1, source_target_pairs={{0,2},{1,3},{4,6},{5,7},{8,10},{9,11},{12,14},{13,15},{16,18},{17,... | collective-permute-start | bytes 6536 | tf_op jit(solution)/shard_map/while/body/eval_jaxpr/ppermute | solution.py:21
  520.3 11.1 %collective-permute-start.6 = (f32[4,4,34,1]{3,2,1,0:T(8,128)}, f32[4,4,34,1]{3,2,1,0:T(8,128)}, u32[]{:S(2)}, u32[]{:S(2)}) collective-permute-start(f32[4,4,34,1]{3,2,1,0:T(8,128)} %get-tuple-element.322), channel_id=1, source_target_pairs={{2,0},{3,1},{6,4},{7,5},{10,8},{11,9},{14,12},{15,13},{18,16},{19,... | collective-permute-start | bytes 6536 | tf_op jit(solution)/shard_map/while/body/eval_jaxpr/ppermute | solution.py:23
  521.5 11.7 %collective-permute-start.7 = (f32[4,4,34,1]{3,2,1,0:T(8,128)}, f32[4,4,34,1]{3,2,1,0:T(8,128)}, u32[]{:S(2)}, u32[]{:S(2)}) collective-permute-start(f32[4,4,34,1]{3,2,1,0:T(8,128)} %get-tuple-element.323), channel_id=1, source_target_pairs={{0,2},{1,3},{4,6},{5,7},{8,10},{9,11},{12,14},{13,15},{16,18},{17,... | collective-permute-start | bytes 6536 | tf_op jit(solution)/shard_map/while/body/eval_jaxpr/ppermute | solution.py:21
  712.7 11.3 %collective-permute-start.7 = (f32[4,4,34,1]{3,2,1,0:T(8,128)}, f32[4,4,34,1]{3,2,1,0:T(8,128)}, u32[]{:S(2)}, u32[]{:S(2)}) collective-permute-start(f32[4,4,34,1]{3,2,1,0:T(8,128)} %get-tuple-element.323), channel_id=1, source_target_pairs={{0,2},{1,3},{4,6},{5,7},{8,10},{9,11},{12,14},{13,15},{16,18},{17,... | collective-permute-start | bytes 6536 | tf_op jit(solution)/shard_map/while/body/eval_jaxpr/ppermute | solution.py:21
  736.5 12.5 %collective-permute-start.6 = (f32[4,4,34,1]{3,2,1,0:T(8,128)}, f32[4,4,34,1]{3,2,1,0:T(8,128)}, u32[]{:S(2)}, u32[]{:S(2)}) collective-permute-start(f32[4,4,34,1]{3,2,1,0:T(8,128)} %get-tuple-element.322), channel_id=1, source_target_pairs={{2,0},{3,1},{6,4},{7,5},{10,8},{11,9},{14,12},{15,13},{18,16},{19,... | collective-permute-start | bytes 6536 | tf_op jit(solution)/shard_map/while/body/eval_jaxpr/ppermute | solution.py:23
  737.8 13.6 %collective-permute-start.7 = (f32[4,4,34,1]{3,2,1,0:T(8,128)}, f32[4,4,34,1]{3,2,1,0:T(8,128)}, u32[]{:S(2)}, u32[]{:S(2)}) collective-permute-start(f32[4,4,34,1]{3,2,1,0:T(8,128)} %get-tuple-element.323), channel_id=1, source_target_pairs={{0,2},{1,3},{4,6},{5,7},{8,10},{9,11},{12,14},{13,15},{16,18},{17,... | collective-permute-start | bytes 6536 | tf_op jit(solution)/shard_map/while/body/eval_jaxpr/ppermute | solution.py:21
  (106 other events, 1172.7 us)
where the time goes:
time: 896 us; the launch traced here: 891 us
  starting transfers between devices  443 us (49%)
  waiting for transfers between devices  191 us (21%)
  other arithmetic  131 us (15%)
  blocking collectives  61 us (7%)
  local copies, waits for them, and re-layouts  54 us (6%)
    ppermute x66, starting transfers between devices, extended(): lax.ppermute(tail, axis, [(i, (i + 1) % count) for i in range(ends)])  358 us
    ppermute x66, waiting for transfers between devices, extended(): lax.ppermute(tail, axis, [(i, (i + 1) % count) for i in range(ends)])  114 us
    ppermute x66, starting transfers between devices, extended(): lax.ppermute(head, axis, [((i + 1) % count, i) for i in range(ends)])  84.9 us
    ppermute x66, waiting for transfers between devices, extended(): lax.ppermute(head, axis, [((i + 1) % count, i) for i in range(ends)])  77.6 us
    psum x1, blocking collectives, local(): lax.psum((gradient_part, objective_part), ('gx', 'gy', 'sa'))  61 us
    add x16, other arithmetic, forward_local(): return centre + coefs[0] * flux  38.3 us
    add x16, other arithmetic, adjoint_round(): total = total + padded  35.3 us
    slice x65, local copies, waits for them, and re-layouts, extended(): lax.slice_in_dim(cells, cells.shape[dim] - width, cells.shape[dim], axis=...  31.2 us
  transfers between devices with their start and end apart: 132, of which 96 were waited for; matrix products, arithmetic and copies ran while one was open for 10% of the time, Pallas kernels for 0%

commit v1 on v0

v1 whole, which is shorter than its diff:
```python
import functools

import jax
import jax.numpy as jnp
from jax import lax
from jax.experimental import pallas as pl
from jax.experimental.pallas import tpu as pltpu
from jax.sharding import PartitionSpec as P

ITERS = 16
KAPPA = 0.1
VERT = 0.05
LANES = 128
SUBLANES = 8
DEPTH = ITERS
OWN = 2 * DEPTH
EXT = OWN + 2 * DEPTH
GROUPS = LANES // DEPTH
INNER = EXT // GROUPS
CHUNK = 512
PHASES = ((0, 4), (4, 8), (8, 12), (12, ITERS - 1))
VMEM_LIMIT = 48 * 1024 * 1024


def vmem():
    return pl.BlockSpec(memory_space=pltpu.VMEM)


def params():
    return pltpu.CompilerParams(vmem_limit_bytes=VMEM_LIMIT)


def sub_id():
    return lax.broadcasted_iota(jnp.int32, (SUBLANES, LANES), 0)


def lane_id():
    return lax.broadcasted_iota(jnp.int32, (SUBLANES, LANES), 1)


def wrap(shift):
    return shift % LANES if isinstance(shift, int) else lax.rem(shift, LANES)


def lane_roll(value, shift):
    if isinstance(shift, int) and shift % LANES == 0:
        return value
    return pltpu.roll(value, wrap(shift), 1)


def pick(flag, yes, no):
    if isinstance(flag, bool):
        return yes if flag else no
    return jnp.where(flag, yes, no)


def odd_tile():
    return lax.rem(lax.axis_index("gx"), 2)


def strip_kinds(count):
    return (None,) if count == 2 else (True, False)


def is_right(kind):
    return lax.axis_index("gy") == 0 if kind is None else kind


def planes(ref, row, half, rows):
    return ref[pl.ds(half * rows + row, SUBLANES, stride=2 * rows), :]


def split_kernel(initial, retard, velx, vely, out_a, out_b, sems):
    odd = odd_tile()
    copies = []
    for field, ref in enumerate((initial, retard, velx, vely)):
        for which, (out, base) in enumerate(((out_a, DEPTH * (1 - odd)), (out_b, DEPTH * odd))):
            source = ref.at[:, :, pl.ds(pl.multiple_of(base, DEPTH), DEPTH), :]
            copy = pltpu.make_async_copy(source, out.at[field], sems.at[2 * field + which])
            copy.start()
            copies.append(copy)
    for copy in copies:
        copy.wait()


def strip_pack_kernel(kinds, initial, retard, velx, vely, *outs):
    odd = odd_tile()
    group = lane_id() // DEPTH
    fields = (initial, retard, velx, vely)
    for number, kind in enumerate(kinds):
        to_y, to_a, to_b = outs[3 * number : 3 * number + 3]
        offset = DEPTH * (1 - lax.axis_index("gy")) if kind is None else (0 if kind else DEPTH)
        for i in range(INNER):
            for half in range(2):
                for pair in range(2):
                    packed = jnp.zeros((SUBLANES, LANES), jnp.float32)
                    for member in range(2):
                        for j in range(2, 6):
                            target = (j + 4 * member) % GROUPS
                            rows = planes(fields[2 * pair + member], 8 * (j - 2) + i, half, OWN)
                            moved = lane_roll(rows, DEPTH * target + offset)
                            packed = jnp.where(group == target, moved, packed)
                    to_y[pair, i, half] = packed
                for out, base in ((to_a, DEPTH * (1 - odd)), (to_b, DEPTH * odd)):
                    packed = jnp.zeros((SUBLANES, LANES), jnp.float32)
                    for field in range(4):
                        for jj in range(2):
                            target = 2 * field + jj
                            rows = planes(fields[field], base + 8 * jj + i, half, OWN)
                            moved = lane_roll(rows, DEPTH * target + offset)
                            packed = jnp.where(group == target, moved, packed)
                    out[i, half] = packed


def source_kernel(kinds, wells, controls, profile, *refs):
    outs, (acc, acc_low) = refs[:-2], refs[-2:]
    x_index, y_index = lax.axis_index("gx"), lax.axis_index("gy")
    all_x, all_blocks = OWN * lax.axis_size("gx"), lax.axis_size("gy")
    layers = 4
    per_block = EXT * layers
    r = lax.broadcasted_iota(jnp.int32, (per_block, 1), 0)
    x = x_index * OWN - DEPTH + r // layers
    ids = []
    for block in [y_index] + [
        1 - y_index if kind is None else (y_index + 1 if kind else y_index - 1) for kind in kinds
    ]:
        inside = (x >= 0) & (x < all_x) & (block >= 0) & (block < all_blocks)
        ids.append(jnp.where(inside, ((r % layers) * all_x + x) * all_blocks + block, -1))
    ids = jnp.concatenate(ids, axis=0)
    acc[...] = jnp.zeros_like(acc)
    acc_low[...] = jnp.zeros_like(acc_low)

    def chunk(c, carry):
        span = pl.ds(pl.multiple_of(c * CHUNK, CHUNK), CHUNK)
        part = profile[span, :]
        high = part.astype(jnp.bfloat16)
        low = (part - high.astype(jnp.float32)).astype(jnp.bfloat16)
        rate = controls[:, span]
        rate_high = rate.astype(jnp.bfloat16).astype(jnp.float32)
        hit = ids == wells[:, span]
        hot_high = jnp.where(hit, rate_high, 0.0).astype(jnp.bfloat16)
        hot_low = jnp.where(hit, rate - rate_high, 0.0).astype(jnp.bfloat16)
        acc[...] += jnp.dot(
            hot_high, jnp.concatenate([high, low], axis=1), preferred_element_type=jnp.float32
        )
        acc_low[...] += jnp.dot(hot_low, high, preferred_element_type=jnp.float32)
        return carry

    lax.fori_loop(0, wells.shape[1] // CHUNK, chunk, 0)
    acc_low[...] += acc[:, :LANES] + acc[:, LANES:]
    upper = sub_id() % 2 == 1
    group = lane_id() // DEPTH

    def both(first, half):
        low_layer = jnp.broadcast_to(acc_low[pl.ds(first + half, 1), :], (SUBLANES, LANES))
        high_layer = jnp.broadcast_to(acc_low[pl.ds(first + 2 + half, 1), :], (SUBLANES, LANES))
        return jnp.where(upper, high_layer, low_layer)

    for e in range(EXT):
        for half in range(2):
            outs[0][e, half] = both(e * layers, half)
    for number, kind in enumerate(kinds):
        offset = DEPTH * y_index if kind is None else (0 if kind else DEPTH)
        for i in range(INNER):
            for half in range(2):
                packed = jnp.zeros((SUBLANES, LANES), jnp.float32)
                for j in range(GROUPS):
                    rows = both((number + 1) * per_block + (j * INNER + i) * layers, half)
                    moved = lane_roll(rows, DEPTH * j + offset)
                    packed = jnp.where(group == j, moved, packed)
                outs[1 + number][i, half] = packed


def coefficients(retard, velx, vely):
    spread = KAPPA * retard
    from_x = retard * velx + spread
    from_y = retard * vely + spread
    keep = 1.0 - (from_x + from_y + (2.0 + 2.0 * VERT / KAPPA) * spread)
    return keep, from_x, from_y, spread


def places(odd):
    return DEPTH * (2 - odd), DEPTH * (1 + odd), 3 * DEPTH * (1 - odd), 3 * DEPTH * odd


def load_coefficients(odd, own, got_a, got_b, coefs, state=None):
    for x in range(OWN):
        for half in range(2):
            raw = [planes(ref, x, half, OWN) for ref in own[-3:]]
            for ref, value in zip(coefs, coefficients(*raw)):
                ref[DEPTH + x, half] = value
            if state is not None:
                state[DEPTH + x, half] = planes(own[0], x, half, OWN)
    _, _, at_a, at_b = places(odd)
    for got, at in ((got_a, at_a), (got_b, at_b)):
        for x in range(DEPTH):
            for half in range(2):
                raw = [planes(got.at[field], x, half, DEPTH) for field in (1, 2, 3)]
                for ref, value in zip(coefs, coefficients(*raw)):
                    ref[at + x, half] = value
                if state is not None:
                    state[at + x, half] = planes(got.at[0], x, half, DEPTH)


def merge_strip(odd, middle, from_a, from_b):
    quarter = lane_id() // (2 * DEPTH)
    rim = jnp.where(quarter == 3 * (1 - odd), from_a, from_b)
    return jnp.where((quarter == 1) | (quarter == 2), middle, rim)


def strip_field(odd, got_y, got_a, got_b, field, i, half):
    middle = lane_roll(got_y[field // 2, i, half], 64 * (field % 2))
    from_a = lane_roll(got_a[i, half], 96 * (1 - odd) + LANES - 32 * field)
    from_b = lane_roll(got_b[i, half], 96 * odd + LANES - 32 * field)
    return merge_strip(odd, middle, from_a, from_b)


def load_strips(odd, got, coefs, state=None):
    for i in range(INNER):
        for half in range(2):
            raw = [strip_field(odd, *got, field, i, half) for field in (1, 2, 3)]
            for ref, value in zip(coefs, coefficients(*raw)):
                ref[i, half] = value
            if state is not None:
                state[i, half] = strip_field(odd, *got, 0, i, half)


class Frame:
    def __init__(self, kinds):
        lane = lane_id()
        self.first, self.last = lane == 0, lane == LANES - 1
        self.column = lane % DEPTH
        self.strip_first, self.strip_last = self.column == 0, self.column == DEPTH - 1
        self.group = lane // DEPTH
        upper = sub_id() % 2 == 1
        self.below = jnp.where(upper, VERT / KAPPA, 0.0)
        self.above = jnp.where(upper, 0.0, VERT / KAPPA)
        self.right = [is_right(kind) for kind in kinds]
        self.to_tile = [pick(right, 127, 113) for right in self.right]
        self.to_strip = [pick(right, 1, 15) for right in self.right]
        self.edge = [self.column == pick(right, 0, DEPTH - 1) for right in self.right]

    def vertical(self, pair):
        low = (VERT / KAPPA) * pair[1] + self.below * pltpu.roll(pair[1], 1, 0)
        high = (VERT / KAPPA) * pair[0] + self.above * pltpu.roll(pair[0], SUBLANES - 1, 0)
        return low, high

    def onto_tile(self, edges, j):
        total = None
        for shift, edge in zip(self.to_tile, edges):
            moved = lane_roll(edge, shift - DEPTH * j)
            total = moved if total is None else total + moved
        return total

    def onto_strip(self, number, value, j, packed):
        moved = lane_roll(value, self.to_strip[number] + DEPTH * j)
        return jnp.where(self.group == j, moved, packed)


def forward_step(frame, tile, strips, first, last, final_step, emit):
    state, keep, from_x, from_y, spread, source = tile
    zero = jnp.zeros((SUBLANES, LANES), jnp.float32)
    count = len(strips)
    edges = [
        [[jnp.where(frame.edge[k], strips[k][0][i, h], 0.0) for h in range(2)] for i in range(INNER)]
        for k in range(count)
    ]
    gathered = [[[zero, zero] for _ in range(INNER)] for _ in range(count)]
    before = [state[first - 1, h] for h in range(2)]
    here = [state[first, h] for h in range(2)]
    for e in range(first, last + 1):
        after = [state[e + 1, h] for h in range(2)]
        j, i = divmod(e, INNER)
        upright = frame.vertical(here)
        fresh = []
        for h in range(2):
            edge = frame.onto_tile([edges[k][i][h] for k in range(count)], j)
            y_low = jnp.where(frame.first, edge, lane_roll(here[h], 1))
            y_high = jnp.where(frame.last, edge, lane_roll(here[h], LANES - 1))
            value = (
                keep[e, h] * here[h]
                + from_x[e, h] * before[h]
                + from_y[e, h] * y_low
                + spread[e, h] * (after[h] + y_high + upright[h])
            )
            fresh.append(value)
            if not final_step:
                for k in range(count):
                    gathered[k][i][h] = frame.onto_strip(k, here[h], j, gathered[k][i][h])
                state[e, h] = value + source[e, h]
        if final_step:
            emit(e, fresh)
        before, here = here, after
    if final_step:
        return
    for k in range(count):
        strip, keep, from_x, from_y, spread, source = strips[k]
        old = [[strip[i, h] for h in range(2)] for i in range(INNER)]
        for i in range(INNER):
            upright = frame.vertical(old[i])
            for h in range(2):
                x_low = old[i - 1][h] if i > 0 else lane_roll(old[INNER - 1][h], DEPTH)
                x_high = old[i + 1][h] if i < INNER - 1 else lane_roll(old[0][h], LANES - DEPTH)
                edge = gathered[k][i][h]
                y_low = jnp.where(frame.strip_first, edge, lane_roll(old[i][h], 1))
                y_high = jnp.where(frame.strip_last, edge, lane_roll(old[i][h], LANES - 1))
                strip[i, h] = (
                    keep[i, h] * old[i][h]
                    + from_x[i, h] * x_low
                    + from_y[i, h] * y_low
                    + spread[i, h] * (x_high + y_high + upright[h])
                    + source[i, h]
                )


def adjoint_step(frame, tile, strips, first, last, final_step, total):
    state, keep, from_x, from_y, spread = tile
    zero = jnp.zeros((SUBLANES, LANES), jnp.float32)
    count = len(strips)
    edges = [
        [
            [
                jnp.where(
                    frame.edge[k],
                    pick(frame.right[k], strips[k][3][i, h], strips[k][4][i, h]) * strips[k][0][i, h],
                    0.0,
                )
                for h in range(2)
            ]
            for i in range(INNER)
        ]
        for k in range(count)
    ]
    gathered = [[[zero, zero] for _ in range(INNER)] for _ in range(count)]

    def row(e):
        value = [state[e, h] for h in range(2)]
        return (
            value,
            [from_x[e, h] * value[h] for h in range(2)],
            [from_y[e, h] * value[h] for h in range(2)],
            [spread[e, h] * value[h] for h in range(2)],
        )

    before, here = row(first - 1), row(first)
    for e in range(first, last + 1):
        after = row(e + 1)
        j, i = divmod(e, INNER)
        value, _, by_y, by_spread = here
        upright = frame.vertical(by_spread)
        for h in range(2):
            edge = frame.onto_tile([edges[k][i][h] for k in range(count)], j)
            y_low = jnp.where(frame.first, edge, lane_roll(by_spread[h], 1))
            y_high = jnp.where(frame.last, edge, lane_roll(by_y[h], LANES - 1))
            fresh = (
                keep[e, h] * value[h] + (after[1][h] + before[3][h]) + (y_low + y_high) + upright[h]
            )
            if DEPTH <= e < DEPTH + OWN:
                total[e - DEPTH, h] += fresh
            if not final_step:
                state[e, h] = fresh
                for k in range(count):
                    edge = pick(frame.right[k], by_spread[h], by_y[h])
                    gathered[k][i][h] = frame.onto_strip(k, edge, j, gathered[k][i][h])
        before, here = here, after
    if final_step:
        return
    for k in range(count):
        strip, keep, from_x, from_y, spread = strips[k]
        old = [[strip[i, h] for h in range(2)] for i in range(INNER)]
        by_x = [[from_x[i, h] * old[i][h] for h in range(2)] for i in range(INNER)]
        by_spread = [[spread[i, h] * old[i][h] for h in range(2)] for i in range(INNER)]
        for i in range(INNER):
            upright = frame.vertical(by_spread[i])
            for h in range(2):
                x_low = by_spread[i - 1][h] if i > 0 else lane_roll(by_spread[INNER - 1][h], DEPTH)
                x_high = by_x[i + 1][h] if i < INNER - 1 else lane_roll(by_x[0][h], LANES - DEPTH)
                by_y = from_y[i, h] * old[i][h]
                edge = gathered[k][i][h]
                y_low = jnp.where(frame.strip_first, edge, lane_roll(by_spread[i][h], 1))
                y_high = jnp.where(frame.strip_last, edge, lane_roll(by_y, LANES - 1))
                strip[i, h] = (
                    keep[i, h] * old[i][h] + (x_low + x_high) + (y_low + y_high) + upright[h]
                )


def sweep(step):
    for begin, end in PHASES:

        def body(_, carry, begin=begin):
            step(begin + 1, EXT - 2 - begin, False)
            return carry

        lax.fori_loop(begin, end, body, 0)
    step(ITERS, EXT - 1 - ITERS, True)


def split_refs(refs, *counts):
    out = []
    for count in counts:
        out.append(refs[:count])
        refs = refs[count:]
    return out


def forward_kernel(kinds, tail_count, *refs):
    n = len(kinds)
    own, (monitor, ranking, got_a, got_b), got_strips, sources, outs, out_strips, tile, start, strips = split_refs(
        refs, 4, 4, 3 * n, 1 + n, 4, 3 * n, 5, 1, 5 * n
    )
    final, start_a, start_b, objective = outs
    start = start[0]
    odd = odd_tile()
    frame = Frame(kinds)
    state, coefs = tile[0], tile[1:]
    load_coefficients(odd, own, got_a, got_b, coefs, state)
    for e in range(EXT):
        for h in range(2):
            state[e, h] += sources[0][e, h]
    strip_refs = []
    for k in range(n):
        mine = strips[5 * k : 5 * k + 5]
        load_strips(odd, got_strips[3 * k : 3 * k + 3], mine[1:], mine[0])
        for i in range(INNER):
            for h in range(2):
                mine[0][i, h] += sources[1 + k][i, h]
        strip_refs.append((*mine, sources[1 + k]))

    sample = sub_id() // 2
    upper = sub_id() % 2 == 1
    tail = jnp.zeros((SUBLANES, LANES), jnp.float32)
    for s in range(4):
        tail = jnp.where(sample == s, jnp.where(ranking[s] < tail_count, 1.0, 0.0), tail)
    objective[...] = jnp.zeros_like(objective)

    def emit(e, fresh):
        x = e - DEPTH
        for h in range(2):
            final[pl.ds(h * OWN + x, SUBLANES, stride=2 * OWN), :] = fresh[h]
            low = jnp.broadcast_to(monitor[pl.ds(h * OWN + x, 1), :], (SUBLANES, LANES))
            high = jnp.broadcast_to(monitor[pl.ds((2 + h) * OWN + x, 1), :], (SUBLANES, LANES))
            weighted = tail * jnp.where(upper, high, low) * fresh[h]
            start[x, h] = weighted * (1.0 / (tail_count * ITERS))
            objective[...] += weighted * fresh[h]

    def step(first, last, final_step):
        forward_step(frame, (*tile, sources[0]), strip_refs, first, last, final_step, emit)

    sweep(step)
    at_a, at_b = DEPTH * (1 - odd), DEPTH * odd
    for x in range(DEPTH):
        for h in range(2):
            start_a[x, h] = start[at_a + x, h]
            start_b[x, h] = start[at_b + x, h]
    for k, kind in enumerate(kinds):
        to_y, to_a, to_b = out_strips[3 * k : 3 * k + 3]
        offset = DEPTH * (1 - lax.axis_index("gy")) if kind is None else (0 if kind else DEPTH)
        for i in range(INNER):
            packed = jnp.zeros((SUBLANES, LANES), jnp.float32)
            for h in range(2):
                for j in range(2, 6):
                    target = (j + 4 * h) % GROUPS
                    moved = lane_roll(start[8 * (j - 2) + i, h], DEPTH * target + offset)
                    packed = jnp.where(frame.group == target, moved, packed)
            to_y[i] = packed
            for out, base in ((to_a, at_a), (to_b, at_b)):
                packed = jnp.zeros((SUBLANES, LANES), jnp.float32)
                for h in range(2):
                    for jj in range(2):
                        target = 2 * h + jj
                        moved = lane_roll(start[base + 8 * jj + i, h], DEPTH * target + offset)
                        packed = jnp.where(frame.group == target, moved, packed)
                out[i] = packed


def adjoint_kernel(kinds, scale, *refs):
    n = len(kinds)
    own, got, got_strips, parts, part_strips, rest, tile, strips, scratch = split_refs(
        refs, 3, 2, 3 * n, 4, 3 * n, 4, 5, 5 * n, 2
    )
    objective, wells, profile, out = rest
    total, rows = scratch
    odd = odd_tile()
    frame = Frame(kinds)
    state, coefs = tile[0], tile[1:]
    load_coefficients(odd, own, *got, coefs)
    for part, at in zip(parts, places(odd)):
        for x in range(DEPTH):
            for h in range(2):
                state[at + x, h] = part[x, h]
    strip_refs = []
    for k in range(n):
        mine = strips[5 * k : 5 * k + 5]
        load_strips(odd, got_strips[3 * k : 3 * k + 3], mine[1:])
        got_y, got_a, got_b = part_strips[3 * k : 3 * k + 3]
        for i in range(INNER):
            for h in range(2):
                mine[0][i, h] = merge_strip(
                    odd,
                    lane_roll(got_y[i], 64 * h),
                    lane_roll(got_a[i], 96 * (1 - odd) + LANES - 32 * h),
                    lane_roll(got_b[i], 96 * odd + LANES - 32 * h),
                )
        strip_refs.append(mine)
    total[...] = jnp.zeros_like(total)

    def step(first, last, final_step):
        adjoint_step(frame, tile, strip_refs, first, last, final_step, total)

    sweep(step)
    for x in range(OWN):
        for h in range(2):
            value = total[x, h]
            value = value + pltpu.roll(value, 4, 0)
            value = value + pltpu.roll(value, 2, 0)
            rows[pl.ds((2 * x + h) * 2, 2), :] = value[:2]
    count = rows.shape[0]
    r = lax.broadcasted_iota(jnp.int32, (count, 1), 0)
    layer = (r % 2) * 2 + (r // 2) % 2
    x = lax.axis_index("gx") * OWN + r // 4
    ids = (layer * (OWN * lax.axis_size("gx")) + x) * lax.axis_size("gy") + lax.axis_index("gy")
    field = rows[...]
    high = field.astype(jnp.bfloat16)
    low = (field - high.astype(jnp.float32)).astype(jnp.bfloat16)
    both = jnp.concatenate([high, low], axis=0)
    contract = (((1,), (1,)), ((), ()))
    controls = wells.shape[1]

    def chunk(c, carry):
        span = pl.ds(pl.multiple_of(c * CHUNK, CHUNK), CHUNK)
        share = profile[span, :]
        share_high = share.astype(jnp.bfloat16)
        share_low = (share - share_high.astype(jnp.float32)).astype(jnp.bfloat16)
        first = lax.dot_general(both, share_high, contract, preferred_element_type=jnp.float32)
        second = lax.dot_general(high, share_low, contract, preferred_element_type=jnp.float32)
        product = first[:count] + first[count:] + second
        chosen = jnp.where(ids == wells[:, span], product, 0.0)
        out[:, span] = jnp.sum(chosen, axis=0, keepdims=True)
        return carry

    lax.fori_loop(0, controls // CHUNK, chunk, 0)
    whole = jnp.sum(jnp.sum(objective[...], axis=0, keepdims=True), axis=1, keepdims=True)
    out[:, controls:] = jnp.broadcast_to(whole * scale, (1, LANES))


def shape(*dims):
    return jax.ShapeDtypeStruct(dims, jnp.float32)


def partner_a(x, count):
    return x ^ 1


def partner_b(x, count):
    other = x + 1 if x % 2 else x - 1
    return other if 0 <= other < count else None


def tile_pairs(partner, count):
    return [(partner(x, count), x) for x in range(count) if partner(x, count) is not None]


def strip_pairs(kind, partner, count_x, count_y):
    pairs = []
    for x in range(count_x):
        for y in range(count_y):
            from_x = partner(x, count_x)
            from_y = 1 - y if kind is None else (y + 1 if kind else y - 1)
            if from_x is not None and 0 <= from_y < count_y:
                pairs.append((from_x * count_y + from_y, x * count_y + y))
    return pairs


def exchange(tiles, strips, kinds, count_x, count_y):
    got = [
        lax.ppermute(tile, "gx", tile_pairs(partner, count_x))
        for tile, partner in zip(tiles, (partner_a, partner_b))
    ]
    got_strips = []
    for k, kind in enumerate(kinds):
        for strip, partner in zip(
            strips[3 * k : 3 * k + 3], (lambda x, count: x, partner_a, partner_b)
        ):
            pairs = strip_pairs(kind, partner, count_x, count_y)
            got_strips.append(lax.ppermute(strip, ("gx", "gy"), pairs))
    return got, got_strips


def local(initial, retard, velx, vely, monitor, controls, profile, wells, ranking):
    samples, layers, width_x, width_y = initial.shape
    count_x, count_y = lax.axis_size("gx"), lax.axis_size("gy")
    assert (samples, layers, width_x, width_y) == (4, 4, OWN, LANES) and count_x % 2 == 0
    number = controls.shape[0]
    assert number % CHUNK == 0
    kinds = strip_kinds(count_y)
    n = len(kinds)
    fields = (initial, retard, velx, vely)
    flat = [field.reshape(-1, LANES) for field in fields]
    half_tile = shape(4, samples, layers, DEPTH, LANES)
    any_space = pl.BlockSpec(memory_space=pl.ANY)
    sent = pl.pallas_call(
        split_kernel,
        out_shape=(half_tile, half_tile),
        in_specs=[any_space] * 4,
        out_specs=(any_space, any_space),
        scratch_shapes=[pltpu.SemaphoreType.DMA((8,))],
        compiler_params=params(),
        name="split",
    )(*fields)
    strip_shape = shape(INNER, 2, SUBLANES, LANES)
    sent_strips = pl.pallas_call(
        functools.partial(strip_pack_kernel, kinds),
        out_shape=(shape(2, INNER, 2, SUBLANES, LANES), strip_shape, strip_shape) * n,
        in_specs=[vmem()] * 4,
        out_specs=(vmem(),) * (3 * n),
        compiler_params=params(),
        name="strips",
    )(*flat)
    got, got_strips = exchange(sent, sent_strips, kinds, count_x, count_y)
    wells = wells.reshape(1, -1)
    blocks = (1 + n) * EXT * layers
    sources = pl.pallas_call(
        functools.partial(source_kernel, kinds),
        out_shape=(shape(EXT, 2, SUBLANES, LANES),) + (strip_shape,) * n,
        in_specs=[vmem()] * 3,
        out_specs=(vmem(),) * (1 + n),
        scratch_shapes=[
            pltpu.VMEM((blocks, 2 * LANES), jnp.float32),
            pltpu.VMEM((blocks, LANES), jnp.float32),
        ],
        compiler_params=params(),
        name="source",
    )(wells, controls.reshape(1, -1), profile)
    got = [part.reshape(4, -1, LANES) for part in got]
    tail_count = samples * lax.axis_size("sa") // 2
    tile_scratch = [pltpu.VMEM((EXT, 2, SUBLANES, LANES), jnp.float32)] * 5
    strip_scratch = [pltpu.VMEM((INNER, 2, SUBLANES, LANES), jnp.float32)] * (5 * n)
    half_start = shape(DEPTH, 2, SUBLANES, LANES)
    packed = shape(INNER, SUBLANES, LANES)
    smem = pl.BlockSpec(memory_space=pltpu.SMEM)
    final, start_a, start_b, objective, *start_strips = pl.pallas_call(
        functools.partial(forward_kernel, kinds, tail_count),
        out_shape=(
            shape(samples * layers * OWN, LANES),
            half_start,
            half_start,
            shape(SUBLANES, LANES),
        )
        + (packed,) * (3 * n),
        in_specs=[vmem()] * 5 + [smem] + [vmem()] * (2 + 3 * n + 1 + n),
        out_specs=(vmem(),) * (4 + 3 * n),
        scratch_shapes=tile_scratch
        + [pltpu.VMEM((OWN, 2, SUBLANES, LANES), jnp.float32)]
        + strip_scratch,
        compiler_params=params(),
        name="forward",
    )(*flat, monitor.reshape(-1, LANES), ranking, *got, *got_strips, *sources)
    start = (start_a, start_b)
    got_start, got_start_strips = exchange(start, start_strips, kinds, count_x, count_y)
    cells = layers * OWN * count_x * LANES * count_y
    summed = pl.pallas_call(
        functools.partial(adjoint_kernel, kinds, 0.5 / (tail_count * cells)),
        out_shape=shape(1, number + LANES),
        in_specs=[vmem()] * (3 + 2 + 3 * n + 4 + 3 * n + 3),
        out_specs=vmem(),
        scratch_shapes=tile_scratch
        + strip_scratch
        + [
            pltpu.VMEM((OWN, 2, SUBLANES, LANES), jnp.float32),
            pltpu.VMEM((OWN * layers, LANES), jnp.float32),
        ],
        compiler_params=params(),
        name="adjoint",
    )(
        *flat[1:],
        *got,
        *got_strips,
        *start,
        *got_start,
        *got_start_strips,
        objective,
        wells,
        profile,
    )
    for axis in ("sa", "gy", "gx"):
        count = lax.axis_size(axis)
        distance = 1
        while distance < count:
            pairs = [(i, i ^ distance) for i in range(count)]
            summed = summed + lax.ppermute(summed, axis, pairs)
            distance *= 2
    return final.reshape(initial.shape), summed[0, :number], summed[0, number : number + 1]


def solution(mesh):
    in_specs = (
        P(("groups", "sa"), None, "gx", "gy"),
        P(("groups", "sa"), None, "gx", "gy"),
        P(("groups", "sa"), None, "gx", "gy"),
        P(("groups", "sa"), None, "gx", "gy"),
        P("groups", "gx", "gy"),
        P("groups"),
        P("groups", None),
        P("groups"),
        P(("groups", "sa")),
    )
    out_specs = (P(("groups", "sa"), None, "gx", "gy"), P("groups"), P("groups"))
    return jax.shard_map(local, mesh=mesh, in_specs=in_specs, out_specs=out_specs, check_vma=False)
```

time: 896 us -> 74.5 us (0.08)
  starting transfers between devices: 443 us -> 28.5 us
  waiting for transfers between devices: 191 us -> 9.3 us
  other arithmetic: 131 us -> 0.08 us
  blocking collectives: 61 us -> 0 us
  local copies, waits for them, and re-layouts: 54 us -> 6.52 us
  Pallas kernels: 0 us -> 28.9 us
    ppermute x132 -> x14, starting transfers between devices: 443 us -> 28.5 us  [the longest x6 11.7 us: exchange(): got_strips.append(lax.ppermute(strip, ('gx', 'gy'), pairs))]
    ppermute x132 -> x14, waiting for transfers between devices: 191 us -> 9.3 us  [the longest x4 7.83 us: local(): summed = summed + lax.ppermute(summed, axis, pairs)]
    add x49 -> x4, other arithmetic: 91 us -> 0.08 us  [local(): summed = summed + lax.ppermute(summed, axis, pairs)]
    psum x1 -> x0, blocking collectives: 61 us -> none  [local(): lax.psum((gradient_part, objective_part), ('gx', 'gy', 'sa'))]
    slice x83 -> x2, local copies, waits for them, and re-layouts: 33.4 us -> 1.12 us  [the longest x1 0.61 us: local(): summed[0, :number]]
    pallas_call x0 -> x5, Pallas kernels: none -> 28.9 us  [the longest x1 11.8 us: local(): pl.pallas_call(functools.partial(adjoint_kernel, kinds, 0.5 / (tail_count...]
    mul x18 -> x0, other arithmetic: 23.9 us -> none  [the longest x16 23.4 us: adjoint_local(): scaled = outer[0] * padded]
  transfers between devices with their start and end apart: 132 -> 14, of which waited for: 96 -> 6; matrix products, arithmetic and copies ran while one was open for 10% -> 0% of each run, Pallas kernels for 0% -> 7%
where the time goes in v1:
time: 74.5 us; the launch traced here: 74.1 us
  Pallas kernels  28.9 us (39%)
  starting transfers between devices  28.5 us (38%)
  waiting for transfers between devices  9.3 us (12%)
  local copies, waits for them, and re-layouts  6.52 us (9%)
  between operations  0.83 us (1%)
    pallas_call x1, Pallas kernels, local(): pl.pallas_call(functools.partial(adjoint_kernel, kinds, 0.5 / (tail_count...  11.8 us
    ppermute x6, starting transfers between devices, exchange(): got_strips.append(lax.ppermute(strip, ('gx', 'gy'), pairs))  11.7 us
    pallas_call x1, Pallas kernels, local(): pl.pallas_call(functools.partial(forward_kernel, kinds, tail_count), out_...  11.4 us
    ppermute x4, starting transfers between devices, exchange(): lax.ppermute(tile, 'gx', tile_pairs(partner, count_x))  9.01 us
    ppermute x4, waiting for transfers between devices, local(): summed = summed + lax.ppermute(summed, axis, pairs)  7.83 us
    ppermute x4, starting transfers between devices, local(): summed = summed + lax.ppermute(summed, axis, pairs)  7.78 us
    unnamed x26, local copies, waits for them, and re-layouts  5.4 us
    pallas_call x1, Pallas kernels, local(): pl.pallas_call(functools.partial(source_kernel, kinds), out_shape=(shape(...  4.27 us
  transfers between devices with their start and end apart: 14, of which 6 were waited for; matrix products, arithmetic and copies ran while one was open for 0% of the time, Pallas kernels for 7%

profile of v1, /device:TPU:0, one launch (start us, length us, event | category | flops | bytes accessed | tf_op | source)
XLA Modules:
  0.0 74.1 jit_solution(15505271388049741664)
XLA Ops:
  0.7 1.1 %copy-done.1 = f32[4,4,32,128]{3,2,1,0:T(8,128)S(1)} copy-done((f32[4,4,32,128]{3,2,1,0:T(8,128)S(1)}, f32[4,4,32,128]{3,2,1,0:T(8,128)}, u32[]{:S(2)}) %copy-start.1) | copy-done | bytes 262168
  1.7 0.9 %copy-done.3 = f32[4,4,32,128]{3,2,1,0:T(8,128)S(1)} copy-done((f32[4,4,32,128]{3,2,1,0:T(8,128)S(1)}, f32[4,4,32,128]{3,2,1,0:T(8,128)}, u32[]{:S(2)}) %copy-start.3) | copy-done | bytes 262168
  2.7 0.9 %copy-done.5 = f32[4,4,32,128]{3,2,1,0:T(8,128)S(1)} copy-done((f32[4,4,32,128]{3,2,1,0:T(8,128)S(1)}, f32[4,4,32,128]{3,2,1,0:T(8,128)}, u32[]{:S(2)}) %copy-start.5) | copy-done | bytes 262168
  3.6 0.9 %copy-done.7 = f32[4,4,32,128]{3,2,1,0:T(8,128)S(1)} copy-done((f32[4,4,32,128]{3,2,1,0:T(8,128)S(1)}, f32[4,4,32,128]{3,2,1,0:T(8,128)}, u32[]{:S(2)}) %copy-start.7) | copy-done | bytes 262168
  4.6 0.2 split.1
  4.8 3.1 %collective-permute-start = (f32[4,4,4,16,128]{4,3,2,1,0:T(8,128)S(1)}, f32[4,4,4,16,128]{4,3,2,1,0:T(8,128)S(1)}, u32[]{:S(2)}, u32[]{:S(2)}) collective-permute-start(f32[4,4,4,16,128]{4,3,2,1,0:T(8,128)S(1)} %get-tuple-element.17), channel_id=1, source_target_pairs={{4,0},{0,4},{12,8},{8,12},{5,1},{1,5},{13,9},{9,13},{6,2},{2,6},{1... | collective-permute-start | bytes 1572872 | tf_op jit(solution)/shard_map/ppermute | solution.py:576
  7.9 0.7 collective-permute-start.1
  8.6 1.2 %strips.1 = (f32[2,8,2,8,128]{4,3,2,1,0:T(8,128)S(1)}, f32[8,2,8,128]{3,2,1,0:T(8,128)S(1)}, f32[8,2,8,128]{3,2,1,0:T(8,128)S(1)}) custom-call(f32[512,128]{1,0:T(8,128)S(1)} %bitcast.21, f32[512,128]{1,0:T(8,128)S(1)} %bitcast.12, f32[512,128]{1,0:T(8,128)S(1)} %bitcast.15, f32[512,128]{1,0:T(8,128)S(1)} %bitcast.18), custom_call_target="tpu_custom_call" | custom-call | tf_op jit(solution)/shard_map/strips/pallas_call | solution.py:611
  9.8 1.5 %collective-permute-start.2 = (f32[2,8,2,8,128]{4,3,2,1,0:T(8,128)S(1)}, f32[2,8,2,8,128]{4,3,2,1,0:T(8,128)S(1)}, u32[]{:S(2)}, u32[]{:S(2)}) collective-permute-start(f32[2,8,2,8,128]{4,3,2,1,0:T(8,128)S(1)} %get-tuple-element.19), channel_id=1, source_target_pairs={{2,0},{0,2},{6,4},{4,6},{10,8},{8,10},{14,12},{12,14},{3,1},{1,3},... | collective-permute-start | bytes 393224 | tf_op jit(solution)/shard_map/ppermute | solution.py:585
  11.4 4.3 %collective-permute-start.3 = (f32[8,2,8,128]{3,2,1,0:T(8,128)S(1)}, f32[8,2,8,128]{3,2,1,0:T(8,128)S(1)}, u32[]{:S(2)}, u32[]{:S(2)}) collective-permute-start(f32[8,2,8,128]{3,2,1,0:T(8,128)S(1)} %get-tuple-element.20), channel_id=1, source_target_pairs={{6,0},{4,2},{2,4},{0,6},{14,8},{12,10},{10,12},{8,14},{7,1},{5,3},... | collective-permute-start | bytes 196616 | tf_op jit(solution)/shard_map/ppermute | solution.py:585
  15.7 0.7 collective-permute-start.4
  16.4 0.7 copy-done.9
  17.1 0.7 copy-done.11
  17.8 4.3 %source.1 = (f32[64,2,8,128]{3,2,1,0:T(8,128)S(1)}, f32[8,2,8,128]{3,2,1,0:T(8,128)S(1)}) custom-call(s32[1,4096]{1,0:T(1,128)S(1)} %bitcast.27, f32[1,4096]{1,0:T(1,128)S(1)} %bitcast.30, f32[4096,128]{1,0:T(8,128)S(1)} %copy-done), custom_call_target="tpu_custom_call" | custom-call | tf_op jit(solution)/shard_map/source/pallas_call | solution.py:622
  22.1 0.2 collective-permute-done.3.refs_9_.refs_6_
  22.4 11.4 %forward.1 = (f32[512,128]{1,0:T(8,128)}, f32[16,2,8,128]{3,2,1,0:T(8,128)S(1)}, f32[16,2,8,128]{3,2,1,0:T(8,128)S(1)}, f32[8,128]{1,0:T(8,128)S(1)}, f32[8,8,12...) custom-call(f32[512,128]{1,0:T(8,128)S(1)} %bitcast.22, f32[512,128]{1,0:T(8,128)S(1)} %bitcast.13, ...), custom_call_target="tpu_custom_call" | custom-call | tf_op jit(solution)/shard_map/forward/pallas_call | solution.py:641
  33.8 4.6 %collective-permute-start.5 = (f32[16,2,8,128]{3,2,1,0:T(8,128)S(1)}, f32[16,2,8,128]{3,2,1,0:T(8,128)S(1)}, u32[]{:S(2)}, u32[]{:S(2)}) collective-permute-start(f32[16,2,8,128]{3,2,1,0:T(8,128)S(1)} %get-tuple-element.25.refs_8_), channel_id=1, source_target_pairs={{4,0},{0,4},{12,8},{8,12},{5,1},{1,5},{13,9},{9,13},{6,2},{2,6},{1... | collective-permute-start | bytes 393224 | tf_op jit(solution)/shard_map/ppermute | solution.py:576
  38.4 0.7 collective-permute-start.6
  39.0 0.6 collective-permute-start.7
  39.7 3.9 %collective-permute-start.8 = (f32[8,8,128]{2,1,0:T(8,128)S(1)}, f32[8,8,128]{2,1,0:T(8,128)S(1)}, u32[]{:S(2)}, u32[]{:S(2)}) collective-permute-start(f32[8,8,128]{2,1,0:T(8,128)S(1)} %get-tuple-element.28), channel_id=1, source_target_pairs={{6,0},{4,2},{2,4},{0,6},{14,8},{12,10},{10,12},{8,14},{7,1},{5,3},... | collective-permute-start | bytes 98312 | tf_op jit(solution)/shard_map/ppermute | solution.py:585
  43.6 0.7 collective-permute-start.9
  44.2 1.2 %collective-permute-done.8.refs_13_ = f32[8,8,128]{2,1,0:T(8,128)S(1)} collective-permute-done((f32[8,8,128]{2,1,0:T(8,128)S(1)}, f32[8,8,128]{2,1,0:T(8,128)S(1)}, u32[]{:S(2)}, u32[]{:S(2)}) %collective-permute-start.8) | collective-permute-done | bytes 32800 | tf_op jit(solution)/shard_map/ppermute | solution.py:585
  45.5 11.8 %adjoint.1 = f32[1,4224]{1,0:T(1,128)S(1)} custom-call(f32[512,128]{1,0:T(8,128)S(1)} %bitcast.14, f32[512,128]{1,0:T(8,128)S(1)} %bitcast.17, f32[512,128]{1,0:T(8,128)S(1)} %bitcast.20, f32[4,256,128]{2,1,0:T(8,128)S(1)} %bitcast.24, f32[4,256,128]{2,1,0:T(8,128)S(1)} %bitcast.26, f32[2,8,2,8,128]{4,3,2,1,0:T(8,128)S(1)} %collective-permute-done.2.refs_8_.refs_5_, ...), custom_call_target="tpu_custom_call" | custom-call | tf_op jit(solution)/shard_map/adjoint/pallas_call | solution.py:661
  57.3 1.2 %collective-permute-done.10 = f32[1,4224]{1,0:T(1,128)S(1)} collective-permute-done((f32[1,4224]{1,0:T(1,128)S(1)}, f32[1,4224]{1,0:T(1,128)S(1)}, u32[]{:S(2)}, u32[]{:S(2)}) %collective-permute-start.10) | collective-permute-done | bytes 16928 | tf_op jit(solution)/shard_map/ppermute | solution.py:690
  58.5 0.6 collective-permute-start.11
  59.1 3.2 %collective-permute-done.11 = f32[1,4224]{1,0:T(1,128)S(1)} collective-permute-done((f32[1,4224]{1,0:T(1,128)S(1)}, f32[1,4224]{1,0:T(1,128)S(1)}, u32[]{:S(2)}, u32[]{:S(2)}) %collective-permute-start.11) | collective-permute-done | bytes 16928 | tf_op jit(solution)/shard_map/ppermute | solution.py:690
  62.3 3.9 %collective-permute-start.12 = (f32[1,4224]{1,0:T(1,128)S(1)}, f32[1,4224]{1,0:T(1,128)S(1)}, u32[]{:S(2)}, u32[]{:S(2)}) collective-permute-start(f32[1,4224]{1,0:T(1,128)S(1)} %add.13), channel_id=1, source_target_pairs={{0,4},{4,0},{8,12},{12,8},{1,5},{5,1},{9,13},{13,9},{2,6},{6,2},{1... | collective-permute-start | bytes 50696 | tf_op jit(solution)/shard_map/ppermute | solution.py:690
  66.3 1.7 %collective-permute-done.12 = f32[1,4224]{1,0:T(1,128)S(1)} collective-permute-done((f32[1,4224]{1,0:T(1,128)S(1)}, f32[1,4224]{1,0:T(1,128)S(1)}, u32[]{:S(2)}, u32[]{:S(2)}) %collective-permute-start.12) | collective-permute-done | bytes 16928 | tf_op jit(solution)/shard_map/ppermute | solution.py:690
  68.0 3.2 %collective-permute-start.13 = (f32[1,4224]{1,0:T(1,128)S(1)}, f32[1,4224]{1,0:T(1,128)S(1)}, u32[]{:S(2)}, u32[]{:S(2)}) collective-permute-start(f32[1,4224]{1,0:T(1,128)S(1)} %add.14), channel_id=1, source_target_pairs={{0,8},{4,12},{8,0},{12,4},{1,9},{5,13},{9,1},{13,5},{2,10},{6,14},... | collective-permute-start | bytes 50696 | tf_op jit(solution)/shard_map/ppermute | solution.py:690
  71.3 1.7 %collective-permute-done.13 = f32[1,4224]{1,0:T(1,128)S(1)} collective-permute-done((f32[1,4224]{1,0:T(1,128)S(1)}, f32[1,4224]{1,0:T(1,128)S(1)}, u32[]{:S(2)}, u32[]{:S(2)}) %collective-permute-start.13) | collective-permute-done | bytes 16928 | tf_op jit(solution)/shard_map/ppermute | solution.py:690
  73.0 0.5 slice.9
  73.5 0.6 slice.8
  (33 shorter events, 0.1 us)
Async XLA Ops:
  0.6 15.7 %copy-start = (f32[4096,128]{1,0:T(8,128)S(1)}, f32[4096,128]{1,0:T(8,128)}, u32[]{:S(2)}) copy-start(f32[4096,128]{1,0:T(8,128)} %refs_17_.1) | copy-start | bytes 6291460
  0.6 1.1 %copy-start.1 = (f32[4,4,32,128]{3,2,1,0:T(8,128)S(1)}, f32[4,4,32,128]{3,2,1,0:T(8,128)}, u32[]{:S(2)}) copy-start(f32[4,4,32,128]{3,2,1,0:T(8,128)} %retard.1) | copy-start | bytes 786436
  1.7 0.9 %copy-start.3 = (f32[4,4,32,128]{3,2,1,0:T(8,128)S(1)}, f32[4,4,32,128]{3,2,1,0:T(8,128)}, u32[]{:S(2)}) copy-start(f32[4,4,32,128]{3,2,1,0:T(8,128)} %velx.1) | copy-start | bytes 786436
  2.7 0.9 %copy-start.5 = (f32[4,4,32,128]{3,2,1,0:T(8,128)S(1)}, f32[4,4,32,128]{3,2,1,0:T(8,128)}, u32[]{:S(2)}) copy-start(f32[4,4,32,128]{3,2,1,0:T(8,128)} %vely.1) | copy-start | bytes 786436
  3.6 0.9 %copy-start.7 = (f32[4,4,32,128]{3,2,1,0:T(8,128)S(1)}, f32[4,4,32,128]{3,2,1,0:T(8,128)}, u32[]{:S(2)}) copy-start(f32[4,4,32,128]{3,2,1,0:T(8,128)} %initial.1) | copy-start | bytes 786436
  4.6 17.8 %copy-start.8 = (f32[4,4,32,128]{3,2,1,0:T(8,128)S(1)}, f32[4,4,32,128]{3,2,1,0:T(8,128)}, u32[]{:S(2)}) copy-start(f32[4,4,32,128]{3,2,1,0:T(8,128)} %initial.1) | copy-start | bytes 786436
  4.8 17.5 %collective-permute-start = (f32[4,4,4,16,128]{4,3,2,1,0:T(8,128)S(1)}, f32[4,4,4,16,128]{4,3,2,1,0:T(8,128)S(1)}, u32[]{:S(2)}, u32[]{:S(2)}) collective-permute-start(f32[4,4,4,16,128]{4,3,2,1,0:T(8,128)S(1)} %get-tuple-element.17), channel_id=1, source_target_pairs={{4,0},{0,4},{12,8},{8,12},{5,1},{1,5},{13,9},{9,13},{6,2},{2,6},{1... | collective-permute-start | bytes 1572872 | tf_op jit(solution)/shard_map/ppermute | solution.py:576
  7.9 14.4 %collective-permute-start.1 = (f32[4,4,4,16,128]{4,3,2,1,0:T(8,128)S(1)}, f32[4,4,4,16,128]{4,3,2,1,0:T(8,128)S(1)}, u32[]{:S(2)}, u32[]{:S(2)}) collective-permute-start(f32[4,4,4,16,128]{4,3,2,1,0:T(8,128)S(1)} %get-tuple-element.18), channel_id=1, source_target_pairs={{8,4},{4,8},{9,5},{5,9},{10,6},{6,10},{11,7},{7,11},{24,20},{20,24... | collective-permute-start | bytes 1572872 | tf_op jit(solution)/shard_map/ppermute | solution.py:576
  9.8 12.5 %collective-permute-start.2 = (f32[2,8,2,8,128]{4,3,2,1,0:T(8,128)S(1)}, f32[2,8,2,8,128]{4,3,2,1,0:T(8,128)S(1)}, u32[]{:S(2)}, u32[]{:S(2)}) collective-permute-start(f32[2,8,2,8,128]{4,3,2,1,0:T(8,128)S(1)} %get-tuple-element.19), channel_id=1, source_target_pairs={{2,0},{0,2},{6,4},{4,6},{10,8},{8,10},{14,12},{12,14},{3,1},{1,3},... | collective-permute-start | bytes 393224 | tf_op jit(solution)/shard_map/ppermute | solution.py:585
  11.4 11.0 %collective-permute-start.3 = (f32[8,2,8,128]{3,2,1,0:T(8,128)S(1)}, f32[8,2,8,128]{3,2,1,0:T(8,128)S(1)}, u32[]{:S(2)}, u32[]{:S(2)}) collective-permute-start(f32[8,2,8,128]{3,2,1,0:T(8,128)S(1)} %get-tuple-element.20), channel_id=1, source_target_pairs={{6,0},{4,2},{2,4},{0,6},{14,8},{12,10},{10,12},{8,14},{7,1},{5,3},... | collective-permute-start | bytes 196616 | tf_op jit(solution)/shard_map/ppermute | solution.py:585
  15.7 6.6 %collective-permute-start.4 = (f32[8,2,8,128]{3,2,1,0:T(8,128)S(1)}, f32[8,2,8,128]{3,2,1,0:T(8,128)S(1)}, u32[]{:S(2)}, u32[]{:S(2)}) collective-permute-start(f32[8,2,8,128]{3,2,1,0:T(8,128)S(1)} %get-tuple-element.21), channel_id=1, source_target_pairs={{10,4},{8,6},{6,8},{4,10},{11,5},{9,7},{7,9},{5,11},{26,20},{24,22... | collective-permute-start | bytes 196616 | tf_op jit(solution)/shard_map/ppermute | solution.py:585
  16.4 0.7 copy-start.9
  17.1 0.7 copy-start.11
  17.8 4.6 %copy-start.10 = (f32[4,32,128]{2,1,0:T(8,128)S(1)}, f32[4,32,128]{2,1,0:T(8,128)}, u32[]{:S(2)}) copy-start(f32[4,32,128]{2,1,0:T(8,128)} %param.13) | copy-start | bytes 196612
  17.8 4.6 %copy-start.12 = (s32[4]{0:T(128)S(1)}, s32[4]{0:T(128)}, u32[]{:S(2)}) copy-start(s32[4]{0:T(128)} %refs_5_.1) | copy-start | bytes 52
  17.8 27.7 %copy-start.2 = (f32[4,4,32,128]{3,2,1,0:T(8,128)S(1)}, f32[4,4,32,128]{3,2,1,0:T(8,128)}, u32[]{:S(2)}) copy-start(f32[4,4,32,128]{3,2,1,0:T(8,128)} %retard.1) | copy-start | bytes 786436
  17.8 27.7 %copy-start.4 = (f32[4,4,32,128]{3,2,1,0:T(8,128)S(1)}, f32[4,4,32,128]{3,2,1,0:T(8,128)}, u32[]{:S(2)}) copy-start(f32[4,4,32,128]{3,2,1,0:T(8,128)} %velx.1) | copy-start | bytes 786436
  17.8 27.7 %copy-start.6 = (f32[4,4,32,128]{3,2,1,0:T(8,128)S(1)}, f32[4,4,32,128]{3,2,1,0:T(8,128)}, u32[]{:S(2)}) copy-start(f32[4,4,32,128]{3,2,1,0:T(8,128)} %vely.1) | copy-start | bytes 786436
  33.8 11.7 %collective-permute-start.5 = (f32[16,2,8,128]{3,2,1,0:T(8,128)S(1)}, f32[16,2,8,128]{3,2,1,0:T(8,128)S(1)}, u32[]{:S(2)}, u32[]{:S(2)}) collective-permute-start(f32[16,2,8,128]{3,2,1,0:T(8,128)S(1)} %get-tuple-element.25.refs_8_), channel_id=1, source_target_pairs={{4,0},{0,4},{12,8},{8,12},{5,1},{1,5},{13,9},{9,13},{6,2},{2,6},{1... | collective-permute-start | bytes 393224 | tf_op jit(solution)/shard_map/ppermute | solution.py:576
  38.4 7.1 %collective-permute-start.6 = (f32[16,2,8,128]{3,2,1,0:T(8,128)S(1)}, f32[16,2,8,128]{3,2,1,0:T(8,128)S(1)}, u32[]{:S(2)}, u32[]{:S(2)}) collective-permute-start(f32[16,2,8,128]{3,2,1,0:T(8,128)S(1)} %get-tuple-element.26.refs_9_), channel_id=1, source_target_pairs={{8,4},{4,8},{9,5},{5,9},{10,6},{6,10},{11,7},{7,11},{24,20},{20,24... | collective-permute-start | bytes 393224 | tf_op jit(solution)/shard_map/ppermute | solution.py:576
  39.0 5.2 %collective-permute-start.7 = (f32[8,8,128]{2,1,0:T(8,128)S(1)}, f32[8,8,128]{2,1,0:T(8,128)S(1)}, u32[]{:S(2)}, u32[]{:S(2)}) collective-permute-start(f32[8,8,128]{2,1,0:T(8,128)S(1)} %get-tuple-element.27), channel_id=1, source_target_pairs={{2,0},{0,2},{6,4},{4,6},{10,8},{8,10},{14,12},{12,14},{3,1},{1,3},... | collective-permute-start | bytes 98312 | tf_op jit(solution)/shard_map/ppermute | solution.py:585
  39.7 5.8 %collective-permute-start.8 = (f32[8,8,128]{2,1,0:T(8,128)S(1)}, f32[8,8,128]{2,1,0:T(8,128)S(1)}, u32[]{:S(2)}, u32[]{:S(2)}) collective-permute-start(f32[8,8,128]{2,1,0:T(8,128)S(1)} %get-tuple-element.28), channel_id=1, source_target_pairs={{6,0},{4,2},{2,4},{0,6},{14,8},{12,10},{10,12},{8,14},{7,1},{5,3},... | collective-permute-start | bytes 98312 | tf_op jit(solution)/shard_map/ppermute | solution.py:585
  43.6 1.9 %collective-permute-start.9 = (f32[8,8,128]{2,1,0:T(8,128)S(1)}, f32[8,8,128]{2,1,0:T(8,128)S(1)}, u32[]{:S(2)}, u32[]{:S(2)}) collective-permute-start(f32[8,8,128]{2,1,0:T(8,128)S(1)} %get-tuple-element.29), channel_id=1, source_target_pairs={{10,4},{8,6},{6,8},{4,10},{11,5},{9,7},{7,9},{5,11},{26,20},{24,22... | collective-permute-start | bytes 98312 | tf_op jit(solution)/shard_map/ppermute | solution.py:585
  57.3 1.2 %collective-permute-start.10 = (f32[1,4224]{1,0:T(1,128)S(1)}, f32[1,4224]{1,0:T(1,128)S(1)}, u32[]{:S(2)}, u32[]{:S(2)}) collective-permute-start(f32[1,4224]{1,0:T(1,128)S(1)} %adjoint.1), channel_id=1, source_target_pairs={{0,1},{1,0},{2,3},{3,2},{4,5},{5,4},{6,7},{7,6},{8,9},{9,8},{10,11... | collective-permute-start | bytes 50696 | tf_op jit(solution)/shard_map/ppermute | solution.py:690
  58.5 3.8 %collective-permute-start.11 = (f32[1,4224]{1,0:T(1,128)S(1)}, f32[1,4224]{1,0:T(1,128)S(1)}, u32[]{:S(2)}, u32[]{:S(2)}) collective-permute-start(f32[1,4224]{1,0:T(1,128)S(1)} %add.12), channel_id=1, source_target_pairs={{0,2},{2,0},{1,3},{3,1},{4,6},{6,4},{5,7},{7,5},{8,10},{10,8},{9,1... | collective-permute-start | bytes 50696 | tf_op jit(solution)/shard_map/ppermute | solution.py:690
  62.3 5.7 %collective-permute-start.12 = (f32[1,4224]{1,0:T(1,128)S(1)}, f32[1,4224]{1,0:T(1,128)S(1)}, u32[]{:S(2)}, u32[]{:S(2)}) collective-permute-start(f32[1,4224]{1,0:T(1,128)S(1)} %add.13), channel_id=1, source_target_pairs={{0,4},{4,0},{8,12},{12,8},{1,5},{5,1},{9,13},{13,9},{2,6},{6,2},{1... | collective-permute-start | bytes 50696 | tf_op jit(solution)/shard_map/ppermute | solution.py:690
  68.0 4.9 %collective-permute-start.13 = (f32[1,4224]{1,0:T(1,128)S(1)}, f32[1,4224]{1,0:T(1,128)S(1)}, u32[]{:S(2)}, u32[]{:S(2)}) collective-permute-start(f32[1,4224]{1,0:T(1,128)S(1)} %add.14), channel_id=1, source_target_pairs={{0,8},{4,12},{8,0},{12,4},{1,9},{5,13},{9,1},{13,5},{2,10},{6,14},... | collective-permute-start | bytes 50696 | tf_op jit(solution)/shard_map/ppermute | solution.py:690

commit v2 on v1

v2 whole, which is shorter than its diff:
```python
import functools

import jax
import jax.numpy as jnp
from jax import lax
from jax.experimental import pallas as pl
from jax.experimental.pallas import tpu as pltpu
from jax.sharding import PartitionSpec as P

ITERS = 16
KAPPA = 0.1
VERT = 0.05
LANES = 128
SUBLANES = 8
DEPTH = ITERS
OWN = 2 * DEPTH
EXT = OWN + 2 * DEPTH
WIDE = 2 * DEPTH
GROUPS = LANES // WIDE
INNER = EXT // GROUPS
JOIN = ITERS // 2
CHUNK = 512
PHASES = ((0, 4), (4, 8), (8, 12), (12, ITERS - 1))
VMEM_LIMIT = 24 * 1024 * 1024


def vmem():
    return pl.BlockSpec(memory_space=pltpu.VMEM)


def params():
    return pltpu.CompilerParams(vmem_limit_bytes=VMEM_LIMIT)


def sub_id():
    return lax.broadcasted_iota(jnp.int32, (SUBLANES, LANES), 0)


def lane_id():
    return lax.broadcasted_iota(jnp.int32, (SUBLANES, LANES), 1)


def wrap(shift):
    return shift % LANES if isinstance(shift, int) else lax.rem(shift, LANES)


def lane_roll(value, shift):
    if isinstance(shift, int) and shift % LANES == 0:
        return value
    return pltpu.roll(value, wrap(shift), 1)


def pick(flag, yes, no):
    if isinstance(flag, bool):
        return yes if flag else no
    return jnp.where(flag, yes, no)


def odd_tile():
    return lax.rem(lax.axis_index("gx"), 2)


def lacks_b():
    x = lax.axis_index("gx")
    return (x == 0) | (x == lax.axis_size("gx") - 1)


def strip_kinds(count):
    return (None,) if count == 2 else (True, False)


def is_right(kind):
    return lax.axis_index("gy") == 0 if kind is None else kind


def planes(ref, row, half, rows):
    return ref[pl.ds(half * rows + row, SUBLANES, stride=2 * rows), :]


def stage_kernel(initial, retard, velx, vely, monitor, controls, wells, *refs):
    own, out_a, out_b, out_monitor, out_controls, out_wells, sems = refs
    odd = odd_tile()
    pairs = [(monitor, out_monitor), (controls, out_controls), (wells, out_wells)]
    for field, ref in enumerate((initial, retard, velx, vely)):
        for out, base in ((out_a, DEPTH * (1 - odd)), (out_b, DEPTH * odd)):
            source = ref.at[:, :, pl.ds(pl.multiple_of(base, DEPTH), DEPTH), :]
            pairs.append((source, out.at[field]))
        pairs.append((ref, own.at[field]))
    copies = [pltpu.make_async_copy(*pair, sems.at[k]) for k, pair in enumerate(pairs)]
    for copy in copies:
        copy.start()
    for copy in copies:
        copy.wait()


def edge_offset(kind):
    return DEPTH * (1 - lax.axis_index("gy")) if kind is None else (0 if kind else DEPTH)


def strip_pack_kernel(kinds, own, *outs):
    odd = odd_tile()
    slot = lane_id() // DEPTH
    for number, kind in enumerate(kinds):
        to_y, to_a, to_b = outs[3 * number : 3 * number + 3]
        offset = edge_offset(kind)

        def put(packed, field, row, half, target):
            moved = lane_roll(planes(own.at[field], row, half, OWN), DEPTH * target + offset)
            return moved if packed is None else jnp.where(slot == target, moved, packed)

        for half in range(2):
            for i in range(INNER):
                packed = None
                for field in range(4):
                    for j in range(2):
                        target = 4 * (field // 2) + 2 * j + field % 2
                        packed = put(packed, field, INNER * j + i, half, target)
                to_y[i, half] = packed
            for out, base in ((to_a, DEPTH * (1 - odd)), (to_b, DEPTH * odd)):
                for i in range(INNER // 2):
                    packed = None
                    for field in range(4):
                        for upper in range(2):
                            row = base + INNER // 2 * upper + i
                            packed = put(packed, field, row, half, 4 * upper + field)
                    out[i, half] = packed


def coefficients(retard, velx, vely):
    spread = KAPPA * retard
    from_x = retard * velx + spread
    from_y = retard * vely + spread
    keep = 1.0 - (from_x + from_y + (2.0 + 2.0 * VERT / KAPPA) * spread)
    return keep, from_x, from_y, spread


def store_tile(refs, row, half, raw, source=None):
    state, retard, velx, vely = raw
    keep, from_x, from_y, spread = coefficients(retard, velx, vely)
    from_y = jnp.where(lane_id() == 0, 0.0, from_y)
    for ref, value in zip(refs, (state, keep, from_x, from_y, spread)):
        ref[row, half] = value


def source_kernel(kinds, wells, controls, profile, own, *refs):
    n = len(kinds)
    sources, tile, edges, (acc, acc_low) = split_refs(refs, 1 + n, 5, 1, 2)
    for x in range(OWN):
        for half in range(2):
            raw = [planes(own.at[field], x, half, OWN) for field in range(4)]
            store_tile(tile, DEPTH + x, half, raw)
    first_j = lane_id() // WIDE == 1
    for field in range(4):
        for i in range(INNER):
            for half in range(2):
                moved = [
                    lane_roll(planes(own.at[field], INNER * j + i, half, OWN), WIDE * (j + 1) + DEPTH)
                    for j in range(2)
                ]
                edges[0][field, i, half] = jnp.where(first_j, *moved)

    x_index, y_index = lax.axis_index("gx"), lax.axis_index("gy")
    all_x, all_blocks = OWN * lax.axis_size("gx"), lax.axis_size("gy")
    layers = 4
    per_block = EXT * layers
    r = lax.broadcasted_iota(jnp.int32, (per_block, 1), 0)
    x = x_index * OWN - DEPTH + r // layers
    ids = []
    for block in [y_index] + [
        1 - y_index if kind is None else (y_index + 1 if kind else y_index - 1) for kind in kinds
    ]:
        inside = (x >= 0) & (x < all_x) & (block >= 0) & (block < all_blocks)
        ids.append(jnp.where(inside, ((r % layers) * all_x + x) * all_blocks + block, -1))
    ids = jnp.concatenate(ids, axis=0)
    acc[...] = jnp.zeros_like(acc)
    acc_low[...] = jnp.zeros_like(acc_low)

    def chunk(c, carry):
        span = pl.ds(pl.multiple_of(c * CHUNK, CHUNK), CHUNK)
        part = profile[span, :]
        high = part.astype(jnp.bfloat16)
        low = (part - high.astype(jnp.float32)).astype(jnp.bfloat16)
        rate = controls[:, span]
        rate_high = rate.astype(jnp.bfloat16).astype(jnp.float32)
        hit = ids == wells[:, span]
        hot_high = jnp.where(hit, rate_high, 0.0).astype(jnp.bfloat16)
        hot_low = jnp.where(hit, rate - rate_high, 0.0).astype(jnp.bfloat16)
        acc[...] += jnp.dot(
            hot_high, jnp.concatenate([high, low], axis=1), preferred_element_type=jnp.float32
        )
        acc_low[...] += jnp.dot(hot_low, high, preferred_element_type=jnp.float32)
        return carry

    lax.fori_loop(0, wells.shape[1] // CHUNK, chunk, 0)
    acc_low[...] += acc[:, :LANES] + acc[:, LANES:]
    upper = sub_id() % 2 == 1
    group = lane_id() // WIDE

    def both(first, half):
        low_layer = jnp.broadcast_to(acc_low[pl.ds(first + half, 1), :], (SUBLANES, LANES))
        high_layer = jnp.broadcast_to(acc_low[pl.ds(first + 2 + half, 1), :], (SUBLANES, LANES))
        return jnp.where(upper, high_layer, low_layer)

    masks = Masks(kinds)
    for number in range(n):
        for i in range(INNER):
            for half in range(2):
                packed = None
                for j in range(GROUPS):
                    e = j * INNER + i
                    here = both(e * layers, half)
                    if number == 0:
                        sources[0][e, half] = here
                    beside = both((number + 1) * per_block + e * layers, half)
                    mixed = jnp.where(masks.own_edge[number], here, beside)
                    moved = lane_roll(mixed, WIDE * j + DEPTH)
                    packed = moved if packed is None else jnp.where(group == j, moved, packed)
                sources[1 + number][i, half] = packed


class Masks:
    def __init__(self, kinds):
        lane = lane_id()
        self.first, self.last = lane == 0, lane == LANES - 1
        self.group = lane // WIDE
        upper = sub_id() % 2 == 1
        self.below = jnp.where(upper, VERT / KAPPA, 0.0)
        self.above = jnp.where(upper, 0.0, VERT / KAPPA)
        self.right = [is_right(kind) for kind in kinds]
        half, eighth, sixteenth = lane % WIDE // DEPTH, lane // DEPTH, lane // JOIN
        self.rim = [half == pick(right, 1, 0) for right in self.right]
        self.not_rim = [half == pick(right, 0, 1) for right in self.right]
        self.own_edge = [eighth != pick(right, 0, LANES // DEPTH - 1) for right in self.right]
        self.outer = [sixteenth == pick(right, LANES // JOIN - 1, 0) for right in self.right]

    def vertical(self, pair):
        low = (VERT / KAPPA) * pair[1] + self.below * pltpu.roll(pair[1], 1, 0)
        high = (VERT / KAPPA) * pair[0] + self.above * pltpu.roll(pair[0], SUBLANES - 1, 0)
        return low, high

    def outer_from(self, strips, e, half, value):
        j, i = divmod(e, INNER)
        for strip, outer in zip(strips, self.outer):
            value = jnp.where(outer, lane_roll(strip[i, half], LANES - DEPTH - WIDE * j), value)
        return value

    def join(self, tile, strips, first, last):
        for e in range(first, last + 1):
            j, i = divmod(e, INNER)
            for h in range(2):
                value = self.outer_from(strips, e, h, tile[e, h])
                tile[e, h] = value
                moved = lane_roll(value, WIDE * j + DEPTH)
                for strip, own in zip(strips, self.not_rim):
                    strip[i, h] = jnp.where((self.group == j) & own, moved, strip[i, h])


def places(odd):
    return DEPTH * (2 - odd), DEPTH * (1 + odd), 3 * DEPTH * (1 - odd), 3 * DEPTH * odd


def merge_strip(masks, number, odd, middle, own_a, own_b, rim_y, rim_a, rim_b):
    inner = (masks.group == 1) | (masks.group == 2)
    at_a = masks.group == 3 * (1 - odd)
    own = jnp.where(inner, middle, jnp.where(at_a, own_a, own_b))
    rim = jnp.where(inner, rim_y, jnp.where(at_a, rim_a, rim_b))
    return jnp.where(masks.rim[number], rim, own)


def forward_step(masks, tile, strips, first, last, sourced):
    state, keep, from_x, from_y, spread, source = tile
    before = [state[first - 1, h] for h in range(2)]
    here = [state[first, h] for h in range(2)]
    for e in range(first, last + 1):
        after = [state[e + 1, h] for h in range(2)]
        upright = masks.vertical(here)
        for h in range(2):
            y_high = jnp.where(masks.last, 0.0, lane_roll(here[h], LANES - 1))
            value = (
                keep[e, h] * here[h]
                + from_x[e, h] * before[h]
                + from_y[e, h] * lane_roll(here[h], 1)
                + spread[e, h] * (after[h] + y_high + upright[h])
            )
            state[e, h] = value + source[e, h] if sourced else value
        before, here = here, after
    for strip, keep, from_x, from_y, spread, source in strips:
        old = [strip[0, h] for h in range(2)]
        here = old
        before = [lane_roll(strip[INNER - 1, h], WIDE) for h in range(2)]
        for i in range(INNER):
            if i < INNER - 1:
                after = [strip[i + 1, h] for h in range(2)]
            else:
                after = [lane_roll(value, LANES - WIDE) for value in old]
            upright = masks.vertical(here)
            for h in range(2):
                value = (
                    keep[i, h] * here[h]
                    + from_x[i, h] * before[h]
                    + from_y[i, h] * lane_roll(here[h], 1)
                    + spread[i, h] * (after[h] + lane_roll(here[h], LANES - 1) + upright[h])
                )
                strip[i, h] = value + source[i, h] if sourced else value
            before, here = here, after


def adjoint_step(masks, tile, strips, first, last):
    state, keep, from_x, from_y, spread, total = tile

    def row(refs, e):
        state, _, from_x, from_y, spread, _ = refs
        value = [state[e, h] for h in range(2)]
        return (
            value,
            [from_x[e, h] * value[h] for h in range(2)],
            [from_y[e, h] * value[h] for h in range(2)],
            [spread[e, h] * value[h] for h in range(2)],
        )

    before, here = row(tile, first - 1), row(tile, first)
    for e in range(first, last + 1):
        after = row(tile, e + 1)
        value, _, by_y, by_spread = here
        upright = masks.vertical(by_spread)
        for h in range(2):
            y_low = jnp.where(masks.first, 0.0, lane_roll(by_spread[h], 1))
            fresh = (
                keep[e, h] * value[h]
                + (after[1][h] + before[3][h])
                + (y_low + lane_roll(by_y[h], LANES - 1))
                + upright[h]
            )
            state[e, h] = fresh
            if DEPTH <= e < DEPTH + OWN:
                total[e - DEPTH, h] += fresh
        before, here = here, after
    for refs in strips:
        strip, keep, from_x, from_y, spread, total = refs
        here = row(refs, 0)
        wrapped = [lane_roll(value, LANES - WIDE) for value in here[1]]
        last_row = row(refs, INNER - 1)
        before = (None, None, None, [lane_roll(value, WIDE) for value in last_row[3]])
        for i in range(INNER):
            after = row(refs, i + 1) if i < INNER - 1 else (None, wrapped, None, None)
            value, _, by_y, by_spread = here
            upright = masks.vertical(by_spread)
            for h in range(2):
                fresh = (
                    keep[i, h] * value[h]
                    + (after[1][h] + before[3][h])
                    + (lane_roll(by_spread[h], 1) + lane_roll(by_y[h], LANES - 1))
                    + upright[h]
                )
                strip[i, h] = fresh
                total[i, h] += fresh
            before, here = here, after


def sweep(step, join):
    for begin, end in PHASES:

        def body(_, carry, begin=begin):
            step(begin + 1, EXT - 2 - begin, True)
            return carry

        if begin == JOIN:
            join(begin, EXT - 1 - begin)
        lax.fori_loop(begin, end, body, 0)
    step(ITERS, EXT - 1 - ITERS, False)


def split_refs(refs, *counts):
    out = []
    for count in counts:
        out.append(refs[:count])
        refs = refs[count:]
    return out


def forward_kernel(kinds, tail_count, *refs):
    n = len(kinds)
    ins, got_strips, sources, tile, edges, outs, strips, out_strips, (start,) = split_refs(
        refs, 4, 3 * n, 1 + n, 5, 1, 4 + 5, 5 * n, 3 * n, 1
    )
    monitor, ranking, got_a, got_b = ins
    final, start_a, start_b, objective, *tile = outs
    odd = odd_tile()
    masks = Masks(kinds)
    state = tile[0]
    _, _, at_a, at_b = places(odd)
    present = jnp.where(lacks_b(), 0.0, 1.0)
    for x in range(DEPTH):
        for h in range(2):
            raw_a = [planes(got_a.at[field], x, h, DEPTH) for field in range(4)]
            raw_b = [planes(got_b.at[field], x, h, DEPTH) for field in range(4)]
            raw_b[:2] = [value * present for value in raw_b[:2]]
            store_tile(tile, at_a + x, h, raw_a)
            store_tile(tile, at_b + x, h, raw_b)
            i = x
            upper = i // (INNER // 2)
            for k in range(n):
                got = got_strips[3 * k : 3 * k + 3]
                side = pick(masks.right[k], DEPTH, 0)
                raw = []
                for field in range(4):
                    slot = DEPTH * (4 * upper + field)
                    rim_b = got[2][i % (INNER // 2), h]
                    rim_b = lane_roll(rim_b, 2 * at_b + side + LANES - slot)
                    raw.append(
                        merge_strip(
                            masks,
                            k,
                            odd,
                            edges[0][field, i, h],
                            lane_roll(raw_a[field], 2 * at_a + DEPTH),
                            lane_roll(raw_b[field], 2 * at_b + DEPTH),
                            lane_roll(
                                got[0][i, h], LANES + WIDE + side - 64 * (field // 2) - DEPTH * (field % 2)
                            ),
                            lane_roll(
                                got[1][i % (INNER // 2), h], 2 * at_a + side + LANES - slot
                            ),
                            rim_b * present if field < 2 else rim_b,
                        )
                    )
                mine = strips[5 * k : 5 * k + 5]
                for ref, value in zip(mine, (raw[0] + sources[1 + k][i, h], *coefficients(*raw[1:]))):
                    ref[i, h] = value
    for e in range(EXT):
        for h in range(2):
            state[e, h] += sources[0][e, h]
    strip_refs = [(*strips[5 * k : 5 * k + 5], sources[1 + k]) for k in range(n)]
    strip_states = [strip[0] for strip in strip_refs]

    def step(first, last, sourced):
        forward_step(masks, (*tile, sources[0]), strip_refs, first, last, sourced)

    sweep(step, functools.partial(masks.join, state, strip_states))

    sample = sub_id() // 2
    upper = sub_id() % 2 == 1
    tail = jnp.zeros((SUBLANES, LANES), jnp.float32)
    for s in range(4):
        tail = jnp.where(sample == s, jnp.where(ranking[s] < tail_count, 1.0, 0.0), tail)
    sums = [jnp.zeros((SUBLANES, LANES), jnp.float32) for _ in range(4)]
    for x in range(OWN):
        for h in range(2):
            fresh = masks.outer_from(strip_states, DEPTH + x, h, state[DEPTH + x, h])
            final[pl.ds(h * OWN + x, SUBLANES, stride=2 * OWN), :] = fresh
            low = jnp.broadcast_to(monitor[pl.ds(h * OWN + x, 1), :], (SUBLANES, LANES))
            high = jnp.broadcast_to(monitor[pl.ds((2 + h) * OWN + x, 1), :], (SUBLANES, LANES))
            weighted = tail * jnp.where(upper, high, low) * fresh
            start[x, h] = weighted * (1.0 / (tail_count * ITERS))
            sums[x % 4] = sums[x % 4] + weighted * fresh
    objective[...] = (sums[0] + sums[1]) + (sums[2] + sums[3])

    base_a, base_b = DEPTH * (1 - odd), DEPTH * odd
    for x in range(DEPTH):
        for h in range(2):
            start_a[x, h] = start[base_a + x, h]
            start_b[x, h] = start[base_b + x, h]
    slot = lane_id() // DEPTH
    for k, kind in enumerate(kinds):
        to_y, to_a, to_b = out_strips[3 * k : 3 * k + 3]
        offset = edge_offset(kind)

        def put(packed, row, h, target):
            moved = lane_roll(start[row, h], DEPTH * target + offset)
            return moved if packed is None else jnp.where(slot == target, moved, packed)

        for i in range(INNER // 2):
            packed = None
            for upper_half in range(2):
                for j in range(2):
                    for h in range(2):
                        row = INNER * j + INNER // 2 * upper_half + i
                        packed = put(packed, row, h, 4 * upper_half + 2 * j + h)
            to_y[i] = packed
        for out, base in ((to_a, base_a), (to_b, base_b)):
            for i in range(INNER // 4):
                packed = None
                for quarter in range(4):
                    for h in range(2):
                        packed = put(packed, base + INNER // 4 * quarter + i, h, 2 * quarter + h)
                out[i] = packed


def adjoint_kernel(kinds, scale, *refs):
    n = len(kinds)
    parts, part_strips, coefs, strip_coefs, rest, (state, total), strips, (rows,) = split_refs(
        refs, 4, 3 * n, 4, 4 * n, 4, 2, 2 * n, 1
    )
    objective, wells, profile, out = rest
    odd = odd_tile()
    masks = Masks(kinds)
    at = places(odd)
    for part, first in zip(parts, at):
        for x in range(DEPTH):
            for h in range(2):
                state[first + x, h] = part[x, h]
    strip_refs = []
    for k in range(n):
        strip, strip_total = strips[2 * k : 2 * k + 2]
        got_y, got_a, got_b = part_strips[3 * k : 3 * k + 3]
        side = pick(masks.right[k], DEPTH, 0)
        for i in range(INNER):
            eighth, quarter = divmod(i, INNER // 2)[0], divmod(i, INNER // 4)[0]
            for h in range(2):
                moved = [
                    lane_roll(part[i, h], 2 * first + DEPTH) for part, first in zip(parts, at)
                ]
                slot = DEPTH * (2 * quarter + h)
                strip[i, h] = merge_strip(
                    masks,
                    k,
                    odd,
                    jnp.where(masks.group == 2 - odd, moved[0], moved[1]),
                    moved[2],
                    moved[3],
                    lane_roll(got_y[i % (INNER // 2)], LANES + WIDE + side - 64 * eighth - DEPTH * h),
                    lane_roll(got_a[i % (INNER // 4)], 2 * at[2] + side + LANES - slot),
                    lane_roll(got_b[i % (INNER // 4)], 2 * at[3] + side + LANES - slot),
                )
        strip_refs.append((strip, *strip_coefs[4 * k : 4 * k + 4], strip_total))
        strip_total[...] = jnp.zeros_like(strip_total)
    total[...] = jnp.zeros_like(total)
    tile = (state, *coefs, total)

    def step(first, last, _):
        adjoint_step(masks, tile, strip_refs, first, last)

    sweep(step, functools.partial(masks.join, state, [refs[0] for refs in strip_refs]))
    totals = [refs[-1] for refs in strip_refs]
    for x in range(OWN):
        for h in range(2):
            value = masks.outer_from(totals, DEPTH + x, h, total[x, h])
            value = value + pltpu.roll(value, 4, 0)
            value = value + pltpu.roll(value, 2, 0)
            rows[pl.ds((2 * x + h) * 2, 2), :] = value[:2]
    count = rows.shape[0]
    r = lax.broadcasted_iota(jnp.int32, (count, 1), 0)
    layer = (r % 2) * 2 + (r // 2) % 2
    x = lax.axis_index("gx") * OWN + r // 4
    ids = (layer * (OWN * lax.axis_size("gx")) + x) * lax.axis_size("gy") + lax.axis_index("gy")
    field = rows[...]
    high = field.astype(jnp.bfloat16)
    low = (field - high.astype(jnp.float32)).astype(jnp.bfloat16)
    both = jnp.concatenate([high, low], axis=0)
    contract = (((1,), (1,)), ((), ()))
    controls = wells.shape[1]

    def chunk(c, carry):
        span = pl.ds(pl.multiple_of(c * CHUNK, CHUNK), CHUNK)
        share = profile[span, :]
        share_high = share.astype(jnp.bfloat16)
        share_low = (share - share_high.astype(jnp.float32)).astype(jnp.bfloat16)
        first = lax.dot_general(both, share_high, contract, preferred_element_type=jnp.float32)
        second = lax.dot_general(high, share_low, contract, preferred_element_type=jnp.float32)
        product = first[:count] + first[count:] + second
        chosen = jnp.where(ids == wells[:, span], product, 0.0)
        out[:, span] = jnp.sum(chosen, axis=0, keepdims=True)
        return carry

    lax.fori_loop(0, controls // CHUNK, chunk, 0)
    whole = jnp.sum(jnp.sum(objective[...], axis=0, keepdims=True), axis=1, keepdims=True)
    out[:, controls:] = jnp.broadcast_to(whole * scale, (1, LANES))


def shape(*dims):
    return jax.ShapeDtypeStruct(dims, jnp.float32)


def same(x, count):
    return x


def partner_a(x, count):
    return x ^ 1


def partner_b(x, count):
    other = x + 1 if x % 2 else x - 1
    return other if 0 <= other < count else None


AXES = ("gx", "gy", "sa")


def swap_pairs(partner, kind, count_x, count_y, count_s):
    pairs = []
    for x in range(count_x):
        for y in range(count_y):
            for s in range(count_s):
                from_x, from_s = partner(x, count_x), s
                from_y = y if kind == "tile" else 1 - y if kind is None else (y + 1 if kind else y - 1)
                if from_x is None:
                    from_x, from_y, from_s = x, y, s ^ 1
                if 0 <= from_y < count_y:
                    pairs.append(
                        ((from_x * count_y + from_y) * count_s + from_s, (x * count_y + y) * count_s + s)
                    )
    return pairs


def exchange(tiles, strips, kinds):
    counts = [lax.axis_size(axis) for axis in AXES]
    got = [
        lax.ppermute(tile, AXES, swap_pairs(partner, "tile", *counts))
        for tile, partner in zip(tiles, (partner_a, partner_b))
    ]
    got_strips = []
    for k, kind in enumerate(kinds):
        for strip, partner in zip(strips[3 * k : 3 * k + 3], (same, partner_a, partner_b)):
            got_strips.append(lax.ppermute(strip, AXES, swap_pairs(partner, kind, *counts)))
    return got, got_strips


def total_over(value, axes):
    count = 1
    for axis in axes:
        count *= lax.axis_size(axis)
    bit = 1
    while bit < count:
        bits = [bit] if 2 * bit >= count else [bit, 2 * bit, 3 * bit]
        got = [lax.ppermute(value, axes, [(i, i ^ b) for i in range(count)]) for b in bits]
        value = value + got[0]
        if len(got) == 3:
            value = value + (got[1] + got[2])
        bit *= 4
    return value


def local(initial, retard, velx, vely, monitor, controls, profile, wells, ranking):
    samples, layers, width_x, width_y = initial.shape
    count_x, count_y = lax.axis_size("gx"), lax.axis_size("gy")
    assert (samples, layers, width_x, width_y) == (4, 4, OWN, LANES)
    assert count_x % 2 == 0 and lax.axis_size("sa") == 2
    number = controls.shape[0]
    assert number % CHUNK == 0
    kinds = strip_kinds(count_y)
    n = len(kinds)
    half_tile = shape(4, samples, layers, DEPTH, LANES)
    hbm = pl.BlockSpec(memory_space=pltpu.HBM)
    any_space = pl.BlockSpec(memory_space=pl.ANY)
    own, *sent, monitor, controls, wells = pl.pallas_call(
        stage_kernel,
        out_shape=(
            shape(4, samples, layers, OWN, LANES),
            half_tile,
            half_tile,
            shape(*monitor.shape),
            shape(1, number),
            jax.ShapeDtypeStruct((1, number), jnp.int32),
        ),
        in_specs=[hbm] * 7,
        out_specs=(any_space,) * 6,
        scratch_shapes=[pltpu.SemaphoreType.DMA((15,))],
        compiler_params=params(),
        name="stage",
    )(initial, retard, velx, vely, monitor, controls.reshape(1, -1), wells.reshape(1, -1))
    own = own.reshape(4, -1, LANES)
    sent_strips = pl.pallas_call(
        functools.partial(strip_pack_kernel, kinds),
        out_shape=(
            shape(INNER, 2, SUBLANES, LANES),
            shape(INNER // 2, 2, SUBLANES, LANES),
            shape(INNER // 2, 2, SUBLANES, LANES),
        )
        * n,
        in_specs=[vmem()],
        out_specs=(vmem(),) * (3 * n),
        compiler_params=params(),
        name="strips",
    )(own)
    got, got_strips = exchange(sent, sent_strips, kinds)
    tile_shape = shape(EXT, 2, SUBLANES, LANES)
    strip_shape = shape(INNER, 2, SUBLANES, LANES)
    blocks = (1 + n) * EXT * layers
    prepared = pl.pallas_call(
        functools.partial(source_kernel, kinds),
        out_shape=(tile_shape,)
        + (strip_shape,) * n
        + (tile_shape,) * 5
        + (shape(4, INNER, 2, SUBLANES, LANES),),
        in_specs=[vmem()] * 4,
        out_specs=(vmem(),) * (1 + n + 5 + 1),
        scratch_shapes=[
            pltpu.VMEM((blocks, 2 * LANES), jnp.float32),
            pltpu.VMEM((blocks, LANES), jnp.float32),
        ],
        compiler_params=params(),
        name="source",
    )(wells, controls, profile, own)
    got = [part.reshape(4, -1, LANES) for part in got]
    tail_count = samples * lax.axis_size("sa") // 2
    half_start = shape(DEPTH, 2, SUBLANES, LANES)
    smem = pl.BlockSpec(memory_space=pltpu.SMEM)
    first_tile = 4 + 3 * n + 1 + n
    final, start_a, start_b, objective, *rest = pl.pallas_call(
        functools.partial(forward_kernel, kinds, tail_count),
        out_shape=(
            shape(samples * layers * OWN, LANES),
            half_start,
            half_start,
            shape(SUBLANES, LANES),
        )
        + (tile_shape,) * 5
        + (strip_shape,) * (5 * n)
        + (
            shape(INNER // 2, SUBLANES, LANES),
            shape(INNER // 4, SUBLANES, LANES),
            shape(INNER // 4, SUBLANES, LANES),
        )
        * n,
        in_specs=[vmem(), smem] + [vmem()] * (2 + 3 * n + 1 + n + 5 + 1),
        out_specs=(vmem(),) * (4 + 5 + 5 * n + 3 * n),
        scratch_shapes=[pltpu.VMEM((OWN, 2, SUBLANES, LANES), jnp.float32)],
        input_output_aliases={first_tile + k: 4 + k for k in range(5)},
        compiler_params=params(),
        name="forward",
    )(monitor.reshape(-1, LANES), ranking, *got, *got_strips, *prepared)
    tile, strips, start_strips = split_refs(rest, 5, 5 * n, 3 * n)
    start = (start_a, start_b)
    got_start, got_start_strips = exchange(start, start_strips, kinds)
    strip_coefs = [strips[5 * k + c] for k in range(n) for c in range(1, 5)]
    cells = layers * OWN * count_x * LANES * count_y
    summed = pl.pallas_call(
        functools.partial(adjoint_kernel, kinds, 0.5 / (tail_count * cells)),
        out_shape=shape(1, number + LANES),
        in_specs=[vmem()] * (4 + 3 * n + 4 + 4 * n + 3),
        out_specs=vmem(),
        scratch_shapes=[
            pltpu.VMEM((EXT, 2, SUBLANES, LANES), jnp.float32),
            pltpu.VMEM((OWN, 2, SUBLANES, LANES), jnp.float32),
        ]
        + [pltpu.VMEM((INNER, 2, SUBLANES, LANES), jnp.float32)] * (2 * n)
        + [pltpu.VMEM((OWN * layers, LANES), jnp.float32)],
        compiler_params=params(),
        name="adjoint",
    )(
        *start,
        *got_start,
        *got_start_strips,
        *tile[1:],
        *strip_coefs,
        objective,
        wells,
        profile,
    )
    summed = total_over(summed, AXES)
    return final.reshape(initial.shape), summed[0, :number], summed[0, number : number + 1]


def solution(mesh):
    in_specs = (
        P(("groups", "sa"), None, "gx", "gy"),
        P(("groups", "sa"), None, "gx", "gy"),
        P(("groups", "sa"), None, "gx", "gy"),
        P(("groups", "sa"), None, "gx", "gy"),
        P("groups", "gx", "gy"),
        P("groups"),
        P("groups", None),
        P("groups"),
        P(("groups", "sa")),
    )
    out_specs = (P(("groups", "sa"), None, "gx", "gy"), P("groups"), P("groups"))
    return jax.shard_map(local, mesh=mesh, in_specs=in_specs, out_specs=out_specs, check_vma=False)
```

time: 74.5 us -> 64.5 us (0.87)
  starting transfers between devices: 28.5 us -> 20.5 us
  Pallas kernels: 28.9 us -> 25.4 us
  local copies, waits for them, and re-layouts: 6.52 us -> 7.34 us
  waiting for transfers between devices: 9.3 us -> 10.1 us
    ppermute x14 -> x16, starting transfers between devices: 28.5 us -> 20.5 us  [the longest x6 8.17 us: exchange(): lax.ppermute(strip, AXES, swap_pairs(partner, kind, *counts))]
    pallas_call x1, Pallas kernels: 11.8 us -> 9.09 us  [local(): pl.pallas_call(functools.partial(adjoint_kernel, kinds, 0.5 / (tail_count...]
    pallas_call x1, Pallas kernels: 11.4 us -> 8.96 us  [local(): pl.pallas_call(functools.partial(forward_kernel, kinds, tail_count), out_...]
    pallas_call x2, Pallas kernels: 4.51 us -> 6.14 us  [the longest x1 5.67 us: local(): pl.pallas_call(functools.partial(source_kernel, kinds), out_shape=(tile_s...]
    unnamed x26 -> x18, local copies, waits for them, and re-layouts: 5.4 us -> 6.22 us
    ppermute x14 -> x16, waiting for transfers between devices: 9.3 us -> 10.1 us  [the longest x6 5.48 us: total_over(): lax.ppermute(value, axes, [(i, i ^ b) for i in range(count)])]
  transfers between devices with their start and end apart: 14 -> 16, of which waited for: 6 -> 7; matrix products, arithmetic and copies ran while one was open for 0% -> 0% of each run, Pallas kernels for 7% -> 11%
where the time goes in v2:
time: 64.5 us; the launch traced here: 64.1 us
  Pallas kernels  25.4 us (39%)
  starting transfers between devices  20.5 us (32%)
  waiting for transfers between devices  10.1 us (16%)
  local copies, waits for them, and re-layouts  7.34 us (11%)
  between operations  0.73 us (1%)
    pallas_call x1, Pallas kernels, local(): pl.pallas_call(functools.partial(adjoint_kernel, kinds, 0.5 / (tail_count...  9.09 us
    pallas_call x1, Pallas kernels, local(): pl.pallas_call(functools.partial(forward_kernel, kinds, tail_count), out_...  8.96 us
    ppermute x6, starting transfers between devices, exchange(): lax.ppermute(strip, AXES, swap_pairs(partner, kind, *counts))  8.17 us
    ppermute x6, starting transfers between devices, total_over(): lax.ppermute(value, axes, [(i, i ^ b) for i in range(count)])  6.52 us
    unnamed x18, local copies, waits for them, and re-layouts  6.22 us
    ppermute x4, starting transfers between devices, exchange(): lax.ppermute(tile, AXES, swap_pairs(partner, 'tile', *counts))  5.79 us
    pallas_call x1, Pallas kernels, local(): pl.pallas_call(functools.partial(source_kernel, kinds), out_shape=(tile_s...  5.67 us
    ppermute x6, waiting for transfers between devices, total_over(): lax.ppermute(value, axes, [(i, i ^ b) for i in range(count)])  5.48 us
  transfers between devices with their start and end apart: 16, of which 7 were waited for; matrix products, arithmetic and copies ran while one was open for 0% of the time, Pallas kernels for 11%

profile of v2, /device:TPU:0, one launch (start us, length us, event | category | flops | bytes accessed | tf_op | source)
XLA Modules:
  0.0 64.1 jit_solution(16654530404666021643)
XLA Ops:
  0.7 1.1 %copy-done.1 = f32[4,4,32,128]{3,2,1,0:T(8,128)S(1)} copy-done((f32[4,4,32,128]{3,2,1,0:T(8,128)S(1)}, f32[4,4,32,128]{3,2,1,0:T(8,128)}, u32[]{:S(2)}) %copy-start.1) | copy-done | bytes 262168
  1.7 0.9 %copy-done.2 = f32[4,4,32,128]{3,2,1,0:T(8,128)S(1)} copy-done((f32[4,4,32,128]{3,2,1,0:T(8,128)S(1)}, f32[4,4,32,128]{3,2,1,0:T(8,128)}, u32[]{:S(2)}) %copy-start.2) | copy-done | bytes 262168
  2.7 0.9 %copy-done.3 = f32[4,4,32,128]{3,2,1,0:T(8,128)S(1)} copy-done((f32[4,4,32,128]{3,2,1,0:T(8,128)S(1)}, f32[4,4,32,128]{3,2,1,0:T(8,128)}, u32[]{:S(2)}) %copy-start.3) | copy-done | bytes 262168
  3.6 0.9 %copy-done.4 = f32[4,4,32,128]{3,2,1,0:T(8,128)S(1)} copy-done((f32[4,4,32,128]{3,2,1,0:T(8,128)S(1)}, f32[4,4,32,128]{3,2,1,0:T(8,128)}, u32[]{:S(2)}) %copy-start.4) | copy-done | bytes 262168
  4.6 0.8 %copy-done.5 = f32[4,32,128]{2,1,0:T(8,128)S(1)} copy-done((f32[4,32,128]{2,1,0:T(8,128)S(1)}, f32[4,32,128]{2,1,0:T(8,128)}, u32[]{:S(2)}) %copy-start.5) | copy-done | bytes 65560
  5.4 0.7 %copy-done.6 = f32[4096]{0:T(1024)S(1)} copy-done((f32[4096]{0:T(1024)S(1)}, f32[4096]{0:T(1024)}, u32[]{:S(2)}) %copy-start.6) | copy-done | bytes 16408
  6.2 0.7 %copy-done.7 = s32[4096]{0:T(1024)S(1)} copy-done((s32[4096]{0:T(1024)S(1)}, s32[4096]{0:T(1024)}, u32[]{:S(2)}) %copy-start.7) | copy-done | bytes 16408
  6.9 0.5 stage.1
  7.4 3.1 %collective-permute-start = (f32[4,4,4,16,128]{4,3,2,1,0:T(8,128)S(1)}, f32[4,4,4,16,128]{4,3,2,1,0:T(8,128)S(1)}, u32[]{:S(2)}, u32[]{:S(2)}) collective-permute-start(f32[4,4,4,16,128]{4,3,2,1,0:T(8,128)S(1)} %get-tuple-element.36), channel_id=1, source_target_pairs={{4,0},{5,1},{6,2},{7,3},{0,4},{1,5},{2,6},{3,7},{12,8},{13,9},{14,... | collective-permute-start | bytes 1572872 | tf_op jit(solution)/shard_map/ppermute | solution.py:609
  10.4 1.2 %strips.1 = (f32[16,2,8,128]{3,2,1,0:T(8,128)S(1)}, f32[8,2,8,128]{3,2,1,0:T(8,128)S(1)}, f32[8,2,8,128]{3,2,1,0:T(8,128)S(1)}) custom-call(f32[4,512,128]{2,1,0:T(8,128)S(1)} %bitcast.9), custom_call_target="tpu_custom_call" | custom-call | tf_op jit(solution)/shard_map/strips/pallas_call | solution.py:663
  11.6 1.6 %collective-permute-start.2 = (f32[16,2,8,128]{3,2,1,0:T(8,128)S(1)}, f32[16,2,8,128]{3,2,1,0:T(8,128)S(1)}, u32[]{:S(2)}, u32[]{:S(2)}) collective-permute-start(f32[16,2,8,128]{3,2,1,0:T(8,128)S(1)} %get-tuple-element.39), channel_id=1, source_target_pairs={{2,0},{3,1},{0,2},{1,3},{6,4},{7,5},{4,6},{5,7},{10,8},{11,9},{8,1... | collective-permute-start | bytes 393224 | tf_op jit(solution)/shard_map/ppermute | solution.py:615
  13.2 3.1 %collective-permute-start.3 = (f32[8,2,8,128]{3,2,1,0:T(8,128)S(1)}, f32[8,2,8,128]{3,2,1,0:T(8,128)S(1)}, u32[]{:S(2)}, u32[]{:S(2)}) collective-permute-start(f32[8,2,8,128]{3,2,1,0:T(8,128)S(1)} %get-tuple-element.40), channel_id=1, source_target_pairs={{6,0},{7,1},{4,2},{5,3},{2,4},{3,5},{0,6},{1,7},{14,8},{15,9},{12,... | collective-permute-start | bytes 196616 | tf_op jit(solution)/shard_map/ppermute | solution.py:615
  16.3 5.7 %source.1 = (f32[64,2,8,128]{3,2,1,0:T(8,128)S(1)}, f32[16,2,8,128]{3,2,1,0:T(8,128)S(1)}, f32[64,2,8,128]{3,2,1,0:T(8,128)S(1)}, f32[64,2,8,128]{3,2,1,0:T(8,12...) custom-call(s32[1,4096]{1,0:T(1,128)S(1)} %get-tuple-element.42.well, ...), custom_call_target="tpu_custom_call" | custom-call | tf_op jit(solution)/shard_map/source/pallas_call | solution.py:680
  22.0 2.9 %collective-permute-done.3.refs_5_ = f32[8,2,8,128]{3,2,1,0:T(8,128)S(1)} collective-permute-done((f32[8,2,8,128]{3,2,1,0:T(8,128)S(1)}, f32[8,2,8,128]{3,2,1,0:T(8,128)S(1)}, u32[]{:S(2)}, u32[]{:S(2)}) %collective-permute-start.3) | collective-permute-done | bytes 65568 | tf_op jit(solution)/shard_map/ppermute | solution.py:615
  24.9 9.0 %forward.1 = (f32[512,128]{1,0:T(8,128)}, f32[16,2,8,128]{3,2,1,0:T(8,128)S(1)}, f32[16,2,8,128]{3,2,1,0:T(8,128)S(1)}, f32[8,128]{1,0:T(8,128)S(1)}, f32[64,2,8...) custom-call(f32[128,128]{1,0:T(8,128)S(1)} %bitcast.13, ...), custom_call_target="tpu_custom_call", output_to_operand_aliasing={{4}: (9, {}), {5}: (10, {}), {6}: (11, {}), {7}: (12, {}), ... | custom-call | tf_op jit(solution)/shard_map/forward/pallas_call | solution.py:700
  33.9 2.7 %collective-permute-start.5 = (f32[16,2,8,128]{3,2,1,0:T(8,128)S(1)}, f32[16,2,8,128]{3,2,1,0:T(8,128)S(1)}, u32[]{:S(2)}, u32[]{:S(2)}) collective-permute-start(f32[16,2,8,128]{3,2,1,0:T(8,128)S(1)} %get-tuple-element.53.refs_0_), channel_id=1, source_target_pairs={{4,0},{5,1},{6,2},{7,3},{0,4},{1,5},{2,6},{3,7},{12,8},{13,9},{14,... | collective-permute-start | bytes 393224 | tf_op jit(solution)/shard_map/ppermute | solution.py:609
  36.6 0.5 collective-permute-start.7
  37.1 3.0 %collective-permute-start.8 = (f32[4,8,128]{2,1,0:T(8,128)S(1)}, f32[4,8,128]{2,1,0:T(8,128)S(1)}, u32[]{:S(2)}, u32[]{:S(2)}) collective-permute-start(f32[4,8,128]{2,1,0:T(8,128)S(1)} %get-tuple-element.56), channel_id=1, source_target_pairs={{6,0},{7,1},{4,2},{5,3},{2,4},{3,5},{0,6},{1,7},{14,8},{15,9},{12,... | collective-permute-start | bytes 49160 | tf_op jit(solution)/shard_map/ppermute | solution.py:615
  40.1 1.7 %collective-permute-done.8.refs_5_ = f32[4,8,128]{2,1,0:T(8,128)S(1)} collective-permute-done((f32[4,8,128]{2,1,0:T(8,128)S(1)}, f32[4,8,128]{2,1,0:T(8,128)S(1)}, u32[]{:S(2)}, u32[]{:S(2)}) %collective-permute-start.8) | collective-permute-done | bytes 16416 | tf_op jit(solution)/shard_map/ppermute | solution.py:615
  41.8 9.1 %adjoint.1 = f32[1,4224]{1,0:T(1,128)S(1)} custom-call(f32[16,2,8,128]{3,2,1,0:T(8,128)S(1)} %get-tuple-element.53.refs_0_, f32[16,2,8,128]{3,2,1,0:T(8,128)S(1)} %get-tuple-element.54.refs_1_, f32[16,2,8,128]{3,2,1,0:T(8,128)S(1)} %collective-permute-done.5.refs_2_, f32[16,2,8,128]{3,2,1,0:T(8,128)S(1)} %collective-permute-done.6.refs_3_, ...), custom_call_target="tpu_custom_call" | custom-call | tf_op jit(solution)/shard_map/adjoint/pallas_call | solution.py:728
  51.0 1.4 %collective-permute-start.11 = (f32[1,4224]{1,0:T(1,128)S(1)}, f32[1,4224]{1,0:T(1,128)S(1)}, u32[]{:S(2)}, u32[]{:S(2)}) collective-permute-start(f32[1,4224]{1,0:T(1,128)S(1)} %adjoint.1), channel_id=1, source_target_pairs={{0,2},{1,3},{2,0},{3,1},{4,6},{5,7},{6,4},{7,5},{8,10},{9,11},{10,... | collective-permute-start | bytes 50696 | tf_op jit(solution)/shard_map/ppermute | solution.py:626
  52.4 0.3 collective-permute-start.10
  52.7 1.5 %collective-permute-done.12 = f32[1,4224]{1,0:T(1,128)S(1)} collective-permute-done((f32[1,4224]{1,0:T(1,128)S(1)}, f32[1,4224]{1,0:T(1,128)S(1)}, u32[]{:S(2)}, u32[]{:S(2)}) %collective-permute-start.12) | collective-permute-done | bytes 16928 | tf_op jit(solution)/shard_map/ppermute | solution.py:626
  54.2 0.5 collective-permute-done.11
  54.8 2.7 %collective-permute-start.15 = (f32[1,4224]{1,0:T(1,128)S(1)}, f32[1,4224]{1,0:T(1,128)S(1)}, u32[]{:S(2)}, u32[]{:S(2)}) collective-permute-start(f32[1,4224]{1,0:T(1,128)S(1)} %add_add_fusion.1), channel_id=1, source_target_pairs={{0,12},{1,13},{2,14},{3,15},{4,8},{5,9},{6,10},{7,11},{8,4},{9,5},... | collective-permute-start | bytes 50696 | tf_op jit(solution)/shard_map/ppermute | solution.py:626
  57.5 1.7 %collective-permute-start.14 = (f32[1,4224]{1,0:T(1,128)S(1)}, f32[1,4224]{1,0:T(1,128)S(1)}, u32[]{:S(2)}, u32[]{:S(2)}) collective-permute-start(f32[1,4224]{1,0:T(1,128)S(1)} %add_add_fusion.1), channel_id=1, source_target_pairs={{0,8},{1,9},{2,10},{3,11},{4,12},{5,13},{6,14},{7,15},{8,0},{9,1},... | collective-permute-start | bytes 50696 | tf_op jit(solution)/shard_map/ppermute | solution.py:626
  59.2 0.3 collective-permute-start.13
  59.5 0.9 %collective-permute-done.15 = f32[1,4224]{1,0:T(1,128)S(1)} collective-permute-done((f32[1,4224]{1,0:T(1,128)S(1)}, f32[1,4224]{1,0:T(1,128)S(1)}, u32[]{:S(2)}, u32[]{:S(2)}) %collective-permute-start.15) | collective-permute-done | bytes 16928 | tf_op jit(solution)/shard_map/ppermute | solution.py:626
  60.4 1.7 %collective-permute-done.14 = f32[1,4224]{1,0:T(1,128)S(1)} collective-permute-done((f32[1,4224]{1,0:T(1,128)S(1)}, f32[1,4224]{1,0:T(1,128)S(1)}, u32[]{:S(2)}, u32[]{:S(2)}) %collective-permute-start.14) | collective-permute-done | bytes 16928 | tf_op jit(solution)/shard_map/ppermute | solution.py:626
  62.2 0.8 %collective-permute-done.13 = f32[1,4224]{1,0:T(1,128)S(1)} collective-permute-done((f32[1,4224]{1,0:T(1,128)S(1)}, f32[1,4224]{1,0:T(1,128)S(1)}, u32[]{:S(2)}, u32[]{:S(2)}) %collective-permute-start.13) | collective-permute-done | bytes 16928 | tf_op jit(solution)/shard_map/ppermute | solution.py:626
  63.0 0.5 slice.9
  63.5 0.6 slice.8
  (27 shorter events, 0.3 us)
Async XLA Ops:
  0.6 15.7 %copy-start = (f32[4096,128]{1,0:T(8,128)S(1)}, f32[4096,128]{1,0:T(8,128)}, u32[]{:S(2)}) copy-start(f32[4096,128]{1,0:T(8,128)} %refs_17_.1) | copy-start | bytes 6291460
  0.6 1.1 %copy-start.1 = (f32[4,4,32,128]{3,2,1,0:T(8,128)S(1)}, f32[4,4,32,128]{3,2,1,0:T(8,128)}, u32[]{:S(2)}) copy-start(f32[4,4,32,128]{3,2,1,0:T(8,128)} %initial.1) | copy-start | bytes 786436
  1.7 0.9 %copy-start.2 = (f32[4,4,32,128]{3,2,1,0:T(8,128)S(1)}, f32[4,4,32,128]{3,2,1,0:T(8,128)}, u32[]{:S(2)}) copy-start(f32[4,4,32,128]{3,2,1,0:T(8,128)} %retard.1) | copy-start | bytes 786436
  2.7 0.9 %copy-start.3 = (f32[4,4,32,128]{3,2,1,0:T(8,128)S(1)}, f32[4,4,32,128]{3,2,1,0:T(8,128)}, u32[]{:S(2)}) copy-start(f32[4,4,32,128]{3,2,1,0:T(8,128)} %velx.1) | copy-start | bytes 786436
  3.6 0.9 %copy-start.4 = (f32[4,4,32,128]{3,2,1,0:T(8,128)S(1)}, f32[4,4,32,128]{3,2,1,0:T(8,128)}, u32[]{:S(2)}) copy-start(f32[4,4,32,128]{3,2,1,0:T(8,128)} %vely.1) | copy-start | bytes 786436
  4.6 0.8 %copy-start.5 = (f32[4,32,128]{2,1,0:T(8,128)S(1)}, f32[4,32,128]{2,1,0:T(8,128)}, u32[]{:S(2)}) copy-start(f32[4,32,128]{2,1,0:T(8,128)} %monitor.1) | copy-start | bytes 196612
  5.4 0.7 %copy-start.6 = (f32[4096]{0:T(1024)S(1)}, f32[4096]{0:T(1024)}, u32[]{:S(2)}) copy-start(f32[4096]{0:T(1024)} %param.14) | copy-start | bytes 49156
  6.2 0.7 %copy-start.7 = (s32[4096]{0:T(1024)S(1)}, s32[4096]{0:T(1024)}, u32[]{:S(2)}) copy-start(s32[4096]{0:T(1024)} %param.16) | copy-start | bytes 49156
  7.4 17.5 %collective-permute-start = (f32[4,4,4,16,128]{4,3,2,1,0:T(8,128)S(1)}, f32[4,4,4,16,128]{4,3,2,1,0:T(8,128)S(1)}, u32[]{:S(2)}, u32[]{:S(2)}) collective-permute-start(f32[4,4,4,16,128]{4,3,2,1,0:T(8,128)S(1)} %get-tuple-element.36), channel_id=1, source_target_pairs={{4,0},{5,1},{6,2},{7,3},{0,4},{1,5},{2,6},{3,7},{12,8},{13,9},{14,... | collective-permute-start | bytes 1572872 | tf_op jit(solution)/shard_map/ppermute | solution.py:609
  10.4 14.4 %collective-permute-start.1 = (f32[4,4,4,16,128]{4,3,2,1,0:T(8,128)S(1)}, f32[4,4,4,16,128]{4,3,2,1,0:T(8,128)S(1)}, u32[]{:S(2)}, u32[]{:S(2)}) collective-permute-start(f32[4,4,4,16,128]{4,3,2,1,0:T(8,128)S(1)} %get-tuple-element.37), channel_id=1, source_target_pairs={{1,0},{0,1},{3,2},{2,3},{8,4},{9,5},{10,6},{11,7},{4,8},{5,9},{6,1... | collective-permute-start | bytes 1572872 | tf_op jit(solution)/shard_map/ppermute | solution.py:609
  10.4 14.4 %copy-start.8 = (s32[4]{0:T(128)S(1)}, s32[4]{0:T(128)}, u32[]{:S(2)}) copy-start(s32[4]{0:T(128)} %refs_1_.1) | copy-start | bytes 52
  11.6 13.2 %collective-permute-start.2 = (f32[16,2,8,128]{3,2,1,0:T(8,128)S(1)}, f32[16,2,8,128]{3,2,1,0:T(8,128)S(1)}, u32[]{:S(2)}, u32[]{:S(2)}) collective-permute-start(f32[16,2,8,128]{3,2,1,0:T(8,128)S(1)} %get-tuple-element.39), channel_id=1, source_target_pairs={{2,0},{3,1},{0,2},{1,3},{6,4},{7,5},{4,6},{5,7},{10,8},{11,9},{8,1... | collective-permute-start | bytes 393224 | tf_op jit(solution)/shard_map/ppermute | solution.py:615
  13.2 11.7 %collective-permute-start.3 = (f32[8,2,8,128]{3,2,1,0:T(8,128)S(1)}, f32[8,2,8,128]{3,2,1,0:T(8,128)S(1)}, u32[]{:S(2)}, u32[]{:S(2)}) collective-permute-start(f32[8,2,8,128]{3,2,1,0:T(8,128)S(1)} %get-tuple-element.40), channel_id=1, source_target_pairs={{6,0},{7,1},{4,2},{5,3},{2,4},{3,5},{0,6},{1,7},{14,8},{15,9},{12,... | collective-permute-start | bytes 196616 | tf_op jit(solution)/shard_map/ppermute | solution.py:615
  16.3 8.6 %collective-permute-start.4 = (f32[8,2,8,128]{3,2,1,0:T(8,128)S(1)}, f32[8,2,8,128]{3,2,1,0:T(8,128)S(1)}, u32[]{:S(2)}, u32[]{:S(2)}) collective-permute-start(f32[8,2,8,128]{3,2,1,0:T(8,128)S(1)} %get-tuple-element.41), channel_id=1, source_target_pairs={{1,0},{0,1},{3,2},{2,3},{10,4},{11,5},{8,6},{9,7},{6,8},{7,9},{4,1... | collective-permute-start | bytes 196616 | tf_op jit(solution)/shard_map/ppermute | solution.py:615
  33.9 7.9 %collective-permute-start.5 = (f32[16,2,8,128]{3,2,1,0:T(8,128)S(1)}, f32[16,2,8,128]{3,2,1,0:T(8,128)S(1)}, u32[]{:S(2)}, u32[]{:S(2)}) collective-permute-start(f32[16,2,8,128]{3,2,1,0:T(8,128)S(1)} %get-tuple-element.53.refs_0_), channel_id=1, source_target_pairs={{4,0},{5,1},{6,2},{7,3},{0,4},{1,5},{2,6},{3,7},{12,8},{13,9},{14,... | collective-permute-start | bytes 393224 | tf_op jit(solution)/shard_map/ppermute | solution.py:609
  36.6 5.2 %collective-permute-start.6 = (f32[16,2,8,128]{3,2,1,0:T(8,128)S(1)}, f32[16,2,8,128]{3,2,1,0:T(8,128)S(1)}, u32[]{:S(2)}, u32[]{:S(2)}) collective-permute-start(f32[16,2,8,128]{3,2,1,0:T(8,128)S(1)} %get-tuple-element.54.refs_1_), channel_id=1, source_target_pairs={{1,0},{0,1},{3,2},{2,3},{8,4},{9,5},{10,6},{11,7},{4,8},{5,9},{6,1... | collective-permute-start | bytes 393224 | tf_op jit(solution)/shard_map/ppermute | solution.py:609
  36.6 5.2 %collective-permute-start.7 = (f32[8,8,128]{2,1,0:T(8,128)S(1)}, f32[8,8,128]{2,1,0:T(8,128)S(1)}, u32[]{:S(2)}, u32[]{:S(2)}) collective-permute-start(f32[8,8,128]{2,1,0:T(8,128)S(1)} %get-tuple-element.55), channel_id=1, source_target_pairs={{2,0},{3,1},{0,2},{1,3},{6,4},{7,5},{4,6},{5,7},{10,8},{11,9},{8,1... | collective-permute-start | bytes 98312 | tf_op jit(solution)/shard_map/ppermute | solution.py:615
  37.1 4.7 %collective-permute-start.8 = (f32[4,8,128]{2,1,0:T(8,128)S(1)}, f32[4,8,128]{2,1,0:T(8,128)S(1)}, u32[]{:S(2)}, u32[]{:S(2)}) collective-permute-start(f32[4,8,128]{2,1,0:T(8,128)S(1)} %get-tuple-element.56), channel_id=1, source_target_pairs={{6,0},{7,1},{4,2},{5,3},{2,4},{3,5},{0,6},{1,7},{14,8},{15,9},{12,... | collective-permute-start | bytes 49160 | tf_op jit(solution)/shard_map/ppermute | solution.py:615
  40.1 1.7 %collective-permute-start.9 = (f32[4,8,128]{2,1,0:T(8,128)S(1)}, f32[4,8,128]{2,1,0:T(8,128)S(1)}, u32[]{:S(2)}, u32[]{:S(2)}) collective-permute-start(f32[4,8,128]{2,1,0:T(8,128)S(1)} %get-tuple-element.57), channel_id=1, source_target_pairs={{1,0},{0,1},{3,2},{2,3},{10,4},{11,5},{8,6},{9,7},{6,8},{7,9},{4,1... | collective-permute-start | bytes 49160 | tf_op jit(solution)/shard_map/ppermute | solution.py:615
  50.9 3.3 %collective-permute-start.12 = (f32[1,4224]{1,0:T(1,128)S(1)}, f32[1,4224]{1,0:T(1,128)S(1)}, u32[]{:S(2)}, u32[]{:S(2)}) collective-permute-start(f32[1,4224]{1,0:T(1,128)S(1)} %adjoint.1), channel_id=1, source_target_pairs={{0,3},{1,2},{2,1},{3,0},{4,7},{5,6},{6,5},{7,4},{8,11},{9,10},{10,... | collective-permute-start | bytes 50696 | tf_op jit(solution)/shard_map/ppermute | solution.py:626
  51.0 3.7 %collective-permute-start.11 = (f32[1,4224]{1,0:T(1,128)S(1)}, f32[1,4224]{1,0:T(1,128)S(1)}, u32[]{:S(2)}, u32[]{:S(2)}) collective-permute-start(f32[1,4224]{1,0:T(1,128)S(1)} %adjoint.1), channel_id=1, source_target_pairs={{0,2},{1,3},{2,0},{3,1},{4,6},{5,7},{6,4},{7,5},{8,10},{9,11},{10,... | collective-permute-start | bytes 50696 | tf_op jit(solution)/shard_map/ppermute | solution.py:626
  52.4 2.4 %collective-permute-start.10 = (f32[1,4224]{1,0:T(1,128)S(1)}, f32[1,4224]{1,0:T(1,128)S(1)}, u32[]{:S(2)}, u32[]{:S(2)}) collective-permute-start(f32[1,4224]{1,0:T(1,128)S(1)} %adjoint.1), channel_id=1, source_target_pairs={{0,1},{1,0},{2,3},{3,2},{4,5},{5,4},{6,7},{7,6},{8,9},{9,8},{10,11... | collective-permute-start | bytes 50696 | tf_op jit(solution)/shard_map/ppermute | solution.py:626
  54.8 5.6 %collective-permute-start.15 = (f32[1,4224]{1,0:T(1,128)S(1)}, f32[1,4224]{1,0:T(1,128)S(1)}, u32[]{:S(2)}, u32[]{:S(2)}) collective-permute-start(f32[1,4224]{1,0:T(1,128)S(1)} %add_add_fusion.1), channel_id=1, source_target_pairs={{0,12},{1,13},{2,14},{3,15},{4,8},{5,9},{6,10},{7,11},{8,4},{9,5},... | collective-permute-start | bytes 50696 | tf_op jit(solution)/shard_map/ppermute | solution.py:626
  57.5 4.6 %collective-permute-start.14 = (f32[1,4224]{1,0:T(1,128)S(1)}, f32[1,4224]{1,0:T(1,128)S(1)}, u32[]{:S(2)}, u32[]{:S(2)}) collective-permute-start(f32[1,4224]{1,0:T(1,128)S(1)} %add_add_fusion.1), channel_id=1, source_target_pairs={{0,8},{1,9},{2,10},{3,11},{4,12},{5,13},{6,14},{7,15},{8,0},{9,1},... | collective-permute-start | bytes 50696 | tf_op jit(solution)/shard_map/ppermute | solution.py:626
  59.2 3.7 %collective-permute-start.13 = (f32[1,4224]{1,0:T(1,128)S(1)}, f32[1,4224]{1,0:T(1,128)S(1)}, u32[]{:S(2)}, u32[]{:S(2)}) collective-permute-start(f32[1,4224]{1,0:T(1,128)S(1)} %add_add_fusion.1), channel_id=1, source_target_pairs={{0,4},{1,5},{2,6},{3,7},{4,0},{5,1},{6,2},{7,3},{8,12},{9,13},{10,... | collective-permute-start | bytes 50696 | tf_op jit(solution)/shard_map/ppermute | solution.py:626

commit v3 on v2

--- a/solution.py
+++ b/solution.py
@@ -20,7 +20,6 @@
 INNER = EXT // GROUPS
 JOIN = ITERS // 2
 CHUNK = 512
-PHASES = ((0, 4), (4, 8), (8, 12), (12, ITERS - 1))
 VMEM_LIMIT = 24 * 1024 * 1024
 
 
@@ -358,16 +357,10 @@
 
 
 def sweep(step, join):
-    for begin, end in PHASES:
-
-        def body(_, carry, begin=begin):
-            step(begin + 1, EXT - 2 - begin, True)
-            return carry
-
-        if begin == JOIN:
-            join(begin, EXT - 1 - begin)
-        lax.fori_loop(begin, end, body, 0)
-    step(ITERS, EXT - 1 - ITERS, False)
+    for t in range(ITERS):
+        if t == JOIN:
+            join(t, EXT - 1 - t)
+        step(t + 1, EXT - 2 - t, t < ITERS - 1)
 
 
 def split_refs(refs, *counts):
@@ -643,6 +636,8 @@
     half_tile = shape(4, samples, layers, DEPTH, LANES)
     hbm = pl.BlockSpec(memory_space=pltpu.HBM)
     any_space = pl.BlockSpec(memory_space=pl.ANY)
+    inputs = (initial, retard, velx, vely, monitor, controls.reshape(1, -1), wells.reshape(1, -1))
+    inputs = [pltpu.with_memory_space_constraint(value, pltpu.HBM) for value in inputs]
     own, *sent, monitor, controls, wells = pl.pallas_call(
         stage_kernel,
         out_shape=(
@@ -658,7 +653,7 @@
         scratch_shapes=[pltpu.SemaphoreType.DMA((15,))],
         compiler_params=params(),
         name="stage",
-    )(initial, retard, velx, vely, monitor, controls.reshape(1, -1), wells.reshape(1, -1))
+    )(*inputs)
     own = own.reshape(4, -1, LANES)
     sent_strips = pl.pallas_call(
         functools.partial(strip_pack_kernel, kinds),

time: 64.5 us -> 57 us (0.88)
  local copies, waits for them, and re-layouts: 7.34 us -> 1.13 us
  Pallas kernels: 25.4 us -> 24.5 us
    unnamed x18 -> x4, local copies, waits for them, and re-layouts: 6.22 us -> 0.01 us
    pallas_call x1, Pallas kernels: 0.48 us -> 1.89 us  [local(): pl.pallas_call(stage_kernel, out_shape=(shape(4, samples, layers, OWN, LA...]
    pallas_call x1, Pallas kernels: 8.96 us -> 7.65 us  [local(): pl.pallas_call(functools.partial(forward_kernel, kinds, tail_count), out_...]
    pallas_call x1, Pallas kernels: 9.09 us -> 8 us  [local(): pl.pallas_call(functools.partial(adjoint_kernel, kinds, 0.5 / (tail_count...]
  transfers between devices with their start and end apart: 16 -> 16, of which waited for: 7 -> 7; matrix products, arithmetic and copies ran while one was open for 0% -> 0% of each run, Pallas kernels for 11% -> 12%
where the time goes in v3:
time: 57 us; the launch traced here: 56.9 us
  Pallas kernels  24.5 us (43%)
  starting transfers between devices  20.5 us (36%)
  waiting for transfers between devices  9.92 us (17%)
  local copies, waits for them, and re-layouts  1.13 us (2%)
  between operations  0.71 us (1%)
    ppermute x6, starting transfers between devices, exchange(): lax.ppermute(strip, AXES, swap_pairs(partner, kind, *counts))  8.17 us
    pallas_call x1, Pallas kernels, local(): pl.pallas_call(functools.partial(adjoint_kernel, kinds, 0.5 / (tail_count...  8 us
    pallas_call x1, Pallas kernels, local(): pl.pallas_call(functools.partial(forward_kernel, kinds, tail_count), out_...  7.65 us
    ppermute x6, starting transfers between devices, total_over(): lax.ppermute(value, axes, [(i, i ^ b) for i in range(count)])  6.52 us
    pallas_call x1, Pallas kernels, local(): pl.pallas_call(functools.partial(source_kernel, kinds), out_shape=(tile_s...  5.84 us
    ppermute x4, starting transfers between devices, exchange(): lax.ppermute(tile, AXES, swap_pairs(partner, 'tile', *counts))  5.79 us
    ppermute x6, waiting for transfers between devices, total_over(): lax.ppermute(value, axes, [(i, i ^ b) for i in range(count)])  5.48 us
    ppermute x6, waiting for transfers between devices, exchange(): lax.ppermute(strip, AXES, swap_pairs(partner, kind, *counts))  4.43 us
  transfers between devices with their start and end apart: 16, of which 7 were waited for; matrix products, arithmetic and copies ran while one was open for 0% of the time, Pallas kernels for 12%

profile of v3, /device:TPU:0, one launch (start us, length us, event | category | flops | bytes accessed | tf_op | source)
XLA Modules:
  0.0 56.9 jit_solution(5919812511737124498)
XLA Ops:
  0.6 1.9 %stage.1 = (f32[4,4,4,32,128]{4,3,2,1,0:T(8,128)S(1)}, f32[4,4,4,16,128]{4,3,2,1,0:T(8,128)S(1)}, f32[4,4,4,16,128]{4,3,2,1,0:T(8,128)S(1)}, f32[4,32,128]{2,1,0...) custom-call(f32[4,4,32,128]{3,2,1,0:T(8,128)} %initial.1, f32[4,4,32,128]{3,2,1,0:T(8,128)} %retard.1, ...), custom_call_target="tpu_custom_call" | custom-call | tf_op jit(solution)/shard_map/stage/pallas_call | solution.py:641
  2.5 3.1 %collective-permute-start = (f32[4,4,4,16,128]{4,3,2,1,0:T(8,128)S(1)}, f32[4,4,4,16,128]{4,3,2,1,0:T(8,128)S(1)}, u32[]{:S(2)}, u32[]{:S(2)}) collective-permute-start(f32[4,4,4,16,128]{4,3,2,1,0:T(8,128)S(1)} %get-tuple-element.36), channel_id=1, source_target_pairs={{4,0},{5,1},{6,2},{7,3},{0,4},{1,5},{2,6},{3,7},{12,8},{13,9},{14,... | collective-permute-start | bytes 1572872 | tf_op jit(solution)/shard_map/ppermute | solution.py:602
  5.6 0.0 collective-permute-start.1
  5.6 1.2 %strips.1 = (f32[16,2,8,128]{3,2,1,0:T(8,128)S(1)}, f32[8,2,8,128]{3,2,1,0:T(8,128)S(1)}, f32[8,2,8,128]{3,2,1,0:T(8,128)S(1)}) custom-call(f32[4,512,128]{2,1,0:T(8,128)S(1)} %bitcast.9), custom_call_target="tpu_custom_call" | custom-call | tf_op jit(solution)/shard_map/strips/pallas_call | solution.py:658
  6.8 1.6 %collective-permute-start.2 = (f32[16,2,8,128]{3,2,1,0:T(8,128)S(1)}, f32[16,2,8,128]{3,2,1,0:T(8,128)S(1)}, u32[]{:S(2)}, u32[]{:S(2)}) collective-permute-start(f32[16,2,8,128]{3,2,1,0:T(8,128)S(1)} %get-tuple-element.39), channel_id=1, source_target_pairs={{2,0},{3,1},{0,2},{1,3},{6,4},{7,5},{4,6},{5,7},{10,8},{11,9},{8,1... | collective-permute-start | bytes 393224 | tf_op jit(solution)/shard_map/ppermute | solution.py:608
  8.4 3.1 %collective-permute-start.3 = (f32[8,2,8,128]{3,2,1,0:T(8,128)S(1)}, f32[8,2,8,128]{3,2,1,0:T(8,128)S(1)}, u32[]{:S(2)}, u32[]{:S(2)}) collective-permute-start(f32[8,2,8,128]{3,2,1,0:T(8,128)S(1)} %get-tuple-element.40), channel_id=1, source_target_pairs={{6,0},{7,1},{4,2},{5,3},{2,4},{3,5},{0,6},{1,7},{14,8},{15,9},{12,... | collective-permute-start | bytes 196616 | tf_op jit(solution)/shard_map/ppermute | solution.py:608
  11.5 0.0 collective-permute-start.4
  11.5 5.8 %source.1 = (f32[64,2,8,128]{3,2,1,0:T(8,128)S(1)}, f32[16,2,8,128]{3,2,1,0:T(8,128)S(1)}, f32[64,2,8,128]{3,2,1,0:T(8,128)S(1)}, f32[64,2,8,128]{3,2,1,0:T(8,12...) custom-call(s32[1,4096]{1,0:T(1,128)S(1)} %get-tuple-element.42.well, ...), custom_call_target="tpu_custom_call" | custom-call | tf_op jit(solution)/shard_map/source/pallas_call | solution.py:675
  17.3 2.7 %collective-permute-done.3.refs_5_ = f32[8,2,8,128]{3,2,1,0:T(8,128)S(1)} collective-permute-done((f32[8,2,8,128]{3,2,1,0:T(8,128)S(1)}, f32[8,2,8,128]{3,2,1,0:T(8,128)S(1)}, u32[]{:S(2)}, u32[]{:S(2)}) %collective-permute-start.3) | collective-permute-done | bytes 65568 | tf_op jit(solution)/shard_map/ppermute | solution.py:608
  20.1 0.0 collective-permute-done.1
  20.1 7.6 %forward.1 = (f32[512,128]{1,0:T(8,128)}, f32[16,2,8,128]{3,2,1,0:T(8,128)S(1)}, f32[16,2,8,128]{3,2,1,0:T(8,128)S(1)}, f32[8,128]{1,0:T(8,128)S(1)}, f32[64,2,8...) custom-call(f32[128,128]{1,0:T(8,128)S(1)} %bitcast.13, ...), custom_call_target="tpu_custom_call", output_to_operand_aliasing={{4}: (9, {}), {5}: (10, {}), {6}: (11, {}), {7}: (12, {}), ... | custom-call | tf_op jit(solution)/shard_map/forward/pallas_call | solution.py:695
  27.7 2.7 %collective-permute-start.5 = (f32[16,2,8,128]{3,2,1,0:T(8,128)S(1)}, f32[16,2,8,128]{3,2,1,0:T(8,128)S(1)}, u32[]{:S(2)}, u32[]{:S(2)}) collective-permute-start(f32[16,2,8,128]{3,2,1,0:T(8,128)S(1)} %get-tuple-element.53.refs_0_), channel_id=1, source_target_pairs={{4,0},{5,1},{6,2},{7,3},{0,4},{1,5},{2,6},{3,7},{12,8},{13,9},{14,... | collective-permute-start | bytes 393224 | tf_op jit(solution)/shard_map/ppermute | solution.py:602
  30.4 0.5 collective-permute-start.7
  31.0 3.0 %collective-permute-start.8 = (f32[4,8,128]{2,1,0:T(8,128)S(1)}, f32[4,8,128]{2,1,0:T(8,128)S(1)}, u32[]{:S(2)}, u32[]{:S(2)}) collective-permute-start(f32[4,8,128]{2,1,0:T(8,128)S(1)} %get-tuple-element.56), channel_id=1, source_target_pairs={{6,0},{7,1},{4,2},{5,3},{2,4},{3,5},{0,6},{1,7},{14,8},{15,9},{12,... | collective-permute-start | bytes 49160 | tf_op jit(solution)/shard_map/ppermute | solution.py:608
  33.9 1.7 %collective-permute-done.8.refs_5_ = f32[4,8,128]{2,1,0:T(8,128)S(1)} collective-permute-done((f32[4,8,128]{2,1,0:T(8,128)S(1)}, f32[4,8,128]{2,1,0:T(8,128)S(1)}, u32[]{:S(2)}, u32[]{:S(2)}) %collective-permute-start.8) | collective-permute-done | bytes 16416 | tf_op jit(solution)/shard_map/ppermute | solution.py:608
  35.6 0.0 collective-permute-done.9.refs_6_
  35.6 0.0 collective-permute-done.7.refs_4_
  35.6 0.0 collective-permute-done.5.refs_2_
  35.7 8.0 %adjoint.1 = f32[1,4224]{1,0:T(1,128)S(1)} custom-call(f32[16,2,8,128]{3,2,1,0:T(8,128)S(1)} %get-tuple-element.53.refs_0_, f32[16,2,8,128]{3,2,1,0:T(8,128)S(1)} %get-tuple-element.54.refs_1_, f32[16,2,8,128]{3,2,1,0:T(8,128)S(1)} %collective-permute-done.5.refs_2_, f32[16,2,8,128]{3,2,1,0:T(8,128)S(1)} %collective-permute-done.6.refs_3_, ...), custom_call_target="tpu_custom_call" | custom-call | tf_op jit(solution)/shard_map/adjoint/pallas_call | solution.py:723
  43.7 0.1 collective-permute-start.12
  43.8 1.4 %collective-permute-start.11 = (f32[1,4224]{1,0:T(1,128)S(1)}, f32[1,4224]{1,0:T(1,128)S(1)}, u32[]{:S(2)}, u32[]{:S(2)}) collective-permute-start(f32[1,4224]{1,0:T(1,128)S(1)} %adjoint.1), channel_id=1, source_target_pairs={{0,2},{1,3},{2,0},{3,1},{4,6},{5,7},{6,4},{7,5},{8,10},{9,11},{10,... | collective-permute-start | bytes 50696 | tf_op jit(solution)/shard_map/ppermute | solution.py:619
  45.2 0.3 collective-permute-start.10
  45.5 1.5 %collective-permute-done.12 = f32[1,4224]{1,0:T(1,128)S(1)} collective-permute-done((f32[1,4224]{1,0:T(1,128)S(1)}, f32[1,4224]{1,0:T(1,128)S(1)}, u32[]{:S(2)}, u32[]{:S(2)}) %collective-permute-start.12) | collective-permute-done | bytes 16928 | tf_op jit(solution)/shard_map/ppermute | solution.py:619
  47.0 0.5 collective-permute-done.11
  47.6 2.7 %collective-permute-start.15 = (f32[1,4224]{1,0:T(1,128)S(1)}, f32[1,4224]{1,0:T(1,128)S(1)}, u32[]{:S(2)}, u32[]{:S(2)}) collective-permute-start(f32[1,4224]{1,0:T(1,128)S(1)} %add_add_fusion.1), channel_id=1, source_target_pairs={{0,12},{1,13},{2,14},{3,15},{4,8},{5,9},{6,10},{7,11},{8,4},{9,5},... | collective-permute-start | bytes 50696 | tf_op jit(solution)/shard_map/ppermute | solution.py:619
  50.3 1.7 %collective-permute-start.14 = (f32[1,4224]{1,0:T(1,128)S(1)}, f32[1,4224]{1,0:T(1,128)S(1)}, u32[]{:S(2)}, u32[]{:S(2)}) collective-permute-start(f32[1,4224]{1,0:T(1,128)S(1)} %add_add_fusion.1), channel_id=1, source_target_pairs={{0,8},{1,9},{2,10},{3,11},{4,12},{5,13},{6,14},{7,15},{8,0},{9,1},... | collective-permute-start | bytes 50696 | tf_op jit(solution)/shard_map/ppermute | solution.py:619
  52.0 0.3 collective-permute-start.13
  52.2 0.9 %collective-permute-done.15 = f32[1,4224]{1,0:T(1,128)S(1)} collective-permute-done((f32[1,4224]{1,0:T(1,128)S(1)}, f32[1,4224]{1,0:T(1,128)S(1)}, u32[]{:S(2)}, u32[]{:S(2)}) %collective-permute-start.15) | collective-permute-done | bytes 16928 | tf_op jit(solution)/shard_map/ppermute | solution.py:619
  53.2 1.7 %collective-permute-done.14 = f32[1,4224]{1,0:T(1,128)S(1)} collective-permute-done((f32[1,4224]{1,0:T(1,128)S(1)}, f32[1,4224]{1,0:T(1,128)S(1)}, u32[]{:S(2)}, u32[]{:S(2)}) %collective-permute-start.14) | collective-permute-done | bytes 16928 | tf_op jit(solution)/shard_map/ppermute | solution.py:619
  54.9 0.8 %collective-permute-done.13 = f32[1,4224]{1,0:T(1,128)S(1)} collective-permute-done((f32[1,4224]{1,0:T(1,128)S(1)}, f32[1,4224]{1,0:T(1,128)S(1)}, u32[]{:S(2)}, u32[]{:S(2)}) %collective-permute-start.13) | collective-permute-done | bytes 16928 | tf_op jit(solution)/shard_map/ppermute | solution.py:619
  55.7 0.5 slice.9
  56.3 0.6 %slice.8 = f32[1,4096]{1,0:T(1,128)} slice(f32[1,4224]{1,0:T(1,128)S(1)} %add_add_fusion), slice={[0:1], [0:4096]} | slice | bytes 32768 | tf_op jit(solution)/shard_map/slice | solution.py:747
  (13 shorter events, 0.1 us)
Async XLA Ops:
  0.6 10.9 %copy-start = (f32[4096,128]{1,0:T(8,128)S(1)}, f32[4096,128]{1,0:T(8,128)}, u32[]{:S(2)}) copy-start(f32[4096,128]{1,0:T(8,128)} %refs_17_.1) | copy-start | bytes 6291460
  2.5 17.5 %collective-permute-start = (f32[4,4,4,16,128]{4,3,2,1,0:T(8,128)S(1)}, f32[4,4,4,16,128]{4,3,2,1,0:T(8,128)S(1)}, u32[]{:S(2)}, u32[]{:S(2)}) collective-permute-start(f32[4,4,4,16,128]{4,3,2,1,0:T(8,128)S(1)} %get-tuple-element.36), channel_id=1, source_target_pairs={{4,0},{5,1},{6,2},{7,3},{0,4},{1,5},{2,6},{3,7},{12,8},{13,9},{14,... | collective-permute-start | bytes 1572872 | tf_op jit(solution)/shard_map/ppermute | solution.py:602
  5.6 14.4 %collective-permute-start.1 = (f32[4,4,4,16,128]{4,3,2,1,0:T(8,128)S(1)}, f32[4,4,4,16,128]{4,3,2,1,0:T(8,128)S(1)}, u32[]{:S(2)}, u32[]{:S(2)}) collective-permute-start(f32[4,4,4,16,128]{4,3,2,1,0:T(8,128)S(1)} %get-tuple-element.37), channel_id=1, source_target_pairs={{1,0},{0,1},{3,2},{2,3},{8,4},{9,5},{10,6},{11,7},{4,8},{5,9},{6,1... | collective-permute-start | bytes 1572872 | tf_op jit(solution)/shard_map/ppermute | solution.py:602
  5.6 14.4 %copy-start.1 = (s32[4]{0:T(128)S(1)}, s32[4]{0:T(128)}, u32[]{:S(2)}) copy-start(s32[4]{0:T(128)} %refs_1_.1) | copy-start | bytes 52
  6.8 13.2 %collective-permute-start.2 = (f32[16,2,8,128]{3,2,1,0:T(8,128)S(1)}, f32[16,2,8,128]{3,2,1,0:T(8,128)S(1)}, u32[]{:S(2)}, u32[]{:S(2)}) collective-permute-start(f32[16,2,8,128]{3,2,1,0:T(8,128)S(1)} %get-tuple-element.39), channel_id=1, source_target_pairs={{2,0},{3,1},{0,2},{1,3},{6,4},{7,5},{4,6},{5,7},{10,8},{11,9},{8,1... | collective-permute-start | bytes 393224 | tf_op jit(solution)/shard_map/ppermute | solution.py:608
  8.4 11.7 %collective-permute-start.3 = (f32[8,2,8,128]{3,2,1,0:T(8,128)S(1)}, f32[8,2,8,128]{3,2,1,0:T(8,128)S(1)}, u32[]{:S(2)}, u32[]{:S(2)}) collective-permute-start(f32[8,2,8,128]{3,2,1,0:T(8,128)S(1)} %get-tuple-element.40), channel_id=1, source_target_pairs={{6,0},{7,1},{4,2},{5,3},{2,4},{3,5},{0,6},{1,7},{14,8},{15,9},{12,... | collective-permute-start | bytes 196616 | tf_op jit(solution)/shard_map/ppermute | solution.py:608
  11.5 8.6 %collective-permute-start.4 = (f32[8,2,8,128]{3,2,1,0:T(8,128)S(1)}, f32[8,2,8,128]{3,2,1,0:T(8,128)S(1)}, u32[]{:S(2)}, u32[]{:S(2)}) collective-permute-start(f32[8,2,8,128]{3,2,1,0:T(8,128)S(1)} %get-tuple-element.41), channel_id=1, source_target_pairs={{1,0},{0,1},{3,2},{2,3},{10,4},{11,5},{8,6},{9,7},{6,8},{7,9},{4,1... | collective-permute-start | bytes 196616 | tf_op jit(solution)/shard_map/ppermute | solution.py:608
  27.7 7.9 %collective-permute-start.5 = (f32[16,2,8,128]{3,2,1,0:T(8,128)S(1)}, f32[16,2,8,128]{3,2,1,0:T(8,128)S(1)}, u32[]{:S(2)}, u32[]{:S(2)}) collective-permute-start(f32[16,2,8,128]{3,2,1,0:T(8,128)S(1)} %get-tuple-element.53.refs_0_), channel_id=1, source_target_pairs={{4,0},{5,1},{6,2},{7,3},{0,4},{1,5},{2,6},{3,7},{12,8},{13,9},{14,... | collective-permute-start | bytes 393224 | tf_op jit(solution)/shard_map/ppermute | solution.py:602
  30.4 5.2 %collective-permute-start.6 = (f32[16,2,8,128]{3,2,1,0:T(8,128)S(1)}, f32[16,2,8,128]{3,2,1,0:T(8,128)S(1)}, u32[]{:S(2)}, u32[]{:S(2)}) collective-permute-start(f32[16,2,8,128]{3,2,1,0:T(8,128)S(1)} %get-tuple-element.54.refs_1_), channel_id=1, source_target_pairs={{1,0},{0,1},{3,2},{2,3},{8,4},{9,5},{10,6},{11,7},{4,8},{5,9},{6,1... | collective-permute-start | bytes 393224 | tf_op jit(solution)/shard_map/ppermute | solution.py:602
  30.4 5.2 %collective-permute-start.7 = (f32[8,8,128]{2,1,0:T(8,128)S(1)}, f32[8,8,128]{2,1,0:T(8,128)S(1)}, u32[]{:S(2)}, u32[]{:S(2)}) collective-permute-start(f32[8,8,128]{2,1,0:T(8,128)S(1)} %get-tuple-element.55), channel_id=1, source_target_pairs={{2,0},{3,1},{0,2},{1,3},{6,4},{7,5},{4,6},{5,7},{10,8},{11,9},{8,1... | collective-permute-start | bytes 98312 | tf_op jit(solution)/shard_map/ppermute | solution.py:608
  31.0 4.7 %collective-permute-start.8 = (f32[4,8,128]{2,1,0:T(8,128)S(1)}, f32[4,8,128]{2,1,0:T(8,128)S(1)}, u32[]{:S(2)}, u32[]{:S(2)}) collective-permute-start(f32[4,8,128]{2,1,0:T(8,128)S(1)} %get-tuple-element.56), channel_id=1, source_target_pairs={{6,0},{7,1},{4,2},{5,3},{2,4},{3,5},{0,6},{1,7},{14,8},{15,9},{12,... | collective-permute-start | bytes 49160 | tf_op jit(solution)/shard_map/ppermute | solution.py:608
  33.9 1.7 %collective-permute-start.9 = (f32[4,8,128]{2,1,0:T(8,128)S(1)}, f32[4,8,128]{2,1,0:T(8,128)S(1)}, u32[]{:S(2)}, u32[]{:S(2)}) collective-permute-start(f32[4,8,128]{2,1,0:T(8,128)S(1)} %get-tuple-element.57), channel_id=1, source_target_pairs={{1,0},{0,1},{3,2},{2,3},{10,4},{11,5},{8,6},{9,7},{6,8},{7,9},{4,1... | collective-permute-start | bytes 49160 | tf_op jit(solution)/shard_map/ppermute | solution.py:608
  43.7 3.3 %collective-permute-start.12 = (f32[1,4224]{1,0:T(1,128)S(1)}, f32[1,4224]{1,0:T(1,128)S(1)}, u32[]{:S(2)}, u32[]{:S(2)}) collective-permute-start(f32[1,4224]{1,0:T(1,128)S(1)} %adjoint.1), channel_id=1, source_target_pairs={{0,3},{1,2},{2,1},{3,0},{4,7},{5,6},{6,5},{7,4},{8,11},{9,10},{10,... | collective-permute-start | bytes 50696 | tf_op jit(solution)/shard_map/ppermute | solution.py:619
  43.8 3.7 %collective-permute-start.11 = (f32[1,4224]{1,0:T(1,128)S(1)}, f32[1,4224]{1,0:T(1,128)S(1)}, u32[]{:S(2)}, u32[]{:S(2)}) collective-permute-start(f32[1,4224]{1,0:T(1,128)S(1)} %adjoint.1), channel_id=1, source_target_pairs={{0,2},{1,3},{2,0},{3,1},{4,6},{5,7},{6,4},{7,5},{8,10},{9,11},{10,... | collective-permute-start | bytes 50696 | tf_op jit(solution)/shard_map/ppermute | solution.py:619
  45.2 2.4 %collective-permute-start.10 = (f32[1,4224]{1,0:T(1,128)S(1)}, f32[1,4224]{1,0:T(1,128)S(1)}, u32[]{:S(2)}, u32[]{:S(2)}) collective-permute-start(f32[1,4224]{1,0:T(1,128)S(1)} %adjoint.1), channel_id=1, source_target_pairs={{0,1},{1,0},{2,3},{3,2},{4,5},{5,4},{6,7},{7,6},{8,9},{9,8},{10,11... | collective-permute-start | bytes 50696 | tf_op jit(solution)/shard_map/ppermute | solution.py:619
  47.6 5.6 %collective-permute-start.15 = (f32[1,4224]{1,0:T(1,128)S(1)}, f32[1,4224]{1,0:T(1,128)S(1)}, u32[]{:S(2)}, u32[]{:S(2)}) collective-permute-start(f32[1,4224]{1,0:T(1,128)S(1)} %add_add_fusion.1), channel_id=1, source_target_pairs={{0,12},{1,13},{2,14},{3,15},{4,8},{5,9},{6,10},{7,11},{8,4},{9,5},... | collective-permute-start | bytes 50696 | tf_op jit(solution)/shard_map/ppermute | solution.py:619
  50.3 4.6 %collective-permute-start.14 = (f32[1,4224]{1,0:T(1,128)S(1)}, f32[1,4224]{1,0:T(1,128)S(1)}, u32[]{:S(2)}, u32[]{:S(2)}) collective-permute-start(f32[1,4224]{1,0:T(1,128)S(1)} %add_add_fusion.1), channel_id=1, source_target_pairs={{0,8},{1,9},{2,10},{3,11},{4,12},{5,13},{6,14},{7,15},{8,0},{9,1},... | collective-permute-start | bytes 50696 | tf_op jit(solution)/shard_map/ppermute | solution.py:619
  52.0 3.7 %collective-permute-start.13 = (f32[1,4224]{1,0:T(1,128)S(1)}, f32[1,4224]{1,0:T(1,128)S(1)}, u32[]{:S(2)}, u32[]{:S(2)}) collective-permute-start(f32[1,4224]{1,0:T(1,128)S(1)} %add_add_fusion.1), channel_id=1, source_target_pairs={{0,4},{1,5},{2,6},{3,7},{4,0},{5,1},{6,2},{7,3},{8,12},{9,13},{10,... | collective-permute-start | bytes 50696 | tf_op jit(solution)/shard_map/ppermute | solution.py:619

commit v4 on v3

--- a/solution.py
+++ b/solution.py
@@ -76,15 +76,7 @@
     return ref[pl.ds(half * rows + row, SUBLANES, stride=2 * rows), :]
 
 
-def stage_kernel(initial, retard, velx, vely, monitor, controls, wells, *refs):
-    own, out_a, out_b, out_monitor, out_controls, out_wells, sems = refs
-    odd = odd_tile()
-    pairs = [(monitor, out_monitor), (controls, out_controls), (wells, out_wells)]
-    for field, ref in enumerate((initial, retard, velx, vely)):
-        for out, base in ((out_a, DEPTH * (1 - odd)), (out_b, DEPTH * odd)):
-            source = ref.at[:, :, pl.ds(pl.multiple_of(base, DEPTH), DEPTH), :]
-            pairs.append((source, out.at[field]))
-        pairs.append((ref, own.at[field]))
+def copy_all(pairs, sems):
     copies = [pltpu.make_async_copy(*pair, sems.at[k]) for k, pair in enumerate(pairs)]
     for copy in copies:
         copy.start()
@@ -92,11 +84,24 @@
         copy.wait()
 
 
+def rims_kernel(initial, retard, velx, vely, out_a, out_b, sems):
+    odd = odd_tile()
+    pairs = []
+    for field, ref in enumerate((initial, retard, velx, vely)):
+        for out, base in ((out_a, DEPTH * (1 - odd)), (out_b, DEPTH * odd)):
+            source = ref.at[:, :, pl.ds(pl.multiple_of(base, DEPTH), DEPTH), :]
+            pairs.append((source, out.at[field]))
+    copy_all(pairs, sems)
+
+
 def edge_offset(kind):
     return DEPTH * (1 - lax.axis_index("gy")) if kind is None else (0 if kind else DEPTH)
 
 
-def strip_pack_kernel(kinds, own, *outs):
+def strip_pack_kernel(kinds, *refs):
+    ins, (own, *copied), outs, (sems,) = split_refs(refs, 7, 4, 3 * len(kinds), 1)
+    pairs = [(ref, own.at[field]) for field, ref in enumerate(ins[:4])]
+    copy_all(pairs + list(zip(ins[4:], copied)), sems)
     odd = odd_tile()
     slot = lane_id() // DEPTH
     for number, kind in enumerate(kinds):
@@ -143,7 +148,7 @@
 
 def source_kernel(kinds, wells, controls, profile, own, *refs):
     n = len(kinds)
-    sources, tile, edges, (acc, acc_low) = split_refs(refs, 1 + n, 5, 1, 2)
+    sources, tile, edges, (saved, split), (acc, acc_low) = split_refs(refs, 1 + n, 5, 1, 2, 2)
     for x in range(OWN):
         for half in range(2):
             raw = [planes(own.at[field], x, half, OWN) for field in range(4)]
@@ -184,9 +189,9 @@
         hit = ids == wells[:, span]
         hot_high = jnp.where(hit, rate_high, 0.0).astype(jnp.bfloat16)
         hot_low = jnp.where(hit, rate - rate_high, 0.0).astype(jnp.bfloat16)
-        acc[...] += jnp.dot(
-            hot_high, jnp.concatenate([high, low], axis=1), preferred_element_type=jnp.float32
-        )
+        split_part = jnp.concatenate([high, low], axis=1)
+        split[span, :] = split_part
+        acc[...] += jnp.dot(hot_high, split_part, preferred_element_type=jnp.float32)
         acc_low[...] += jnp.dot(hot_low, high, preferred_element_type=jnp.float32)
         return carry
 
@@ -215,6 +220,10 @@
                     moved = lane_roll(mixed, WIDE * j + DEPTH)
                     packed = moved if packed is None else jnp.where(group == j, moved, packed)
                 sources[1 + number][i, half] = packed
+    for x in range(OWN):
+        for half in range(2):
+            tile[0][DEPTH + x, half] += sources[0][DEPTH + x, half]
+    ahead(functools.partial(forward_step, masks, (*tile, sources[0]), sourced=True), tile[0], saved)
 
 
 class Masks:
@@ -266,12 +275,12 @@
     return jnp.where(masks.rim[number], rim, own)
 
 
-def forward_step(masks, tile, strips, first, last, sourced):
+def forward_step(masks, tile, first, last, lower=None, upper=None, sourced=True):
     state, keep, from_x, from_y, spread, source = tile
-    before = [state[first - 1, h] for h in range(2)]
+    before = lower or [state[first - 1, h] for h in range(2)]
     here = [state[first, h] for h in range(2)]
     for e in range(first, last + 1):
-        after = [state[e + 1, h] for h in range(2)]
+        after = upper if upper and e == last else [state[e + 1, h] for h in range(2)]
         upright = masks.vertical(here)
         for h in range(2):
             y_high = jnp.where(masks.last, 0.0, lane_roll(here[h], LANES - 1))
@@ -283,6 +292,9 @@
             )
             state[e, h] = value + source[e, h] if sourced else value
         before, here = here, after
+
+
+def forward_strips(masks, strips, sourced):
     for strip, keep, from_x, from_y, spread, source in strips:
         old = [strip[0, h] for h in range(2)]
         here = old
@@ -304,22 +316,22 @@
             before, here = here, after
 
 
-def adjoint_step(masks, tile, strips, first, last):
+def scaled(refs, e, value=None):
+    state, _, from_x, from_y, spread, _ = refs
+    value = value or [state[e, h] for h in range(2)]
+    return (
+        value,
+        [from_x[e, h] * value[h] for h in range(2)],
+        [from_y[e, h] * value[h] for h in range(2)],
+        [spread[e, h] * value[h] for h in range(2)],
+    )
+
+
+def adjoint_step(masks, tile, first, last, lower=None, upper=None):
     state, keep, from_x, from_y, spread, total = tile
-
-    def row(refs, e):
-        state, _, from_x, from_y, spread, _ = refs
-        value = [state[e, h] for h in range(2)]
-        return (
-            value,
-            [from_x[e, h] * value[h] for h in range(2)],
-            [from_y[e, h] * value[h] for h in range(2)],
-            [spread[e, h] * value[h] for h in range(2)],
-        )
-
-    before, here = row(tile, first - 1), row(tile, first)
+    before, here = scaled(tile, first - 1, lower), scaled(tile, first)
     for e in range(first, last + 1):
-        after = row(tile, e + 1)
+        after = scaled(tile, e + 1, upper if e == last else None)
         value, _, by_y, by_spread = here
         upright = masks.vertical(by_spread)
         for h in range(2):
@@ -334,14 +346,17 @@
             if DEPTH <= e < DEPTH + OWN:
                 total[e - DEPTH, h] += fresh
         before, here = here, after
+
+
+def adjoint_strips(masks, strips):
     for refs in strips:
         strip, keep, from_x, from_y, spread, total = refs
-        here = row(refs, 0)
+        here = scaled(refs, 0)
         wrapped = [lane_roll(value, LANES - WIDE) for value in here[1]]
-        last_row = row(refs, INNER - 1)
+        last_row = scaled(refs, INNER - 1)
         before = (None, None, None, [lane_roll(value, WIDE) for value in last_row[3]])
         for i in range(INNER):
-            after = row(refs, i + 1) if i < INNER - 1 else (None, wrapped, None, None)
+            after = scaled(refs, i + 1) if i < INNER - 1 else (None, wrapped, None, None)
             value, _, by_y, by_spread = here
             upright = masks.vertical(by_spread)
             for h in range(2):
@@ -356,11 +371,26 @@
             before, here = here, after
 
 
-def sweep(step, join):
+def ahead(step, state, saved):
+    for t in range(JOIN):
+        low, high = DEPTH + 1 + t, DEPTH + OWN - 2 - t
+        for h in range(2):
+            saved[t, h] = state[low, h]
+            saved[t, 2 + h] = state[high, h]
+        step(low, high)
+
+
+def sweep(step, strip_step, join, saved):
     for t in range(ITERS):
+        sourced = t < ITERS - 1
         if t == JOIN:
             join(t, EXT - 1 - t)
-        step(t + 1, EXT - 2 - t, t < ITERS - 1)
+        if t < JOIN:
+            step(t + 1, DEPTH + t, sourced, upper=[saved[t, h] for h in range(2)])
+            step(DEPTH + OWN - 1 - t, EXT - 2 - t, sourced, lower=[saved[t, 2 + h] for h in range(2)])
+        else:
+            step(t + 1, EXT - 2 - t, sourced)
+        strip_step(sourced)
 
 
 def split_refs(refs, *counts):
@@ -373,11 +403,11 @@
 
 def forward_kernel(kinds, tail_count, *refs):
     n = len(kinds)
-    ins, got_strips, sources, tile, edges, outs, strips, out_strips, (start,) = split_refs(
-        refs, 4, 3 * n, 1 + n, 5, 1, 4 + 5, 5 * n, 3 * n, 1
+    ins, got_strips, sources, tile, (edges, saved), outs, strips, out_strips = split_refs(
+        refs, 4, 3 * n, 1 + n, 5, 2, 5 + 5, 5 * n, 3 * n
     )
     monitor, ranking, got_a, got_b = ins
-    final, start_a, start_b, objective, *tile = outs
+    final, start_a, start_b, objective, start, *tile = outs
     odd = odd_tile()
     masks = Masks(kinds)
     state = tile[0]
@@ -405,7 +435,7 @@
                             masks,
                             k,
                             odd,
-                            edges[0][field, i, h],
+                            edges[field, i, h],
                             lane_roll(raw_a[field], 2 * at_a + DEPTH),
                             lane_roll(raw_b[field], 2 * at_b + DEPTH),
                             lane_roll(
@@ -420,16 +450,21 @@
                 mine = strips[5 * k : 5 * k + 5]
                 for ref, value in zip(mine, (raw[0] + sources[1 + k][i, h], *coefficients(*raw[1:]))):
                     ref[i, h] = value
-    for e in range(EXT):
+    for e in (*range(DEPTH), *range(DEPTH + OWN, EXT)):
         for h in range(2):
             state[e, h] += sources[0][e, h]
     strip_refs = [(*strips[5 * k : 5 * k + 5], sources[1 + k]) for k in range(n)]
     strip_states = [strip[0] for strip in strip_refs]
 
-    def step(first, last, sourced):
-        forward_step(masks, (*tile, sources[0]), strip_refs, first, last, sourced)
-
-    sweep(step, functools.partial(masks.join, state, strip_states))
+    def step(first, last, sourced, **beside):
+        forward_step(masks, (*tile, sources[0]), first, last, sourced=sourced, **beside)
+
+    sweep(
+        step,
+        functools.partial(forward_strips, masks, strip_refs),
+        functools.partial(masks.join, state, strip_states),
+        saved,
+    )
 
     sample = sub_id() // 2
     upper = sub_id() % 2 == 1
@@ -444,11 +479,11 @@
             low = jnp.broadcast_to(monitor[pl.ds(h * OWN + x, 1), :], (SUBLANES, LANES))
             high = jnp.broadcast_to(monitor[pl.ds((2 + h) * OWN + x, 1), :], (SUBLANES, LANES))
             weighted = tail * jnp.where(upper, high, low) * fresh
-            start[x, h] = weighted * (1.0 / (tail_count * ITERS))
+            start[DEPTH + x, h] = weighted * (1.0 / (tail_count * ITERS))
             sums[x % 4] = sums[x % 4] + weighted * fresh
     objective[...] = (sums[0] + sums[1]) + (sums[2] + sums[3])
 
-    base_a, base_b = DEPTH * (1 - odd), DEPTH * odd
+    base_a, base_b, _, _ = places(odd)
     for x in range(DEPTH):
         for h in range(2):
             start_a[x, h] = start[base_a + x, h]
@@ -467,7 +502,7 @@
             for upper_half in range(2):
                 for j in range(2):
                     for h in range(2):
-                        row = INNER * j + INNER // 2 * upper_half + i
+                        row = DEPTH + INNER * j + INNER // 2 * upper_half + i
                         packed = put(packed, row, h, 4 * upper_half + 2 * j + h)
             to_y[i] = packed
         for out, base in ((to_a, base_a), (to_b, base_b)):
@@ -479,15 +514,30 @@
                 out[i] = packed
 
 
+def adjoint_ahead_kernel(*refs):
+    coefs, (state, total, saved, edges) = refs[1:5], refs[5:]
+    masks = Masks(())
+    total[...] = jnp.zeros_like(total)
+    first_j = masks.group == 1
+    for i in range(INNER):
+        for h in range(2):
+            moved = [
+                lane_roll(state[DEPTH + INNER * j + i, h], WIDE * (j + 1) + DEPTH) for j in range(2)
+            ]
+            edges[i, h] = jnp.where(first_j, *moved)
+    ahead(functools.partial(adjoint_step, masks, (state, *coefs, total)), state, saved)
+
+
 def adjoint_kernel(kinds, scale, *refs):
     n = len(kinds)
-    parts, part_strips, coefs, strip_coefs, rest, (state, total), strips, (rows,) = split_refs(
-        refs, 4, 3 * n, 4, 4 * n, 4, 2, 2 * n, 1
+    parts, part_strips, (state, total, saved, edges), coefs, strip_coefs, rest, tile, strips, (rows,) = split_refs(
+        refs, 2, 3 * n, 4, 4, 4 * n, 4, 2, 2 * n, 1
     )
     objective, wells, profile, out = rest
+    state, total = tile
     odd = odd_tile()
     masks = Masks(kinds)
-    at = places(odd)
+    at = places(odd)[2:]
     for part, first in zip(parts, at):
         for x in range(DEPTH):
             for h in range(2):
@@ -508,22 +558,25 @@
                     masks,
                     k,
                     odd,
-                    jnp.where(masks.group == 2 - odd, moved[0], moved[1]),
-                    moved[2],
-                    moved[3],
+                    edges[i, h],
+                    moved[0],
+                    moved[1],
                     lane_roll(got_y[i % (INNER // 2)], LANES + WIDE + side - 64 * eighth - DEPTH * h),
-                    lane_roll(got_a[i % (INNER // 4)], 2 * at[2] + side + LANES - slot),
-                    lane_roll(got_b[i % (INNER // 4)], 2 * at[3] + side + LANES - slot),
+                    lane_roll(got_a[i % (INNER // 4)], 2 * at[0] + side + LANES - slot),
+                    lane_roll(got_b[i % (INNER // 4)], 2 * at[1] + side + LANES - slot),
                 )
         strip_refs.append((strip, *strip_coefs[4 * k : 4 * k + 4], strip_total))
         strip_total[...] = jnp.zeros_like(strip_total)
-    total[...] = jnp.zeros_like(total)
-    tile = (state, *coefs, total)
-
-    def step(first, last, _):
-        adjoint_step(masks, tile, strip_refs, first, last)
-
-    sweep(step, functools.partial(masks.join, state, [refs[0] for refs in strip_refs]))
+
+    def step(first, last, _, **beside):
+        adjoint_step(masks, (state, *coefs, total), first, last, **beside)
+
+    sweep(
+        step,
+        lambda _: adjoint_strips(masks, strip_refs),
+        functools.partial(masks.join, state, [refs[0] for refs in strip_refs]),
+        saved,
+    )
     totals = [refs[-1] for refs in strip_refs]
     for x in range(OWN):
         for h in range(2):
@@ -545,9 +598,7 @@
 
     def chunk(c, carry):
         span = pl.ds(pl.multiple_of(c * CHUNK, CHUNK), CHUNK)
-        share = profile[span, :]
-        share_high = share.astype(jnp.bfloat16)
-        share_low = (share - share_high.astype(jnp.float32)).astype(jnp.bfloat16)
+        share_high, share_low = profile[span, :LANES], profile[span, LANES:]
         first = lax.dot_general(both, share_high, contract, preferred_element_type=jnp.float32)
         second = lax.dot_general(high, share_low, contract, preferred_element_type=jnp.float32)
         product = first[:count] + first[count:] + second
@@ -609,6 +660,16 @@
     return got, got_strips
 
 
+def add_kernel(value, *refs):
+    got, (gradient, objective) = refs[:-2], refs[-2:]
+    total = value[...] + got[0][...]
+    if len(got) == 3:
+        total = total + (got[1][...] + got[2][...])
+    number = gradient.shape[1]
+    gradient[...] = total[:, :number]
+    objective[...] = total[:, number : number + 1]
+
+
 def total_over(value, axes):
     count = 1
     for axis in axes:
@@ -617,11 +678,20 @@
     while bit < count:
         bits = [bit] if 2 * bit >= count else [bit, 2 * bit, 3 * bit]
         got = [lax.ppermute(value, axes, [(i, i ^ b) for i in range(count)]) for b in bits]
+        bit *= 4
+        if bit >= count:
+            break
         value = value + got[0]
         if len(got) == 3:
             value = value + (got[1] + got[2])
-        bit *= 4
-    return value
+    return pl.pallas_call(
+        add_kernel,
+        out_shape=(shape(1, value.shape[1] - LANES), shape(1, 1)),
+        in_specs=[vmem()] * (1 + len(got)),
+        out_specs=(vmem(), vmem()),
+        compiler_params=params(),
+        name="total",
+    )(value, *got)
 
 
 def local(initial, retard, velx, vely, monitor, controls, profile, wells, ranking):
@@ -636,50 +706,60 @@
     half_tile = shape(4, samples, layers, DEPTH, LANES)
     hbm = pl.BlockSpec(memory_space=pltpu.HBM)
     any_space = pl.BlockSpec(memory_space=pl.ANY)
-    inputs = (initial, retard, velx, vely, monitor, controls.reshape(1, -1), wells.reshape(1, -1))
-    inputs = [pltpu.with_memory_space_constraint(value, pltpu.HBM) for value in inputs]
-    own, *sent, monitor, controls, wells = pl.pallas_call(
-        stage_kernel,
+    fields = (initial, retard, velx, vely)
+
+    def in_hbm(values):
+        return [pltpu.with_memory_space_constraint(value, pltpu.HBM) for value in values]
+
+    sent = pl.pallas_call(
+        rims_kernel,
+        out_shape=(half_tile, half_tile),
+        in_specs=[hbm] * 4,
+        out_specs=(any_space, any_space),
+        scratch_shapes=[pltpu.SemaphoreType.DMA((8,))],
+        compiler_params=params(),
+        name="rims",
+    )(*in_hbm(fields))
+    own, monitor, controls, wells, *sent_strips = pl.pallas_call(
+        functools.partial(strip_pack_kernel, kinds),
         out_shape=(
-            shape(4, samples, layers, OWN, LANES),
-            half_tile,
-            half_tile,
-            shape(*monitor.shape),
+            shape(4, samples * layers * OWN, LANES),
+            shape(layers * OWN, LANES),
             shape(1, number),
             jax.ShapeDtypeStruct((1, number), jnp.int32),
-        ),
-        in_specs=[hbm] * 7,
-        out_specs=(any_space,) * 6,
-        scratch_shapes=[pltpu.SemaphoreType.DMA((15,))],
-        compiler_params=params(),
-        name="stage",
-    )(*inputs)
-    own = own.reshape(4, -1, LANES)
-    sent_strips = pl.pallas_call(
-        functools.partial(strip_pack_kernel, kinds),
-        out_shape=(
+        )
+        + (
             shape(INNER, 2, SUBLANES, LANES),
             shape(INNER // 2, 2, SUBLANES, LANES),
             shape(INNER // 2, 2, SUBLANES, LANES),
         )
         * n,
-        in_specs=[vmem()],
-        out_specs=(vmem(),) * (3 * n),
+        in_specs=[hbm] * 7,
+        out_specs=(vmem(),) * (4 + 3 * n),
+        scratch_shapes=[pltpu.SemaphoreType.DMA((7,))],
         compiler_params=params(),
         name="strips",
-    )(own)
+    )(
+        *in_hbm(value.reshape(-1, LANES) for value in (*fields, monitor)),
+        *in_hbm(value.reshape(1, -1) for value in (controls, wells)),
+    )
     got, got_strips = exchange(sent, sent_strips, kinds)
     tile_shape = shape(EXT, 2, SUBLANES, LANES)
     strip_shape = shape(INNER, 2, SUBLANES, LANES)
+    saved_shape = shape(JOIN, 4, SUBLANES, LANES)
     blocks = (1 + n) * EXT * layers
-    prepared = pl.pallas_call(
+    *prepared, split = pl.pallas_call(
         functools.partial(source_kernel, kinds),
         out_shape=(tile_shape,)
         + (strip_shape,) * n
         + (tile_shape,) * 5
-        + (shape(4, INNER, 2, SUBLANES, LANES),),
+        + (
+            shape(4, INNER, 2, SUBLANES, LANES),
+            saved_shape,
+            jax.ShapeDtypeStruct((number, 2 * LANES), jnp.bfloat16),
+        ),
         in_specs=[vmem()] * 4,
-        out_specs=(vmem(),) * (1 + n + 5 + 1),
+        out_specs=(vmem(),) * (1 + n + 5 + 3),
         scratch_shapes=[
             pltpu.VMEM((blocks, 2 * LANES), jnp.float32),
             pltpu.VMEM((blocks, LANES), jnp.float32),
@@ -692,13 +772,14 @@
     half_start = shape(DEPTH, 2, SUBLANES, LANES)
     smem = pl.BlockSpec(memory_space=pltpu.SMEM)
     first_tile = 4 + 3 * n + 1 + n
-    final, start_a, start_b, objective, *rest = pl.pallas_call(
+    final, start_a, start_b, objective, start, *rest = pl.pallas_call(
         functools.partial(forward_kernel, kinds, tail_count),
         out_shape=(
             shape(samples * layers * OWN, LANES),
             half_start,
             half_start,
             shape(SUBLANES, LANES),
+            tile_shape,
         )
         + (tile_shape,) * 5
         + (strip_shape,) * (5 * n)
@@ -708,43 +789,47 @@
             shape(INNER // 4, SUBLANES, LANES),
         )
         * n,
-        in_specs=[vmem(), smem] + [vmem()] * (2 + 3 * n + 1 + n + 5 + 1),
-        out_specs=(vmem(),) * (4 + 5 + 5 * n + 3 * n),
-        scratch_shapes=[pltpu.VMEM((OWN, 2, SUBLANES, LANES), jnp.float32)],
-        input_output_aliases={first_tile + k: 4 + k for k in range(5)},
+        in_specs=[vmem(), smem] + [vmem()] * (2 + 3 * n + 1 + n + 5 + 2),
+        out_specs=(vmem(),) * (5 + 5 + 5 * n + 3 * n),
+        input_output_aliases={first_tile + k: 5 + k for k in range(5)},
         compiler_params=params(),
         name="forward",
-    )(monitor.reshape(-1, LANES), ranking, *got, *got_strips, *prepared)
+    )(monitor, ranking, *got, *got_strips, *prepared)
     tile, strips, start_strips = split_refs(rest, 5, 5 * n, 3 * n)
-    start = (start_a, start_b)
-    got_start, got_start_strips = exchange(start, start_strips, kinds)
+    got_start, got_start_strips = exchange((start_a, start_b), start_strips, kinds)
     strip_coefs = [strips[5 * k + c] for k in range(n) for c in range(1, 5)]
+    begun = pl.pallas_call(
+        adjoint_ahead_kernel,
+        out_shape=(tile_shape, shape(OWN, 2, SUBLANES, LANES), saved_shape, strip_shape),
+        in_specs=[vmem()] * 5,
+        out_specs=(vmem(),) * 4,
+        input_output_aliases={0: 0},
+        compiler_params=params(),
+        name="ahead",
+    )(start, *tile[1:])
     cells = layers * OWN * count_x * LANES * count_y
-    summed = pl.pallas_call(
+    summed, _, _ = pl.pallas_call(
         functools.partial(adjoint_kernel, kinds, 0.5 / (tail_count * cells)),
-        out_shape=shape(1, number + LANES),
-        in_specs=[vmem()] * (4 + 3 * n + 4 + 4 * n + 3),
-        out_specs=vmem(),
-        scratch_shapes=[
-            pltpu.VMEM((EXT, 2, SUBLANES, LANES), jnp.float32),
-            pltpu.VMEM((OWN, 2, SUBLANES, LANES), jnp.float32),
-        ]
-        + [pltpu.VMEM((INNER, 2, SUBLANES, LANES), jnp.float32)] * (2 * n)
+        out_shape=(shape(1, number + LANES), tile_shape, shape(OWN, 2, SUBLANES, LANES)),
+        in_specs=[vmem()] * (2 + 3 * n + 4 + 4 + 4 * n + 3),
+        out_specs=(vmem(),) * 3,
+        input_output_aliases={2 + 3 * n: 1, 3 + 3 * n: 2},
+        scratch_shapes=[pltpu.VMEM((INNER, 2, SUBLANES, LANES), jnp.float32)] * (2 * n)
         + [pltpu.VMEM((OWN * layers, LANES), jnp.float32)],
         compiler_params=params(),
         name="adjoint",
     )(
-        *start,
         *got_start,
         *got_start_strips,
+        *begun,
         *tile[1:],
         *strip_coefs,
         objective,
         wells,
-        profile,
+        split,
     )
-    summed = total_over(summed, AXES)
-    return final.reshape(initial.shape), summed[0, :number], summed[0, number : number + 1]
+    gradient, objective = total_over(summed, AXES)
+    return final.reshape(initial.shape), gradient.reshape(-1), objective.reshape(-1)
 
 
 def solution(mesh):

time: 57 us -> 54.7 us (0.960)
  waiting for transfers between devices: 9.92 us -> 6.76 us
  Pallas kernels: 24.5 us -> 26.5 us
  local copies, waits for them, and re-layouts: 1.13 us -> 0.01 us
    ppermute x6, waiting for transfers between devices: 4.43 us -> 1.27 us  [exchange(): lax.ppermute(strip, AXES, swap_pairs(partner, kind, *counts))]
    pallas_call x1 -> x3, Pallas kernels: 1.89 us -> 3.16 us  [the longest x1 1.5 us: local(): pl.pallas_call(rims_kernel, out_shape=(half_tile, half_tile), in_specs=[h...]
    pallas_call x1, Pallas kernels: 1.17 us -> 2.44 us  [local(): pl.pallas_call(functools.partial(strip_pack_kernel, kinds), out_shape=(sh...]
    slice x2 -> x0, local copies, waits for them, and re-layouts: 1.12 us -> none  [the longest x1 0.61 us: local(): summed[0, :number]]
    pallas_call x1, Pallas kernels: 5.84 us -> 6.68 us  [local(): pl.pallas_call(functools.partial(source_kernel, kinds), out_shape=(tile_s...]
    pallas_call x1, Pallas kernels: 8 us -> 7.3 us  [local(): pl.pallas_call(functools.partial(adjoint_kernel, kinds, 0.5 / (tail_count...]
    pallas_call x1, Pallas kernels: 7.65 us -> 6.96 us  [local(): pl.pallas_call(functools.partial(forward_kernel, kinds, tail_count), out_...]
  transfers between devices with their start and end apart: 16 -> 16, of which waited for: 7 -> 7; matrix products, arithmetic and copies ran while one was open for 0% -> 0% of each run, Pallas kernels for 12% -> 19%
where the time goes in v4:
time: 54.7 us; the launch traced here: 54.5 us
  Pallas kernels  26.5 us (48%)
  starting transfers between devices  20.5 us (37%)
  waiting for transfers between devices  6.76 us (12%)
  between operations  0.72 us (1%)
    ppermute x6, starting transfers between devices, exchange(): lax.ppermute(strip, AXES, swap_pairs(partner, kind, *counts))  8.17 us
    pallas_call x1, Pallas kernels, local(): pl.pallas_call(functools.partial(adjoint_kernel, kinds, 0.5 / (tail_count...  7.3 us
    pallas_call x1, Pallas kernels, local(): pl.pallas_call(functools.partial(forward_kernel, kinds, tail_count), out_...  6.96 us
    pallas_call x1, Pallas kernels, local(): pl.pallas_call(functools.partial(source_kernel, kinds), out_shape=(tile_s...  6.68 us
    ppermute x6, starting transfers between devices, total_over(): lax.ppermute(value, axes, [(i, i ^ b) for i in range(count)])  6.52 us
    ppermute x4, starting transfers between devices, exchange(): lax.ppermute(tile, AXES, swap_pairs(partner, 'tile', *counts))  5.79 us
    ppermute x6, waiting for transfers between devices, total_over(): lax.ppermute(value, axes, [(i, i ^ b) for i in range(count)])  5.48 us
    pallas_call x1, Pallas kernels, local(): pl.pallas_call(functools.partial(strip_pack_kernel, kinds), out_shape=(sh...  2.44 us
  transfers between devices with their start and end apart: 16, of which 7 were waited for; matrix products, arithmetic and copies ran while one was open for 0% of the time, Pallas kernels for 19%

profile of v4, /device:TPU:0, one launch (start us, length us, event | category | flops | bytes accessed | tf_op | source)
XLA Modules:
  0.0 54.5 jit_solution(3657829661097625234)
XLA Ops:
  0.6 1.5 %rims.1 = (f32[4,4,4,16,128]{4,3,2,1,0:T(8,128)S(1)}, f32[4,4,4,16,128]{4,3,2,1,0:T(8,128)S(1)}) custom-call(f32[4,4,32,128]{3,2,1,0:T(8,128)} %initial.1, f32[4,4,32,128]{3,2,1,0:T(8,128)} %retard.1, f32[4,4,32,128]{3,2,1,0:T(8,128)} %velx.1, f32[4,4,32,128]{3,2,1,0:T(8,128)} %vely.1), custom_call_target="tpu_custom_call" | custom-call | tf_op jit(solution)/shard_map/rims/pallas_call | solution.py:714
  2.2 3.1 %collective-permute-start = (f32[4,4,4,16,128]{4,3,2,1,0:T(8,128)S(1)}, f32[4,4,4,16,128]{4,3,2,1,0:T(8,128)S(1)}, u32[]{:S(2)}, u32[]{:S(2)}) collective-permute-start(f32[4,4,4,16,128]{4,3,2,1,0:T(8,128)S(1)} %get-tuple-element.46), channel_id=1, source_target_pairs={{4,0},{5,1},{6,2},{7,3},{0,4},{1,5},{2,6},{3,7},{12,8},{13,9},{14,... | collective-permute-start | bytes 1572872 | tf_op jit(solution)/shard_map/ppermute | solution.py:653
  5.2 0.0 collective-permute-start.1
  5.2 2.4 %strips.1 = (f32[4,512,128]{2,1,0:T(8,128)S(1)}, f32[128,128]{1,0:T(8,128)S(1)}, f32[1,4096]{1,0:T(1,128)S(1)}, s32[1,4096]{1,0:T(1,128)S(1)}, f32[16,2,8,128]{3...) custom-call(f32[512,128]{1,0:T(8,128)} %bitcast.14, f32[512,128]{1,0:T(8,128)} %bitcast.15, ...), custom_call_target="tpu_custom_call" | custom-call | tf_op jit(solution)/shard_map/strips/pallas_call | solution.py:723
  7.7 1.6 %collective-permute-start.2 = (f32[16,2,8,128]{3,2,1,0:T(8,128)S(1)}, f32[16,2,8,128]{3,2,1,0:T(8,128)S(1)}, u32[]{:S(2)}, u32[]{:S(2)}) collective-permute-start(f32[16,2,8,128]{3,2,1,0:T(8,128)S(1)} %get-tuple-element.48), channel_id=1, source_target_pairs={{2,0},{3,1},{0,2},{1,3},{6,4},{7,5},{4,6},{5,7},{10,8},{11,9},{8,1... | collective-permute-start | bytes 393224 | tf_op jit(solution)/shard_map/ppermute | solution.py:659
  9.3 3.1 %collective-permute-start.3 = (f32[8,2,8,128]{3,2,1,0:T(8,128)S(1)}, f32[8,2,8,128]{3,2,1,0:T(8,128)S(1)}, u32[]{:S(2)}, u32[]{:S(2)}) collective-permute-start(f32[8,2,8,128]{3,2,1,0:T(8,128)S(1)} %get-tuple-element.49), channel_id=1, source_target_pairs={{6,0},{7,1},{4,2},{5,3},{2,4},{3,5},{0,6},{1,7},{14,8},{15,9},{12,... | collective-permute-start | bytes 196616 | tf_op jit(solution)/shard_map/ppermute | solution.py:659
  12.4 0.0 collective-permute-start.4
  12.4 6.7 %source.1 = (f32[64,2,8,128]{3,2,1,0:T(8,128)S(1)}, f32[16,2,8,128]{3,2,1,0:T(8,128)S(1)}, f32[64,2,8,128]{3,2,1,0:T(8,128)S(1)}, f32[64,2,8,128]{3,2,1,0:T(8,12...) custom-call(s32[1,4096]{1,0:T(1,128)S(1)} %get-tuple-element.51.well, ...), custom_call_target="tpu_custom_call" | custom-call | tf_op jit(solution)/shard_map/source/pallas_call | solution.py:751
  19.1 0.6 %collective-permute-done.3.refs_5_ = f32[8,2,8,128]{3,2,1,0:T(8,128)S(1)} collective-permute-done((f32[8,2,8,128]{3,2,1,0:T(8,128)S(1)}, f32[8,2,8,128]{3,2,1,0:T(8,128)S(1)}, u32[]{:S(2)}, u32[]{:S(2)}) %collective-permute-start.3) | collective-permute-done | bytes 65568 | tf_op jit(solution)/shard_map/ppermute | solution.py:659
  19.7 0.0 collective-permute-done.1
  19.7 7.0 %forward.1 = (f32[512,128]{1,0:T(8,128)}, f32[16,2,8,128]{3,2,1,0:T(8,128)S(1)}, f32[16,2,8,128]{3,2,1,0:T(8,128)S(1)}, f32[8,128]{1,0:T(8,128)S(1)}, f32[64,2,8...) custom-call(f32[128,128]{1,0:T(8,128)S(1)} %get-tuple-element.45.ref, ...), custom_call_target="tpu_custom_call", output_to_operand_aliasing={{5}: (9, {}), {6}: (10, {}), {7}: (11, {}), {8}: (12, {}), ... | custom-call | tf_op jit(solution)/shard_map/forward/pallas_call | solution.py:775
  26.7 2.7 %collective-permute-start.5 = (f32[16,2,8,128]{3,2,1,0:T(8,128)S(1)}, f32[16,2,8,128]{3,2,1,0:T(8,128)S(1)}, u32[]{:S(2)}, u32[]{:S(2)}) collective-permute-start(f32[16,2,8,128]{3,2,1,0:T(8,128)S(1)} %get-tuple-element.64), channel_id=1, source_target_pairs={{4,0},{5,1},{6,2},{7,3},{0,4},{1,5},{2,6},{3,7},{12,8},{13,9},{14,... | collective-permute-start | bytes 393224 | tf_op jit(solution)/shard_map/ppermute | solution.py:653
  29.3 0.0 collective-permute-start.6
  29.4 0.5 collective-permute-start.7
  29.9 3.0 %collective-permute-start.8 = (f32[4,8,128]{2,1,0:T(8,128)S(1)}, f32[4,8,128]{2,1,0:T(8,128)S(1)}, u32[]{:S(2)}, u32[]{:S(2)}) collective-permute-start(f32[4,8,128]{2,1,0:T(8,128)S(1)} %get-tuple-element.67), channel_id=1, source_target_pairs={{6,0},{7,1},{4,2},{5,3},{2,4},{3,5},{0,6},{1,7},{14,8},{15,9},{12,... | collective-permute-start | bytes 49160 | tf_op jit(solution)/shard_map/ppermute | solution.py:659
  32.8 0.0 collective-permute-start.9
  32.8 1.0 %ahead.1 = (f32[64,2,8,128]{3,2,1,0:T(8,128)S(1)}, f32[32,2,8,128]{3,2,1,0:T(8,128)S(1)}, f32[8,4,8,128]{3,2,1,0:T(8,128)S(1)}, f32[16,2,8,128]{3,2,1,0:T(8,128)S(1)}) custom-call(f32[64,2,8,128]{3,2,1,0:T(8,128)S(1)} %get-tuple-element.69.refs_0_, f32[64,2,8,128]{3,2,1,0:T(8,128)S(1)} %get-tuple-element.70.refs_1_.refs_9_, ...), custom_call_target="tpu_custom_call", output_to_operand_aliasing={{0}: (0, {})} | custom-call | tf_op jit(solution)/shard_map/ahead/pallas_call | solution.py:801
  33.9 0.7 %collective-permute-done.8.refs_3_ = f32[4,8,128]{2,1,0:T(8,128)S(1)} collective-permute-done((f32[4,8,128]{2,1,0:T(8,128)S(1)}, f32[4,8,128]{2,1,0:T(8,128)S(1)}, u32[]{:S(2)}, u32[]{:S(2)}) %collective-permute-start.8) | collective-permute-done | bytes 16416 | tf_op jit(solution)/shard_map/ppermute | solution.py:659
  34.6 0.0 collective-permute-done.6.refs_1_
  34.6 7.3 %adjoint.1 = (f32[1,4224]{1,0:T(1,128)S(1)}, f32[64,2,8,128]{3,2,1,0:T(8,128)S(1)}, f32[32,2,8,128]{3,2,1,0:T(8,128)S(1)}) custom-call(f32[16,2,8,128]{3,2,1,0:T(8,128)S(1)} %collective-permute-done.5.refs_0_, f32[16,2,8,128]{3,2,1,0:T(8,128)S(1)} %collective-permute-done.6.refs_1_, ...), custom_call_target="tpu_custom_call", output_to_operand_aliasing={{1}: (5, {}), {2}: (6, {})} | custom-call | tf_op jit(solution)/shard_map/adjoint/pallas_call | solution.py:811
  41.9 0.1 collective-permute-start.12
  42.0 1.4 %collective-permute-start.11 = (f32[1,4224]{1,0:T(1,128)S(1)}, f32[1,4224]{1,0:T(1,128)S(1)}, u32[]{:S(2)}, u32[]{:S(2)}) collective-permute-start(f32[1,4224]{1,0:T(1,128)S(1)} %get-tuple-element.84), channel_id=1, source_target_pairs={{0,2},{1,3},{2,0},{3,1},{4,6},{5,7},{6,4},{7,5},{8,10},{9,11},{10,... | collective-permute-start | bytes 50696 | tf_op jit(solution)/shard_map/ppermute | solution.py:680
  43.4 0.3 collective-permute-start.10
  43.8 1.4 %collective-permute-done.12 = f32[1,4224]{1,0:T(1,128)S(1)} collective-permute-done((f32[1,4224]{1,0:T(1,128)S(1)}, f32[1,4224]{1,0:T(1,128)S(1)}, u32[]{:S(2)}, u32[]{:S(2)}) %collective-permute-start.12) | collective-permute-done | bytes 16928 | tf_op jit(solution)/shard_map/ppermute | solution.py:680
  45.2 0.6 %collective-permute-done.11 = f32[1,4224]{1,0:T(1,128)S(1)} collective-permute-done((f32[1,4224]{1,0:T(1,128)S(1)}, f32[1,4224]{1,0:T(1,128)S(1)}, u32[]{:S(2)}, u32[]{:S(2)}) %collective-permute-start.11) | collective-permute-done | bytes 16928 | tf_op jit(solution)/shard_map/ppermute | solution.py:680
  45.8 2.7 %collective-permute-start.15 = (f32[1,4224]{1,0:T(1,128)S(1)}, f32[1,4224]{1,0:T(1,128)S(1)}, u32[]{:S(2)}, u32[]{:S(2)}) collective-permute-start(f32[1,4224]{1,0:T(1,128)S(1)} %add_add_fusion.value), channel_id=1, source_target_pairs={{0,12},{1,13},{2,14},{3,15},{4,8},{5,9},{6,10},{7,11},{8,4},{9,5},... | collective-permute-start | bytes 50696 | tf_op jit(solution)/shard_map/ppermute | solution.py:680
  48.5 1.7 %collective-permute-start.14 = (f32[1,4224]{1,0:T(1,128)S(1)}, f32[1,4224]{1,0:T(1,128)S(1)}, u32[]{:S(2)}, u32[]{:S(2)}) collective-permute-start(f32[1,4224]{1,0:T(1,128)S(1)} %add_add_fusion.value), channel_id=1, source_target_pairs={{0,8},{1,9},{2,10},{3,11},{4,12},{5,13},{6,14},{7,15},{8,0},{9,1},... | collective-permute-start | bytes 50696 | tf_op jit(solution)/shard_map/ppermute | solution.py:680
  50.2 0.3 collective-permute-start.13
  50.5 0.9 %collective-permute-done.15.refs_2_ = f32[1,4224]{1,0:T(1,128)S(1)} collective-permute-done((f32[1,4224]{1,0:T(1,128)S(1)}, f32[1,4224]{1,0:T(1,128)S(1)}, u32[]{:S(2)}, u32[]{:S(2)}) %collective-permute-start.15) | collective-permute-done | bytes 16928 | tf_op jit(solution)/shard_map/ppermute | solution.py:680
  51.4 1.7 %collective-permute-done.14.refs_1_ = f32[1,4224]{1,0:T(1,128)S(1)} collective-permute-done((f32[1,4224]{1,0:T(1,128)S(1)}, f32[1,4224]{1,0:T(1,128)S(1)}, u32[]{:S(2)}, u32[]{:S(2)}) %collective-permute-start.14) | collective-permute-done | bytes 16928 | tf_op jit(solution)/shard_map/ppermute | solution.py:680
  53.2 0.8 %collective-permute-done.13.refs_0_ = f32[1,4224]{1,0:T(1,128)S(1)} collective-permute-done((f32[1,4224]{1,0:T(1,128)S(1)}, f32[1,4224]{1,0:T(1,128)S(1)}, u32[]{:S(2)}, u32[]{:S(2)}) %collective-permute-start.13) | collective-permute-done | bytes 16928 | tf_op jit(solution)/shard_map/ppermute | solution.py:680
  53.9 0.6 %total.1 = (f32[1,4096]{1,0:T(1,128)}, f32[1,1]{1,0:T(1,128)}) custom-call(f32[1,4224]{1,0:T(1,128)S(1)} %add_add_fusion.value, f32[1,4224]{1,0:T(1,128)S(1)} %collective-permute-done.13.refs_0_, f32[1,4224]{1,0:T(1,128)S(1)} %collective-permute-done.14.refs_1_, f32[1,4224]{1,0:T(1,128)S(1)} %collective-permute-done.15.refs_2_), custom_call_target="tpu_custom_call" | custom-call | tf_op jit(solution)/shard_map/total/pallas_call | solution.py:687
  (12 shorter events, 0.1 us)
Async XLA Ops:
  0.6 11.7 %copy-start = (f32[4096,128]{1,0:T(8,128)S(1)}, f32[4096,128]{1,0:T(8,128)}, u32[]{:S(2)}) copy-start(f32[4096,128]{1,0:T(8,128)} %profile.1) | copy-start | bytes 6291460
  2.2 17.5 %collective-permute-start = (f32[4,4,4,16,128]{4,3,2,1,0:T(8,128)S(1)}, f32[4,4,4,16,128]{4,3,2,1,0:T(8,128)S(1)}, u32[]{:S(2)}, u32[]{:S(2)}) collective-permute-start(f32[4,4,4,16,128]{4,3,2,1,0:T(8,128)S(1)} %get-tuple-element.46), channel_id=1, source_target_pairs={{4,0},{5,1},{6,2},{7,3},{0,4},{1,5},{2,6},{3,7},{12,8},{13,9},{14,... | collective-permute-start | bytes 1572872 | tf_op jit(solution)/shard_map/ppermute | solution.py:653
  5.2 14.4 %collective-permute-start.1 = (f32[4,4,4,16,128]{4,3,2,1,0:T(8,128)S(1)}, f32[4,4,4,16,128]{4,3,2,1,0:T(8,128)S(1)}, u32[]{:S(2)}, u32[]{:S(2)}) collective-permute-start(f32[4,4,4,16,128]{4,3,2,1,0:T(8,128)S(1)} %get-tuple-element.47), channel_id=1, source_target_pairs={{1,0},{0,1},{3,2},{2,3},{8,4},{9,5},{10,6},{11,7},{4,8},{5,9},{6,1... | collective-permute-start | bytes 1572872 | tf_op jit(solution)/shard_map/ppermute | solution.py:653
  5.2 14.4 %copy-start.1 = (s32[4]{0:T(128)S(1)}, s32[4]{0:T(128)}, u32[]{:S(2)}) copy-start(s32[4]{0:T(128)} %refs_1_.1) | copy-start | bytes 52
  7.7 12.0 %collective-permute-start.2 = (f32[16,2,8,128]{3,2,1,0:T(8,128)S(1)}, f32[16,2,8,128]{3,2,1,0:T(8,128)S(1)}, u32[]{:S(2)}, u32[]{:S(2)}) collective-permute-start(f32[16,2,8,128]{3,2,1,0:T(8,128)S(1)} %get-tuple-element.48), channel_id=1, source_target_pairs={{2,0},{3,1},{0,2},{1,3},{6,4},{7,5},{4,6},{5,7},{10,8},{11,9},{8,1... | collective-permute-start | bytes 393224 | tf_op jit(solution)/shard_map/ppermute | solution.py:659
  9.3 10.4 %collective-permute-start.3 = (f32[8,2,8,128]{3,2,1,0:T(8,128)S(1)}, f32[8,2,8,128]{3,2,1,0:T(8,128)S(1)}, u32[]{:S(2)}, u32[]{:S(2)}) collective-permute-start(f32[8,2,8,128]{3,2,1,0:T(8,128)S(1)} %get-tuple-element.49), channel_id=1, source_target_pairs={{6,0},{7,1},{4,2},{5,3},{2,4},{3,5},{0,6},{1,7},{14,8},{15,9},{12,... | collective-permute-start | bytes 196616 | tf_op jit(solution)/shard_map/ppermute | solution.py:659
  12.4 7.3 %collective-permute-start.4 = (f32[8,2,8,128]{3,2,1,0:T(8,128)S(1)}, f32[8,2,8,128]{3,2,1,0:T(8,128)S(1)}, u32[]{:S(2)}, u32[]{:S(2)}) collective-permute-start(f32[8,2,8,128]{3,2,1,0:T(8,128)S(1)} %get-tuple-element.50), channel_id=1, source_target_pairs={{1,0},{0,1},{3,2},{2,3},{10,4},{11,5},{8,6},{9,7},{6,8},{7,9},{4,1... | collective-permute-start | bytes 196616 | tf_op jit(solution)/shard_map/ppermute | solution.py:659
  26.7 7.9 %collective-permute-start.5 = (f32[16,2,8,128]{3,2,1,0:T(8,128)S(1)}, f32[16,2,8,128]{3,2,1,0:T(8,128)S(1)}, u32[]{:S(2)}, u32[]{:S(2)}) collective-permute-start(f32[16,2,8,128]{3,2,1,0:T(8,128)S(1)} %get-tuple-element.64), channel_id=1, source_target_pairs={{4,0},{5,1},{6,2},{7,3},{0,4},{1,5},{2,6},{3,7},{12,8},{13,9},{14,... | collective-permute-start | bytes 393224 | tf_op jit(solution)/shard_map/ppermute | solution.py:653
  29.3 5.2 %collective-permute-start.6 = (f32[16,2,8,128]{3,2,1,0:T(8,128)S(1)}, f32[16,2,8,128]{3,2,1,0:T(8,128)S(1)}, u32[]{:S(2)}, u32[]{:S(2)}) collective-permute-start(f32[16,2,8,128]{3,2,1,0:T(8,128)S(1)} %get-tuple-element.65), channel_id=1, source_target_pairs={{1,0},{0,1},{3,2},{2,3},{8,4},{9,5},{10,6},{11,7},{4,8},{5,9},{6,1... | collective-permute-start | bytes 393224 | tf_op jit(solution)/shard_map/ppermute | solution.py:653
  29.4 5.2 %collective-permute-start.7 = (f32[8,8,128]{2,1,0:T(8,128)S(1)}, f32[8,8,128]{2,1,0:T(8,128)S(1)}, u32[]{:S(2)}, u32[]{:S(2)}) collective-permute-start(f32[8,8,128]{2,1,0:T(8,128)S(1)} %get-tuple-element.66), channel_id=1, source_target_pairs={{2,0},{3,1},{0,2},{1,3},{6,4},{7,5},{4,6},{5,7},{10,8},{11,9},{8,1... | collective-permute-start | bytes 98312 | tf_op jit(solution)/shard_map/ppermute | solution.py:659
  29.9 4.7 %collective-permute-start.8 = (f32[4,8,128]{2,1,0:T(8,128)S(1)}, f32[4,8,128]{2,1,0:T(8,128)S(1)}, u32[]{:S(2)}, u32[]{:S(2)}) collective-permute-start(f32[4,8,128]{2,1,0:T(8,128)S(1)} %get-tuple-element.67), channel_id=1, source_target_pairs={{6,0},{7,1},{4,2},{5,3},{2,4},{3,5},{0,6},{1,7},{14,8},{15,9},{12,... | collective-permute-start | bytes 49160 | tf_op jit(solution)/shard_map/ppermute | solution.py:659
  32.8 1.7 %collective-permute-start.9 = (f32[4,8,128]{2,1,0:T(8,128)S(1)}, f32[4,8,128]{2,1,0:T(8,128)S(1)}, u32[]{:S(2)}, u32[]{:S(2)}) collective-permute-start(f32[4,8,128]{2,1,0:T(8,128)S(1)} %get-tuple-element.68), channel_id=1, source_target_pairs={{1,0},{0,1},{3,2},{2,3},{10,4},{11,5},{8,6},{9,7},{6,8},{7,9},{4,1... | collective-permute-start | bytes 49160 | tf_op jit(solution)/shard_map/ppermute | solution.py:659
  41.9 3.3 %collective-permute-start.12 = (f32[1,4224]{1,0:T(1,128)S(1)}, f32[1,4224]{1,0:T(1,128)S(1)}, u32[]{:S(2)}, u32[]{:S(2)}) collective-permute-start(f32[1,4224]{1,0:T(1,128)S(1)} %get-tuple-element.84), channel_id=1, source_target_pairs={{0,3},{1,2},{2,1},{3,0},{4,7},{5,6},{6,5},{7,4},{8,11},{9,10},{10,... | collective-permute-start | bytes 50696 | tf_op jit(solution)/shard_map/ppermute | solution.py:680
  42.0 3.7 %collective-permute-start.11 = (f32[1,4224]{1,0:T(1,128)S(1)}, f32[1,4224]{1,0:T(1,128)S(1)}, u32[]{:S(2)}, u32[]{:S(2)}) collective-permute-start(f32[1,4224]{1,0:T(1,128)S(1)} %get-tuple-element.84), channel_id=1, source_target_pairs={{0,2},{1,3},{2,0},{3,1},{4,6},{5,7},{6,4},{7,5},{8,10},{9,11},{10,... | collective-permute-start | bytes 50696 | tf_op jit(solution)/shard_map/ppermute | solution.py:680
  43.4 2.4 %collective-permute-start.10 = (f32[1,4224]{1,0:T(1,128)S(1)}, f32[1,4224]{1,0:T(1,128)S(1)}, u32[]{:S(2)}, u32[]{:S(2)}) collective-permute-start(f32[1,4224]{1,0:T(1,128)S(1)} %get-tuple-element.84), channel_id=1, source_target_pairs={{0,1},{1,0},{2,3},{3,2},{4,5},{5,4},{6,7},{7,6},{8,9},{9,8},{10,11... | collective-permute-start | bytes 50696 | tf_op jit(solution)/shard_map/ppermute | solution.py:680
  45.8 5.6 %collective-permute-start.15 = (f32[1,4224]{1,0:T(1,128)S(1)}, f32[1,4224]{1,0:T(1,128)S(1)}, u32[]{:S(2)}, u32[]{:S(2)}) collective-permute-start(f32[1,4224]{1,0:T(1,128)S(1)} %add_add_fusion.value), channel_id=1, source_target_pairs={{0,12},{1,13},{2,14},{3,15},{4,8},{5,9},{6,10},{7,11},{8,4},{9,5},... | collective-permute-start | bytes 50696 | tf_op jit(solution)/shard_map/ppermute | solution.py:680
  48.5 4.6 %collective-permute-start.14 = (f32[1,4224]{1,0:T(1,128)S(1)}, f32[1,4224]{1,0:T(1,128)S(1)}, u32[]{:S(2)}, u32[]{:S(2)}) collective-permute-start(f32[1,4224]{1,0:T(1,128)S(1)} %add_add_fusion.value), channel_id=1, source_target_pairs={{0,8},{1,9},{2,10},{3,11},{4,12},{5,13},{6,14},{7,15},{8,0},{9,1},... | collective-permute-start | bytes 50696 | tf_op jit(solution)/shard_map/ppermute | solution.py:680
  50.2 3.7 %collective-permute-start.13 = (f32[1,4224]{1,0:T(1,128)S(1)}, f32[1,4224]{1,0:T(1,128)S(1)}, u32[]{:S(2)}, u32[]{:S(2)}) collective-permute-start(f32[1,4224]{1,0:T(1,128)S(1)} %add_add_fusion.value), channel_id=1, source_target_pairs={{0,4},{1,5},{2,6},{3,7},{4,0},{5,1},{6,2},{7,3},{8,12},{9,13},{10,... | collective-permute-start | bytes 50696 | tf_op jit(solution)/shard_map/ppermute | solution.py:680

commit v5 on v4

--- a/solution.py
+++ b/solution.py
@@ -19,7 +19,7 @@
 GROUPS = LANES // WIDE
 INNER = EXT // GROUPS
 JOIN = ITERS // 2
-CHUNK = 512
+CHUNK = 2048
 VMEM_LIMIT = 24 * 1024 * 1024
 
 
@@ -126,7 +126,9 @@
                     for field in range(4):
                         for upper in range(2):
                             row = base + INNER // 2 * upper + i
-                            packed = put(packed, field, row, half, 4 * upper + field)
+                            target = 4 * upper + field
+                            target = slot_b(odd, target) if out is to_b else target
+                            packed = put(packed, field, row, half, target)
                     out[i, half] = packed
 
 
@@ -263,16 +265,22 @@
                     strip[i, h] = jnp.where((self.group == j) & own, moved, strip[i, h])
 
 
+def slot_b(odd, slot):
+    return lax.rem(slot + 6 - 4 * odd, LANES // DEPTH)
+
+
 def places(odd):
     return DEPTH * (2 - odd), DEPTH * (1 + odd), 3 * DEPTH * (1 - odd), 3 * DEPTH * odd
 
 
-def merge_strip(masks, number, odd, middle, own_a, own_b, rim_y, rim_a, rim_b):
+def merge_strip(masks, number, odd, slot, middle, own_a, own_b, rim_y, rim_a, rim_b):
+    first_a = places(odd)[2]
     inner = (masks.group == 1) | (masks.group == 2)
-    at_a = masks.group == 3 * (1 - odd)
-    own = jnp.where(inner, middle, jnp.where(at_a, own_a, own_b))
-    rim = jnp.where(inner, rim_y, jnp.where(at_a, rim_a, rim_b))
-    return jnp.where(masks.rim[number], rim, own)
+    own = jnp.where(masks.group == 3 * (1 - odd), own_a, own_b)
+    own = jnp.where(inner, middle, own)
+    rim = jnp.where(lane_id() // DEPTH == slot, rim_a, rim_b)
+    rim = lane_roll(rim, 2 * first_a + pick(masks.right[number], DEPTH, 0) + LANES - DEPTH * slot)
+    return jnp.where(masks.rim[number], jnp.where(inner, rim_y, rim), own)
 
 
 def forward_step(masks, tile, first, last, lower=None, upper=None, sourced=True):
@@ -413,6 +421,7 @@
     state = tile[0]
     _, _, at_a, at_b = places(odd)
     present = jnp.where(lacks_b(), 0.0, 1.0)
+    present_lanes = jnp.where(masks.group == 3 * odd, present, 1.0)
     for x in range(DEPTH):
         for h in range(2):
             raw_a = [planes(got_a.at[field], x, h, DEPTH) for field in range(4)]
@@ -425,28 +434,24 @@
             for k in range(n):
                 got = got_strips[3 * k : 3 * k + 3]
                 side = pick(masks.right[k], DEPTH, 0)
-                raw = []
-                for field in range(4):
-                    slot = DEPTH * (4 * upper + field)
-                    rim_b = got[2][i % (INNER // 2), h]
-                    rim_b = lane_roll(rim_b, 2 * at_b + side + LANES - slot)
-                    raw.append(
-                        merge_strip(
-                            masks,
-                            k,
-                            odd,
-                            edges[field, i, h],
-                            lane_roll(raw_a[field], 2 * at_a + DEPTH),
-                            lane_roll(raw_b[field], 2 * at_b + DEPTH),
-                            lane_roll(
-                                got[0][i, h], LANES + WIDE + side - 64 * (field // 2) - DEPTH * (field % 2)
-                            ),
-                            lane_roll(
-                                got[1][i % (INNER // 2), h], 2 * at_a + side + LANES - slot
-                            ),
-                            rim_b * present if field < 2 else rim_b,
-                        )
+                raw = [
+                    merge_strip(
+                        masks,
+                        k,
+                        odd,
+                        4 * upper + field,
+                        edges[field, i, h],
+                        lane_roll(raw_a[field], 2 * at_a + DEPTH),
+                        lane_roll(raw_b[field], 2 * at_b + DEPTH),
+                        lane_roll(
+                            got[0][i, h], LANES + WIDE + side - 64 * (field // 2) - DEPTH * (field % 2)
+                        ),
+                        got[1][i % (INNER // 2), h],
+                        got[2][i % (INNER // 2), h],
                     )
+                    for field in range(4)
+                ]
+                raw[:2] = [value * present_lanes for value in raw[:2]]
                 mine = strips[5 * k : 5 * k + 5]
                 for ref, value in zip(mine, (raw[0] + sources[1 + k][i, h], *coefficients(*raw[1:]))):
                     ref[i, h] = value
@@ -510,7 +515,9 @@
                 packed = None
                 for quarter in range(4):
                     for h in range(2):
-                        packed = put(packed, base + INNER // 4 * quarter + i, h, 2 * quarter + h)
+                        target = 2 * quarter + h
+                        target = slot_b(odd, target) if out is to_b else target
+                        packed = put(packed, base + INNER // 4 * quarter + i, h, target)
                 out[i] = packed
 
 
@@ -553,18 +560,19 @@
                 moved = [
                     lane_roll(part[i, h], 2 * first + DEPTH) for part, first in zip(parts, at)
                 ]
-                slot = DEPTH * (2 * quarter + h)
-                strip[i, h] = merge_strip(
+                beside = merge_strip(
                     masks,
                     k,
                     odd,
+                    2 * quarter + h,
                     edges[i, h],
                     moved[0],
                     moved[1],
                     lane_roll(got_y[i % (INNER // 2)], LANES + WIDE + side - 64 * eighth - DEPTH * h),
-                    lane_roll(got_a[i % (INNER // 4)], 2 * at[0] + side + LANES - slot),
-                    lane_roll(got_b[i % (INNER // 4)], 2 * at[1] + side + LANES - slot),
+                    got_a[i % (INNER // 4)],
+                    got_b[i % (INNER // 4)],
                 )
+                strip[i, h] = beside
         strip_refs.append((strip, *strip_coefs[4 * k : 4 * k + 4], strip_total))
         strip_total[...] = jnp.zeros_like(strip_total)
 

time: 54.7 us -> 53.5 us (0.978)
  Pallas kernels: 26.5 us -> 24 us
  waiting for transfers between devices: 6.76 us -> 8.04 us
    pallas_call x1, Pallas kernels: 6.68 us -> 5.4 us  [local(): pl.pallas_call(functools.partial(source_kernel, kinds), out_shape=(tile_s...]
    ppermute x6, waiting for transfers between devices: 1.27 us -> 2.54 us  [exchange(): lax.ppermute(strip, AXES, swap_pairs(partner, kind, *counts))]
    pallas_call x1, Pallas kernels: 7.3 us -> 6.21 us  [local(): pl.pallas_call(functools.partial(adjoint_kernel, kinds, 0.5 / (tail_count...]
  transfers between devices with their start and end apart: 16 -> 16, of which waited for: 7 -> 7; matrix products, arithmetic and copies ran while one was open for 0% -> 0% of each run, Pallas kernels for 19% -> 17%
where the time goes in v5:
time: 53.5 us; the launch traced here: 53.3 us
  Pallas kernels  24 us (45%)
  starting transfers between devices  20.5 us (38%)
  waiting for transfers between devices  8.04 us (15%)
  between operations  0.72 us (1%)
    ppermute x6, starting transfers between devices, exchange(): lax.ppermute(strip, AXES, swap_pairs(partner, kind, *counts))  8.17 us
    pallas_call x1, Pallas kernels, local(): pl.pallas_call(functools.partial(forward_kernel, kinds, tail_count), out_...  6.82 us
    ppermute x6, starting transfers between devices, total_over(): lax.ppermute(value, axes, [(i, i ^ b) for i in range(count)])  6.52 us
    pallas_call x1, Pallas kernels, local(): pl.pallas_call(functools.partial(adjoint_kernel, kinds, 0.5 / (tail_count...  6.21 us
    ppermute x4, starting transfers between devices, exchange(): lax.ppermute(tile, AXES, swap_pairs(partner, 'tile', *counts))  5.79 us
    ppermute x6, waiting for transfers between devices, total_over(): lax.ppermute(value, axes, [(i, i ^ b) for i in range(count)])  5.49 us
    pallas_call x1, Pallas kernels, local(): pl.pallas_call(functools.partial(source_kernel, kinds), out_shape=(tile_s...  5.4 us
    ppermute x6, waiting for transfers between devices, exchange(): lax.ppermute(strip, AXES, swap_pairs(partner, kind, *counts))  2.54 us
  transfers between devices with their start and end apart: 16, of which 7 were waited for; matrix products, arithmetic and copies ran while one was open for 0% of the time, Pallas kernels for 17%

profile of v5, /device:TPU:0, one launch (start us, length us, event | category | flops | bytes accessed | tf_op | source)
XLA Modules:
  0.0 53.3 jit_solution(3231227045640399805)
XLA Ops:
  0.6 1.5 %rims.1 = (f32[4,4,4,16,128]{4,3,2,1,0:T(8,128)S(1)}, f32[4,4,4,16,128]{4,3,2,1,0:T(8,128)S(1)}) custom-call(f32[4,4,32,128]{3,2,1,0:T(8,128)} %initial.1, f32[4,4,32,128]{3,2,1,0:T(8,128)} %retard.1, f32[4,4,32,128]{3,2,1,0:T(8,128)} %velx.1, f32[4,4,32,128]{3,2,1,0:T(8,128)} %vely.1), custom_call_target="tpu_custom_call" | custom-call | tf_op jit(solution)/shard_map/rims/pallas_call | solution.py:722
  2.2 3.1 %collective-permute-start = (f32[4,4,4,16,128]{4,3,2,1,0:T(8,128)S(1)}, f32[4,4,4,16,128]{4,3,2,1,0:T(8,128)S(1)}, u32[]{:S(2)}, u32[]{:S(2)}) collective-permute-start(f32[4,4,4,16,128]{4,3,2,1,0:T(8,128)S(1)} %get-tuple-element.46), channel_id=1, source_target_pairs={{4,0},{5,1},{6,2},{7,3},{0,4},{1,5},{2,6},{3,7},{12,8},{13,9},{14,... | collective-permute-start | bytes 1572872 | tf_op jit(solution)/shard_map/ppermute | solution.py:661
  5.2 0.0 collective-permute-start.1
  5.2 2.4 %strips.1 = (f32[4,512,128]{2,1,0:T(8,128)S(1)}, f32[128,128]{1,0:T(8,128)S(1)}, f32[1,4096]{1,0:T(1,128)S(1)}, s32[1,4096]{1,0:T(1,128)S(1)}, f32[16,2,8,128]{3...) custom-call(f32[512,128]{1,0:T(8,128)} %bitcast.14, f32[512,128]{1,0:T(8,128)} %bitcast.15, ...), custom_call_target="tpu_custom_call" | custom-call | tf_op jit(solution)/shard_map/strips/pallas_call | solution.py:731
  7.7 1.6 %collective-permute-start.2 = (f32[16,2,8,128]{3,2,1,0:T(8,128)S(1)}, f32[16,2,8,128]{3,2,1,0:T(8,128)S(1)}, u32[]{:S(2)}, u32[]{:S(2)}) collective-permute-start(f32[16,2,8,128]{3,2,1,0:T(8,128)S(1)} %get-tuple-element.48), channel_id=1, source_target_pairs={{2,0},{3,1},{0,2},{1,3},{6,4},{7,5},{4,6},{5,7},{10,8},{11,9},{8,1... | collective-permute-start | bytes 393224 | tf_op jit(solution)/shard_map/ppermute | solution.py:667
  9.3 3.1 %collective-permute-start.3 = (f32[8,2,8,128]{3,2,1,0:T(8,128)S(1)}, f32[8,2,8,128]{3,2,1,0:T(8,128)S(1)}, u32[]{:S(2)}, u32[]{:S(2)}) collective-permute-start(f32[8,2,8,128]{3,2,1,0:T(8,128)S(1)} %get-tuple-element.49), channel_id=1, source_target_pairs={{6,0},{7,1},{4,2},{5,3},{2,4},{3,5},{0,6},{1,7},{14,8},{15,9},{12,... | collective-permute-start | bytes 196616 | tf_op jit(solution)/shard_map/ppermute | solution.py:667
  12.4 5.4 %source.1 = (f32[64,2,8,128]{3,2,1,0:T(8,128)S(1)}, f32[16,2,8,128]{3,2,1,0:T(8,128)S(1)}, f32[64,2,8,128]{3,2,1,0:T(8,128)S(1)}, f32[64,2,8,128]{3,2,1,0:T(8,12...) custom-call(s32[1,4096]{1,0:T(1,128)S(1)} %get-tuple-element.51.well, ...), custom_call_target="tpu_custom_call" | custom-call | tf_op jit(solution)/shard_map/source/pallas_call | solution.py:759
  17.8 1.9 %collective-permute-done.3.refs_5_ = f32[8,2,8,128]{3,2,1,0:T(8,128)S(1)} collective-permute-done((f32[8,2,8,128]{3,2,1,0:T(8,128)S(1)}, f32[8,2,8,128]{3,2,1,0:T(8,128)S(1)}, u32[]{:S(2)}, u32[]{:S(2)}) %collective-permute-start.3) | collective-permute-done | bytes 65568 | tf_op jit(solution)/shard_map/ppermute | solution.py:667
  19.7 0.0 collective-permute-done.1
  19.7 6.8 %forward.1 = (f32[512,128]{1,0:T(8,128)}, f32[16,2,8,128]{3,2,1,0:T(8,128)S(1)}, f32[16,2,8,128]{3,2,1,0:T(8,128)S(1)}, f32[8,128]{1,0:T(8,128)S(1)}, f32[64,2,8...) custom-call(f32[128,128]{1,0:T(8,128)S(1)} %get-tuple-element.45.ref, ...), custom_call_target="tpu_custom_call", output_to_operand_aliasing={{5}: (9, {}), {6}: (10, {}), {7}: (11, {}), {8}: (12, {}), ... | custom-call | tf_op jit(solution)/shard_map/forward/pallas_call | solution.py:783
  26.5 2.7 %collective-permute-start.5 = (f32[16,2,8,128]{3,2,1,0:T(8,128)S(1)}, f32[16,2,8,128]{3,2,1,0:T(8,128)S(1)}, u32[]{:S(2)}, u32[]{:S(2)}) collective-permute-start(f32[16,2,8,128]{3,2,1,0:T(8,128)S(1)} %get-tuple-element.64), channel_id=1, source_target_pairs={{4,0},{5,1},{6,2},{7,3},{0,4},{1,5},{2,6},{3,7},{12,8},{13,9},{14,... | collective-permute-start | bytes 393224 | tf_op jit(solution)/shard_map/ppermute | solution.py:661
  29.2 0.0 collective-permute-start.6
  29.2 0.5 %collective-permute-start.7 = (f32[8,8,128]{2,1,0:T(8,128)S(1)}, f32[8,8,128]{2,1,0:T(8,128)S(1)}, u32[]{:S(2)}, u32[]{:S(2)}) collective-permute-start(f32[8,8,128]{2,1,0:T(8,128)S(1)} %get-tuple-element.66), channel_id=1, source_target_pairs={{2,0},{3,1},{0,2},{1,3},{6,4},{7,5},{4,6},{5,7},{10,8},{11,9},{8,1... | collective-permute-start | bytes 98312 | tf_op jit(solution)/shard_map/ppermute | solution.py:667
  29.8 3.0 %collective-permute-start.8 = (f32[4,8,128]{2,1,0:T(8,128)S(1)}, f32[4,8,128]{2,1,0:T(8,128)S(1)}, u32[]{:S(2)}, u32[]{:S(2)}) collective-permute-start(f32[4,8,128]{2,1,0:T(8,128)S(1)} %get-tuple-element.67), channel_id=1, source_target_pairs={{6,0},{7,1},{4,2},{5,3},{2,4},{3,5},{0,6},{1,7},{14,8},{15,9},{12,... | collective-permute-start | bytes 49160 | tf_op jit(solution)/shard_map/ppermute | solution.py:667
  32.7 0.0 collective-permute-start.9
  32.7 1.0 %ahead.1 = (f32[64,2,8,128]{3,2,1,0:T(8,128)S(1)}, f32[32,2,8,128]{3,2,1,0:T(8,128)S(1)}, f32[8,4,8,128]{3,2,1,0:T(8,128)S(1)}, f32[16,2,8,128]{3,2,1,0:T(8,128)S(1)}) custom-call(f32[64,2,8,128]{3,2,1,0:T(8,128)S(1)} %get-tuple-element.69.refs_0_, f32[64,2,8,128]{3,2,1,0:T(8,128)S(1)} %get-tuple-element.70.refs_1_.refs_9_, ...), custom_call_target="tpu_custom_call", output_to_operand_aliasing={{0}: (0, {})} | custom-call | tf_op jit(solution)/shard_map/ahead/pallas_call | solution.py:809
  33.8 0.7 %collective-permute-done.8.refs_3_ = f32[4,8,128]{2,1,0:T(8,128)S(1)} collective-permute-done((f32[4,8,128]{2,1,0:T(8,128)S(1)}, f32[4,8,128]{2,1,0:T(8,128)S(1)}, u32[]{:S(2)}, u32[]{:S(2)}) %collective-permute-start.8) | collective-permute-done | bytes 16416 | tf_op jit(solution)/shard_map/ppermute | solution.py:667
  34.4 0.0 collective-permute-done.7.refs_2_
  34.4 0.0 collective-permute-done.5.refs_0_
  34.4 6.2 %adjoint.1 = (f32[1,4224]{1,0:T(1,128)S(1)}, f32[64,2,8,128]{3,2,1,0:T(8,128)S(1)}, f32[32,2,8,128]{3,2,1,0:T(8,128)S(1)}) custom-call(f32[16,2,8,128]{3,2,1,0:T(8,128)S(1)} %collective-permute-done.5.refs_0_, f32[16,2,8,128]{3,2,1,0:T(8,128)S(1)} %collective-permute-done.6.refs_1_, ...), custom_call_target="tpu_custom_call", output_to_operand_aliasing={{1}: (5, {}), {2}: (6, {})} | custom-call | tf_op jit(solution)/shard_map/adjoint/pallas_call | solution.py:819
  40.7 0.1 collective-permute-start.12
  40.8 1.4 %collective-permute-start.11 = (f32[1,4224]{1,0:T(1,128)S(1)}, f32[1,4224]{1,0:T(1,128)S(1)}, u32[]{:S(2)}, u32[]{:S(2)}) collective-permute-start(f32[1,4224]{1,0:T(1,128)S(1)} %get-tuple-element.84), channel_id=1, source_target_pairs={{0,2},{1,3},{2,0},{3,1},{4,6},{5,7},{6,4},{7,5},{8,10},{9,11},{10,... | collective-permute-start | bytes 50696 | tf_op jit(solution)/shard_map/ppermute | solution.py:688
  42.2 0.3 collective-permute-start.10
  42.5 1.4 %collective-permute-done.12 = f32[1,4224]{1,0:T(1,128)S(1)} collective-permute-done((f32[1,4224]{1,0:T(1,128)S(1)}, f32[1,4224]{1,0:T(1,128)S(1)}, u32[]{:S(2)}, u32[]{:S(2)}) %collective-permute-start.12) | collective-permute-done | bytes 16928 | tf_op jit(solution)/shard_map/ppermute | solution.py:688
  44.0 0.6 %collective-permute-done.11 = f32[1,4224]{1,0:T(1,128)S(1)} collective-permute-done((f32[1,4224]{1,0:T(1,128)S(1)}, f32[1,4224]{1,0:T(1,128)S(1)}, u32[]{:S(2)}, u32[]{:S(2)}) %collective-permute-start.11) | collective-permute-done | bytes 16928 | tf_op jit(solution)/shard_map/ppermute | solution.py:688
  44.6 2.7 %collective-permute-start.15 = (f32[1,4224]{1,0:T(1,128)S(1)}, f32[1,4224]{1,0:T(1,128)S(1)}, u32[]{:S(2)}, u32[]{:S(2)}) collective-permute-start(f32[1,4224]{1,0:T(1,128)S(1)} %add_add_fusion.value), channel_id=1, source_target_pairs={{0,12},{1,13},{2,14},{3,15},{4,8},{5,9},{6,10},{7,11},{8,4},{9,5},... | collective-permute-start | bytes 50696 | tf_op jit(solution)/shard_map/ppermute | solution.py:688
  47.3 1.7 %collective-permute-start.14 = (f32[1,4224]{1,0:T(1,128)S(1)}, f32[1,4224]{1,0:T(1,128)S(1)}, u32[]{:S(2)}, u32[]{:S(2)}) collective-permute-start(f32[1,4224]{1,0:T(1,128)S(1)} %add_add_fusion.value), channel_id=1, source_target_pairs={{0,8},{1,9},{2,10},{3,11},{4,12},{5,13},{6,14},{7,15},{8,0},{9,1},... | collective-permute-start | bytes 50696 | tf_op jit(solution)/shard_map/ppermute | solution.py:688
  49.0 0.3 collective-permute-start.13
  49.2 1.0 %collective-permute-done.15.refs_2_ = f32[1,4224]{1,0:T(1,128)S(1)} collective-permute-done((f32[1,4224]{1,0:T(1,128)S(1)}, f32[1,4224]{1,0:T(1,128)S(1)}, u32[]{:S(2)}, u32[]{:S(2)}) %collective-permute-start.15) | collective-permute-done | bytes 16928 | tf_op jit(solution)/shard_map/ppermute | solution.py:688
  50.2 1.7 %collective-permute-done.14.refs_1_ = f32[1,4224]{1,0:T(1,128)S(1)} collective-permute-done((f32[1,4224]{1,0:T(1,128)S(1)}, f32[1,4224]{1,0:T(1,128)S(1)}, u32[]{:S(2)}, u32[]{:S(2)}) %collective-permute-start.14) | collective-permute-done | bytes 16928 | tf_op jit(solution)/shard_map/ppermute | solution.py:688
  51.9 0.8 %collective-permute-done.13.refs_0_ = f32[1,4224]{1,0:T(1,128)S(1)} collective-permute-done((f32[1,4224]{1,0:T(1,128)S(1)}, f32[1,4224]{1,0:T(1,128)S(1)}, u32[]{:S(2)}, u32[]{:S(2)}) %collective-permute-start.13) | collective-permute-done | bytes 16928 | tf_op jit(solution)/shard_map/ppermute | solution.py:688
  52.7 0.6 %total.1 = (f32[1,4096]{1,0:T(1,128)}, f32[1,1]{1,0:T(1,128)}) custom-call(f32[1,4224]{1,0:T(1,128)S(1)} %add_add_fusion.value, f32[1,4224]{1,0:T(1,128)S(1)} %collective-permute-done.13.refs_0_, f32[1,4224]{1,0:T(1,128)S(1)} %collective-permute-done.14.refs_1_, f32[1,4224]{1,0:T(1,128)S(1)} %collective-permute-done.15.refs_2_), custom_call_target="tpu_custom_call" | custom-call | tf_op jit(solution)/shard_map/total/pallas_call | solution.py:695
  (12 shorter events, 0.1 us)
Async XLA Ops:
  0.6 11.8 %copy-start = (f32[4096,128]{1,0:T(8,128)S(1)}, f32[4096,128]{1,0:T(8,128)}, u32[]{:S(2)}) copy-start(f32[4096,128]{1,0:T(8,128)} %profile.1) | copy-start | bytes 6291460
  2.2 17.5 %collective-permute-start = (f32[4,4,4,16,128]{4,3,2,1,0:T(8,128)S(1)}, f32[4,4,4,16,128]{4,3,2,1,0:T(8,128)S(1)}, u32[]{:S(2)}, u32[]{:S(2)}) collective-permute-start(f32[4,4,4,16,128]{4,3,2,1,0:T(8,128)S(1)} %get-tuple-element.46), channel_id=1, source_target_pairs={{4,0},{5,1},{6,2},{7,3},{0,4},{1,5},{2,6},{3,7},{12,8},{13,9},{14,... | collective-permute-start | bytes 1572872 | tf_op jit(solution)/shard_map/ppermute | solution.py:661
  5.2 14.4 %collective-permute-start.1 = (f32[4,4,4,16,128]{4,3,2,1,0:T(8,128)S(1)}, f32[4,4,4,16,128]{4,3,2,1,0:T(8,128)S(1)}, u32[]{:S(2)}, u32[]{:S(2)}) collective-permute-start(f32[4,4,4,16,128]{4,3,2,1,0:T(8,128)S(1)} %get-tuple-element.47), channel_id=1, source_target_pairs={{1,0},{0,1},{3,2},{2,3},{8,4},{9,5},{10,6},{11,7},{4,8},{5,9},{6,1... | collective-permute-start | bytes 1572872 | tf_op jit(solution)/shard_map/ppermute | solution.py:661
  5.2 14.4 %copy-start.1 = (s32[4]{0:T(128)S(1)}, s32[4]{0:T(128)}, u32[]{:S(2)}) copy-start(s32[4]{0:T(128)} %refs_1_.1) | copy-start | bytes 52
  7.7 12.0 %collective-permute-start.2 = (f32[16,2,8,128]{3,2,1,0:T(8,128)S(1)}, f32[16,2,8,128]{3,2,1,0:T(8,128)S(1)}, u32[]{:S(2)}, u32[]{:S(2)}) collective-permute-start(f32[16,2,8,128]{3,2,1,0:T(8,128)S(1)} %get-tuple-element.48), channel_id=1, source_target_pairs={{2,0},{3,1},{0,2},{1,3},{6,4},{7,5},{4,6},{5,7},{10,8},{11,9},{8,1... | collective-permute-start | bytes 393224 | tf_op jit(solution)/shard_map/ppermute | solution.py:667
  9.3 10.4 %collective-permute-start.3 = (f32[8,2,8,128]{3,2,1,0:T(8,128)S(1)}, f32[8,2,8,128]{3,2,1,0:T(8,128)S(1)}, u32[]{:S(2)}, u32[]{:S(2)}) collective-permute-start(f32[8,2,8,128]{3,2,1,0:T(8,128)S(1)} %get-tuple-element.49), channel_id=1, source_target_pairs={{6,0},{7,1},{4,2},{5,3},{2,4},{3,5},{0,6},{1,7},{14,8},{15,9},{12,... | collective-permute-start | bytes 196616 | tf_op jit(solution)/shard_map/ppermute | solution.py:667
  12.4 7.3 %collective-permute-start.4 = (f32[8,2,8,128]{3,2,1,0:T(8,128)S(1)}, f32[8,2,8,128]{3,2,1,0:T(8,128)S(1)}, u32[]{:S(2)}, u32[]{:S(2)}) collective-permute-start(f32[8,2,8,128]{3,2,1,0:T(8,128)S(1)} %get-tuple-element.50), channel_id=1, source_target_pairs={{1,0},{0,1},{3,2},{2,3},{10,4},{11,5},{8,6},{9,7},{6,8},{7,9},{4,1... | collective-permute-start | bytes 196616 | tf_op jit(solution)/shard_map/ppermute | solution.py:667
  26.5 7.9 %collective-permute-start.5 = (f32[16,2,8,128]{3,2,1,0:T(8,128)S(1)}, f32[16,2,8,128]{3,2,1,0:T(8,128)S(1)}, u32[]{:S(2)}, u32[]{:S(2)}) collective-permute-start(f32[16,2,8,128]{3,2,1,0:T(8,128)S(1)} %get-tuple-element.64), channel_id=1, source_target_pairs={{4,0},{5,1},{6,2},{7,3},{0,4},{1,5},{2,6},{3,7},{12,8},{13,9},{14,... | collective-permute-start | bytes 393224 | tf_op jit(solution)/shard_map/ppermute | solution.py:661
  29.2 5.2 %collective-permute-start.6 = (f32[16,2,8,128]{3,2,1,0:T(8,128)S(1)}, f32[16,2,8,128]{3,2,1,0:T(8,128)S(1)}, u32[]{:S(2)}, u32[]{:S(2)}) collective-permute-start(f32[16,2,8,128]{3,2,1,0:T(8,128)S(1)} %get-tuple-element.65), channel_id=1, source_target_pairs={{1,0},{0,1},{3,2},{2,3},{8,4},{9,5},{10,6},{11,7},{4,8},{5,9},{6,1... | collective-permute-start | bytes 393224 | tf_op jit(solution)/shard_map/ppermute | solution.py:661
  29.2 5.2 %collective-permute-start.7 = (f32[8,8,128]{2,1,0:T(8,128)S(1)}, f32[8,8,128]{2,1,0:T(8,128)S(1)}, u32[]{:S(2)}, u32[]{:S(2)}) collective-permute-start(f32[8,8,128]{2,1,0:T(8,128)S(1)} %get-tuple-element.66), channel_id=1, source_target_pairs={{2,0},{3,1},{0,2},{1,3},{6,4},{7,5},{4,6},{5,7},{10,8},{11,9},{8,1... | collective-permute-start | bytes 98312 | tf_op jit(solution)/shard_map/ppermute | solution.py:667
  29.8 4.7 %collective-permute-start.8 = (f32[4,8,128]{2,1,0:T(8,128)S(1)}, f32[4,8,128]{2,1,0:T(8,128)S(1)}, u32[]{:S(2)}, u32[]{:S(2)}) collective-permute-start(f32[4,8,128]{2,1,0:T(8,128)S(1)} %get-tuple-element.67), channel_id=1, source_target_pairs={{6,0},{7,1},{4,2},{5,3},{2,4},{3,5},{0,6},{1,7},{14,8},{15,9},{12,... | collective-permute-start | bytes 49160 | tf_op jit(solution)/shard_map/ppermute | solution.py:667
  32.7 1.7 %collective-permute-start.9 = (f32[4,8,128]{2,1,0:T(8,128)S(1)}, f32[4,8,128]{2,1,0:T(8,128)S(1)}, u32[]{:S(2)}, u32[]{:S(2)}) collective-permute-start(f32[4,8,128]{2,1,0:T(8,128)S(1)} %get-tuple-element.68), channel_id=1, source_target_pairs={{1,0},{0,1},{3,2},{2,3},{10,4},{11,5},{8,6},{9,7},{6,8},{7,9},{4,1... | collective-permute-start | bytes 49160 | tf_op jit(solution)/shard_map/ppermute | solution.py:667
  40.7 3.3 %collective-permute-start.12 = (f32[1,4224]{1,0:T(1,128)S(1)}, f32[1,4224]{1,0:T(1,128)S(1)}, u32[]{:S(2)}, u32[]{:S(2)}) collective-permute-start(f32[1,4224]{1,0:T(1,128)S(1)} %get-tuple-element.84), channel_id=1, source_target_pairs={{0,3},{1,2},{2,1},{3,0},{4,7},{5,6},{6,5},{7,4},{8,11},{9,10},{10,... | collective-permute-start | bytes 50696 | tf_op jit(solution)/shard_map/ppermute | solution.py:688
  40.8 3.7 %collective-permute-start.11 = (f32[1,4224]{1,0:T(1,128)S(1)}, f32[1,4224]{1,0:T(1,128)S(1)}, u32[]{:S(2)}, u32[]{:S(2)}) collective-permute-start(f32[1,4224]{1,0:T(1,128)S(1)} %get-tuple-element.84), channel_id=1, source_target_pairs={{0,2},{1,3},{2,0},{3,1},{4,6},{5,7},{6,4},{7,5},{8,10},{9,11},{10,... | collective-permute-start | bytes 50696 | tf_op jit(solution)/shard_map/ppermute | solution.py:688
  42.2 2.4 %collective-permute-start.10 = (f32[1,4224]{1,0:T(1,128)S(1)}, f32[1,4224]{1,0:T(1,128)S(1)}, u32[]{:S(2)}, u32[]{:S(2)}) collective-permute-start(f32[1,4224]{1,0:T(1,128)S(1)} %get-tuple-element.84), channel_id=1, source_target_pairs={{0,1},{1,0},{2,3},{3,2},{4,5},{5,4},{6,7},{7,6},{8,9},{9,8},{10,11... | collective-permute-start | bytes 50696 | tf_op jit(solution)/shard_map/ppermute | solution.py:688
  44.6 5.6 %collective-permute-start.15 = (f32[1,4224]{1,0:T(1,128)S(1)}, f32[1,4224]{1,0:T(1,128)S(1)}, u32[]{:S(2)}, u32[]{:S(2)}) collective-permute-start(f32[1,4224]{1,0:T(1,128)S(1)} %add_add_fusion.value), channel_id=1, source_target_pairs={{0,12},{1,13},{2,14},{3,15},{4,8},{5,9},{6,10},{7,11},{8,4},{9,5},... | collective-permute-start | bytes 50696 | tf_op jit(solution)/shard_map/ppermute | solution.py:688
  47.3 4.6 %collective-permute-start.14 = (f32[1,4224]{1,0:T(1,128)S(1)}, f32[1,4224]{1,0:T(1,128)S(1)}, u32[]{:S(2)}, u32[]{:S(2)}) collective-permute-start(f32[1,4224]{1,0:T(1,128)S(1)} %add_add_fusion.value), channel_id=1, source_target_pairs={{0,8},{1,9},{2,10},{3,11},{4,12},{5,13},{6,14},{7,15},{8,0},{9,1},... | collective-permute-start | bytes 50696 | tf_op jit(solution)/shard_map/ppermute | solution.py:688
  49.0 3.7 %collective-permute-start.13 = (f32[1,4224]{1,0:T(1,128)S(1)}, f32[1,4224]{1,0:T(1,128)S(1)}, u32[]{:S(2)}, u32[]{:S(2)}) collective-permute-start(f32[1,4224]{1,0:T(1,128)S(1)} %add_add_fusion.value), channel_id=1, source_target_pairs={{0,4},{1,5},{2,6},{3,7},{4,0},{5,1},{6,2},{7,3},{8,12},{9,13},{10,... | collective-permute-start | bytes 50696 | tf_op jit(solution)/shard_map/ppermute | solution.py:688

commit v6 on v5

--- a/solution.py
+++ b/solution.py
@@ -148,9 +148,9 @@
         ref[row, half] = value
 
 
-def source_kernel(kinds, wells, controls, profile, own, *refs):
+def source_kernel(kinds, tail_count, wells, controls, profile, own, monitor, ranking, *refs):
     n = len(kinds)
-    sources, tile, edges, (saved, split), (acc, acc_low) = split_refs(refs, 1 + n, 5, 1, 2, 2)
+    sources, tile, edges, (saved, weights, split), (acc, acc_low) = split_refs(refs, 1 + n, 5, 1, 3, 2)
     for x in range(OWN):
         for half in range(2):
             raw = [planes(own.at[field], x, half, OWN) for field in range(4)]
@@ -222,9 +222,16 @@
                     moved = lane_roll(mixed, WIDE * j + DEPTH)
                     packed = moved if packed is None else jnp.where(group == j, moved, packed)
                 sources[1 + number][i, half] = packed
+    sample = sub_id() // 2
+    tail = jnp.zeros((SUBLANES, LANES), jnp.float32)
+    for s in range(4):
+        tail = jnp.where(sample == s, jnp.where(ranking[s] < tail_count, 1.0, 0.0), tail)
     for x in range(OWN):
         for half in range(2):
             tile[0][DEPTH + x, half] += sources[0][DEPTH + x, half]
+            low = jnp.broadcast_to(monitor[pl.ds(half * OWN + x, 1), :], (SUBLANES, LANES))
+            high = jnp.broadcast_to(monitor[pl.ds((2 + half) * OWN + x, 1), :], (SUBLANES, LANES))
+            weights[x, half] = tail * jnp.where(upper, high, low)
     ahead(functools.partial(forward_step, masks, (*tile, sources[0]), sourced=True), tile[0], saved)
 
 
@@ -411,10 +418,10 @@
 
 def forward_kernel(kinds, tail_count, *refs):
     n = len(kinds)
-    ins, got_strips, sources, tile, (edges, saved), outs, strips, out_strips = split_refs(
-        refs, 4, 3 * n, 1 + n, 5, 2, 5 + 5, 5 * n, 3 * n
+    ins, got_strips, sources, tile, (edges, saved, weights), outs, strips, out_strips, states = split_refs(
+        refs, 2, 3 * n, 1 + n, 5, 3, 5 + 5, 4 * n, 3 * n, n
     )
-    monitor, ranking, got_a, got_b = ins
+    got_a, got_b = ins
     final, start_a, start_b, objective, start, *tile = outs
     odd = odd_tile()
     masks = Masks(kinds)
@@ -452,13 +459,13 @@
                     for field in range(4)
                 ]
                 raw[:2] = [value * present_lanes for value in raw[:2]]
-                mine = strips[5 * k : 5 * k + 5]
+                mine = (states[k], *strips[4 * k : 4 * k + 4])
                 for ref, value in zip(mine, (raw[0] + sources[1 + k][i, h], *coefficients(*raw[1:]))):
                     ref[i, h] = value
     for e in (*range(DEPTH), *range(DEPTH + OWN, EXT)):
         for h in range(2):
             state[e, h] += sources[0][e, h]
-    strip_refs = [(*strips[5 * k : 5 * k + 5], sources[1 + k]) for k in range(n)]
+    strip_refs = [(states[k], *strips[4 * k : 4 * k + 4], sources[1 + k]) for k in range(n)]
     strip_states = [strip[0] for strip in strip_refs]
 
     def step(first, last, sourced, **beside):
@@ -471,19 +478,12 @@
         saved,
     )
 
-    sample = sub_id() // 2
-    upper = sub_id() % 2 == 1
-    tail = jnp.zeros((SUBLANES, LANES), jnp.float32)
-    for s in range(4):
-        tail = jnp.where(sample == s, jnp.where(ranking[s] < tail_count, 1.0, 0.0), tail)
     sums = [jnp.zeros((SUBLANES, LANES), jnp.float32) for _ in range(4)]
     for x in range(OWN):
         for h in range(2):
             fresh = masks.outer_from(strip_states, DEPTH + x, h, state[DEPTH + x, h])
             final[pl.ds(h * OWN + x, SUBLANES, stride=2 * OWN), :] = fresh
-            low = jnp.broadcast_to(monitor[pl.ds(h * OWN + x, 1), :], (SUBLANES, LANES))
-            high = jnp.broadcast_to(monitor[pl.ds((2 + h) * OWN + x, 1), :], (SUBLANES, LANES))
-            weighted = tail * jnp.where(upper, high, low) * fresh
+            weighted = weights[x, h] * fresh
             start[DEPTH + x, h] = weighted * (1.0 / (tail_count * ITERS))
             sums[x % 4] = sums[x % 4] + weighted * fresh
     objective[...] = (sums[0] + sums[1]) + (sums[2] + sums[3])
@@ -522,7 +522,9 @@
 
 
 def adjoint_ahead_kernel(*refs):
-    coefs, (state, total, saved, edges) = refs[1:5], refs[5:]
+    coefs, (final, state, total, saved, edges, final_out, sem) = refs[1:5], refs[5:]
+    leave = pltpu.make_async_copy(final, final_out, sem)
+    leave.start()
     masks = Masks(())
     total[...] = jnp.zeros_like(total)
     first_j = masks.group == 1
@@ -533,15 +535,16 @@
             ]
             edges[i, h] = jnp.where(first_j, *moved)
     ahead(functools.partial(adjoint_step, masks, (state, *coefs, total)), state, saved)
+    leave.wait()
 
 
 def adjoint_kernel(kinds, scale, *refs):
     n = len(kinds)
-    parts, part_strips, (state, total, saved, edges), coefs, strip_coefs, rest, tile, strips, (rows,) = split_refs(
-        refs, 2, 3 * n, 4, 4, 4 * n, 4, 2, 2 * n, 1
+    parts, part_strips, (_, _, saved, edges), coefs, strip_coefs, rest, outs, strips, (rows,) = split_refs(
+        refs, 2, 3 * n, 4, 4, 4 * n, 3, 3, 2 * n, 1
     )
-    objective, wells, profile, out = rest
-    state, total = tile
+    objective, wells, profile = rest
+    out, state, total = outs
     odd = odd_tile()
     masks = Masks(kinds)
     at = places(odd)[2:]
@@ -713,6 +716,8 @@
     n = len(kinds)
     half_tile = shape(4, samples, layers, DEPTH, LANES)
     hbm = pl.BlockSpec(memory_space=pltpu.HBM)
+    smem = pl.BlockSpec(memory_space=pltpu.SMEM)
+    tail_count = samples * lax.axis_size("sa") // 2
     any_space = pl.BlockSpec(memory_space=pl.ANY)
     fields = (initial, retard, velx, vely)
 
@@ -757,29 +762,28 @@
     saved_shape = shape(JOIN, 4, SUBLANES, LANES)
     blocks = (1 + n) * EXT * layers
     *prepared, split = pl.pallas_call(
-        functools.partial(source_kernel, kinds),
+        functools.partial(source_kernel, kinds, tail_count),
         out_shape=(tile_shape,)
         + (strip_shape,) * n
         + (tile_shape,) * 5
         + (
             shape(4, INNER, 2, SUBLANES, LANES),
             saved_shape,
+            shape(OWN, 2, SUBLANES, LANES),
             jax.ShapeDtypeStruct((number, 2 * LANES), jnp.bfloat16),
         ),
-        in_specs=[vmem()] * 4,
-        out_specs=(vmem(),) * (1 + n + 5 + 3),
+        in_specs=[vmem()] * 5 + [smem],
+        out_specs=(vmem(),) * (1 + n + 5 + 4),
         scratch_shapes=[
             pltpu.VMEM((blocks, 2 * LANES), jnp.float32),
             pltpu.VMEM((blocks, LANES), jnp.float32),
         ],
         compiler_params=params(),
         name="source",
-    )(wells, controls, profile, own)
+    )(wells, controls, profile, own, monitor, ranking)
     got = [part.reshape(4, -1, LANES) for part in got]
-    tail_count = samples * lax.axis_size("sa") // 2
     half_start = shape(DEPTH, 2, SUBLANES, LANES)
-    smem = pl.BlockSpec(memory_space=pltpu.SMEM)
-    first_tile = 4 + 3 * n + 1 + n
+    first_tile = 2 + 3 * n + 1 + n
     final, start_a, start_b, objective, start, *rest = pl.pallas_call(
         functools.partial(forward_kernel, kinds, tail_count),
         out_shape=(
@@ -790,35 +794,46 @@
             tile_shape,
         )
         + (tile_shape,) * 5
-        + (strip_shape,) * (5 * n)
+        + (strip_shape,) * (4 * n)
         + (
             shape(INNER // 2, SUBLANES, LANES),
             shape(INNER // 4, SUBLANES, LANES),
             shape(INNER // 4, SUBLANES, LANES),
         )
         * n,
-        in_specs=[vmem(), smem] + [vmem()] * (2 + 3 * n + 1 + n + 5 + 2),
-        out_specs=(vmem(),) * (5 + 5 + 5 * n + 3 * n),
+        in_specs=[vmem()] * (2 + 3 * n + 1 + n + 5 + 3),
+        out_specs=(vmem(),) * (5 + 5 + 4 * n + 3 * n),
+        scratch_shapes=[pltpu.VMEM((INNER, 2, SUBLANES, LANES), jnp.float32)] * n,
         input_output_aliases={first_tile + k: 5 + k for k in range(5)},
         compiler_params=params(),
         name="forward",
-    )(monitor, ranking, *got, *got_strips, *prepared)
-    tile, strips, start_strips = split_refs(rest, 5, 5 * n, 3 * n)
+    )(*got, *got_strips, *prepared)
+    tile, strip_coefs, start_strips = split_refs(rest, 5, 4 * n, 3 * n)
     got_start, got_start_strips = exchange((start_a, start_b), start_strips, kinds)
-    strip_coefs = [strips[5 * k + c] for k in range(n) for c in range(1, 5)]
-    begun = pl.pallas_call(
+    *begun, final = pl.pallas_call(
         adjoint_ahead_kernel,
-        out_shape=(tile_shape, shape(OWN, 2, SUBLANES, LANES), saved_shape, strip_shape),
-        in_specs=[vmem()] * 5,
-        out_specs=(vmem(),) * 4,
+        out_shape=(
+            tile_shape,
+            shape(OWN, 2, SUBLANES, LANES),
+            saved_shape,
+            strip_shape,
+            shape(*final.shape),
+        ),
+        in_specs=[vmem()] * 6,
+        out_specs=(vmem(),) * 4 + (hbm,),
+        scratch_shapes=[pltpu.SemaphoreType.DMA],
         input_output_aliases={0: 0},
         compiler_params=params(),
         name="ahead",
-    )(start, *tile[1:])
+    )(start, *tile[1:], final)
     cells = layers * OWN * count_x * LANES * count_y
     summed, _, _ = pl.pallas_call(
         functools.partial(adjoint_kernel, kinds, 0.5 / (tail_count * cells)),
-        out_shape=(shape(1, number + LANES), tile_shape, shape(OWN, 2, SUBLANES, LANES)),
+        out_shape=(
+            shape(1, number + LANES),
+            tile_shape,
+            shape(OWN, 2, SUBLANES, LANES),
+        ),
         in_specs=[vmem()] * (2 + 3 * n + 4 + 4 + 4 * n + 3),
         out_specs=(vmem(),) * 3,
         input_output_aliases={2 + 3 * n: 1, 3 + 3 * n: 2},

time: 53.5 us -> 53.1 us (level)
  waiting for transfers between devices: 8.04 us -> 7.34 us
    ppermute x6, waiting for transfers between devices: 2.54 us -> 1.85 us  [exchange(): lax.ppermute(strip, AXES, swap_pairs(partner, kind, *counts))]
    pallas_call x1, Pallas kernels: 5.4 us -> 6.06 us  [local(): pl.pallas_call(functools.partial(source_kernel, kinds, tail_count), out_s...]
    pallas_call x1, Pallas kernels: 6.82 us -> 6.27 us  [local(): pl.pallas_call(functools.partial(forward_kernel, kinds, tail_count), out_...]
  transfers between devices with their start and end apart: 16 -> 16, of which waited for: 7 -> 7; matrix products, arithmetic and copies ran while one was open for 0% -> 0% of each run, Pallas kernels for 17% -> 18%
where the time goes in v6:
time: 53.1 us; the launch traced here: 52.9 us
  Pallas kernels  24.3 us (46%)
  starting transfers between devices  20.6 us (39%)
  waiting for transfers between devices  7.34 us (14%)
  between operations  0.73 us (1%)
    ppermute x6, starting transfers between devices, exchange(): lax.ppermute(strip, AXES, swap_pairs(partner, kind, *counts))  8.17 us
    ppermute x6, starting transfers between devices, total_over(): lax.ppermute(value, axes, [(i, i ^ b) for i in range(count)])  6.52 us
    pallas_call x1, Pallas kernels, local(): pl.pallas_call(functools.partial(adjoint_kernel, kinds, 0.5 / (tail_count...  6.32 us
    pallas_call x1, Pallas kernels, local(): pl.pallas_call(functools.partial(forward_kernel, kinds, tail_count), out_...  6.27 us
    pallas_call x1, Pallas kernels, local(): pl.pallas_call(functools.partial(source_kernel, kinds, tail_count), out_s...  6.06 us
    ppermute x4, starting transfers between devices, exchange(): lax.ppermute(tile, AXES, swap_pairs(partner, 'tile', *counts))  5.86 us
    ppermute x6, waiting for transfers between devices, total_over(): lax.ppermute(value, axes, [(i, i ^ b) for i in range(count)])  5.48 us
    pallas_call x1, Pallas kernels, local(): pl.pallas_call(functools.partial(strip_pack_kernel, kinds), out_shape=(sh...  2.43 us
  transfers between devices with their start and end apart: 16, of which 7 were waited for; matrix products, arithmetic and copies ran while one was open for 0% of the time, Pallas kernels for 18%

profile of v6, /device:TPU:0, one launch (start us, length us, event | category | flops | bytes accessed | tf_op | source)
XLA Modules:
  0.0 52.9 jit_solution(5485686611498039508)
XLA Ops:
  0.7 1.5 %rims.1 = (f32[4,4,4,16,128]{4,3,2,1,0:T(8,128)S(1)}, f32[4,4,4,16,128]{4,3,2,1,0:T(8,128)S(1)}) custom-call(f32[4,4,32,128]{3,2,1,0:T(8,128)} %initial.1, f32[4,4,32,128]{3,2,1,0:T(8,128)} %retard.1, f32[4,4,32,128]{3,2,1,0:T(8,128)} %velx.1, f32[4,4,32,128]{3,2,1,0:T(8,128)} %vely.1), custom_call_target="tpu_custom_call" | custom-call | tf_op jit(solution)/shard_map/rims/pallas_call | solution.py:727
  2.2 3.1 %collective-permute-start = (f32[4,4,4,16,128]{4,3,2,1,0:T(8,128)S(1)}, f32[4,4,4,16,128]{4,3,2,1,0:T(8,128)S(1)}, u32[]{:S(2)}, u32[]{:S(2)}) collective-permute-start(f32[4,4,4,16,128]{4,3,2,1,0:T(8,128)S(1)} %get-tuple-element.47), channel_id=1, source_target_pairs={{4,0},{5,1},{6,2},{7,3},{0,4},{1,5},{2,6},{3,7},{12,8},{13,9},{14,... | collective-permute-start | bytes 1572872 | tf_op jit(solution)/shard_map/ppermute | solution.py:664
  5.3 0.0 collective-permute-start.1
  5.3 2.4 %strips.1 = (f32[4,512,128]{2,1,0:T(8,128)S(1)}, f32[128,128]{1,0:T(8,128)S(1)}, f32[1,4096]{1,0:T(1,128)S(1)}, s32[1,4096]{1,0:T(1,128)S(1)}, f32[16,2,8,128]{3...) custom-call(f32[512,128]{1,0:T(8,128)} %bitcast.14, f32[512,128]{1,0:T(8,128)} %bitcast.15, ...), custom_call_target="tpu_custom_call" | custom-call | tf_op jit(solution)/shard_map/strips/pallas_call | solution.py:736
  7.7 1.6 %collective-permute-start.2 = (f32[16,2,8,128]{3,2,1,0:T(8,128)S(1)}, f32[16,2,8,128]{3,2,1,0:T(8,128)S(1)}, u32[]{:S(2)}, u32[]{:S(2)}) collective-permute-start(f32[16,2,8,128]{3,2,1,0:T(8,128)S(1)} %get-tuple-element.49), channel_id=1, source_target_pairs={{2,0},{3,1},{0,2},{1,3},{6,4},{7,5},{4,6},{5,7},{10,8},{11,9},{8,1... | collective-permute-start | bytes 393224 | tf_op jit(solution)/shard_map/ppermute | solution.py:670
  9.3 3.1 %collective-permute-start.3 = (f32[8,2,8,128]{3,2,1,0:T(8,128)S(1)}, f32[8,2,8,128]{3,2,1,0:T(8,128)S(1)}, u32[]{:S(2)}, u32[]{:S(2)}) collective-permute-start(f32[8,2,8,128]{3,2,1,0:T(8,128)S(1)} %get-tuple-element.50), channel_id=1, source_target_pairs={{6,0},{7,1},{4,2},{5,3},{2,4},{3,5},{0,6},{1,7},{14,8},{15,9},{12,... | collective-permute-start | bytes 196616 | tf_op jit(solution)/shard_map/ppermute | solution.py:670
  12.4 6.1 %source.1 = (f32[64,2,8,128]{3,2,1,0:T(8,128)S(1)}, f32[16,2,8,128]{3,2,1,0:T(8,128)S(1)}, f32[64,2,8,128]{3,2,1,0:T(8,128)S(1)}, f32[64,2,8,128]{3,2,1,0:T(8,12...) custom-call(s32[1,4096]{1,0:T(1,128)S(1)} %get-tuple-element.52.well, ...), custom_call_target="tpu_custom_call" | custom-call | tf_op jit(solution)/shard_map/source/pallas_call | solution.py:764
  18.5 1.2 %collective-permute-done.3.refs_3_ = f32[8,2,8,128]{3,2,1,0:T(8,128)S(1)} collective-permute-done((f32[8,2,8,128]{3,2,1,0:T(8,128)S(1)}, f32[8,2,8,128]{3,2,1,0:T(8,128)S(1)}, u32[]{:S(2)}, u32[]{:S(2)}) %collective-permute-start.3) | collective-permute-done | bytes 65568 | tf_op jit(solution)/shard_map/ppermute | solution.py:670
  19.7 0.0 collective-permute-done.4.refs_4_
  19.7 0.0 collective-permute-done.2.refs_2_
  19.7 0.0 collective-permute-done
  19.7 0.0 collective-permute-done.1
  19.7 6.3 %forward.1 = (f32[512,128]{1,0:T(8,128)S(1)}, f32[16,2,8,128]{3,2,1,0:T(8,128)S(1)}, f32[16,2,8,128]{3,2,1,0:T(8,128)S(1)}, f32[8,128]{1,0:T(8,128)S(1)}, f32[64...) custom-call(f32[4,256,128]{2,1,0:T(8,128)S(1)} %bitcast.12, ...), custom_call_target="tpu_custom_call", output_to_operand_aliasing={{5}: (7, {}), {6}: (8, {}), {7}: (9, {}), {8}: (10, {}), {9... | custom-call | tf_op jit(solution)/shard_map/forward/pallas_call | solution.py:787
  26.0 2.8 %collective-permute-start.5 = (f32[16,2,8,128]{3,2,1,0:T(8,128)S(1)}, f32[16,2,8,128]{3,2,1,0:T(8,128)S(1)}, u32[]{:S(2)}, u32[]{:S(2)}) collective-permute-start(f32[16,2,8,128]{3,2,1,0:T(8,128)S(1)} %get-tuple-element.73), channel_id=1, source_target_pairs={{4,0},{5,1},{6,2},{7,3},{0,4},{1,5},{2,6},{3,7},{12,8},{13,9},{14,... | collective-permute-start | bytes 393224 | tf_op jit(solution)/shard_map/ppermute | solution.py:664
  28.7 0.0 collective-permute-start.6
  28.7 0.5 %collective-permute-start.7 = (f32[8,8,128]{2,1,0:T(8,128)S(1)}, f32[8,8,128]{2,1,0:T(8,128)S(1)}, u32[]{:S(2)}, u32[]{:S(2)}) collective-permute-start(f32[8,8,128]{2,1,0:T(8,128)S(1)} %get-tuple-element.75), channel_id=1, source_target_pairs={{2,0},{3,1},{0,2},{1,3},{6,4},{7,5},{4,6},{5,7},{10,8},{11,9},{8,1... | collective-permute-start | bytes 98312 | tf_op jit(solution)/shard_map/ppermute | solution.py:670
  29.3 3.0 %collective-permute-start.8 = (f32[4,8,128]{2,1,0:T(8,128)S(1)}, f32[4,8,128]{2,1,0:T(8,128)S(1)}, u32[]{:S(2)}, u32[]{:S(2)}) collective-permute-start(f32[4,8,128]{2,1,0:T(8,128)S(1)} %get-tuple-element.76), channel_id=1, source_target_pairs={{6,0},{7,1},{4,2},{5,3},{2,4},{3,5},{0,6},{1,7},{14,8},{15,9},{12,... | collective-permute-start | bytes 49160 | tf_op jit(solution)/shard_map/ppermute | solution.py:670
  32.2 1.1 %ahead.1 = (f32[64,2,8,128]{3,2,1,0:T(8,128)S(1)}, f32[32,2,8,128]{3,2,1,0:T(8,128)S(1)}, f32[8,4,8,128]{3,2,1,0:T(8,128)S(1)}, f32[16,2,8,128]{3,2,1,0:T(8,128)S(1)}, f32[512,128]{1,0:T(8,128)}) custom-call(f32[64,2,8,128]{3,2,1,0:T(8,128)S(1)} %get-tuple-element.66.refs_0_, ...), custom_call_target="tpu_custom_call", output_to_operand_aliasing={{0}: (0, {})} | custom-call | tf_op jit(solution)/shard_map/ahead/pallas_call | solution.py:813
  33.3 0.6 %collective-permute-done.8.refs_3_ = f32[4,8,128]{2,1,0:T(8,128)S(1)} collective-permute-done((f32[4,8,128]{2,1,0:T(8,128)S(1)}, f32[4,8,128]{2,1,0:T(8,128)S(1)}, u32[]{:S(2)}, u32[]{:S(2)}) %collective-permute-start.8) | collective-permute-done | bytes 16416 | tf_op jit(solution)/shard_map/ppermute | solution.py:670
  34.0 6.3 %adjoint.1 = (f32[1,4224]{1,0:T(1,128)S(1)}, f32[64,2,8,128]{3,2,1,0:T(8,128)S(1)}, f32[32,2,8,128]{3,2,1,0:T(8,128)S(1)}) custom-call(f32[16,2,8,128]{3,2,1,0:T(8,128)S(1)} %collective-permute-done.5.refs_0_, f32[16,2,8,128]{3,2,1,0:T(8,128)S(1)} %collective-permute-done.6.refs_1_, ...), custom_call_target="tpu_custom_call", output_to_operand_aliasing={{1}: (5, {}), {2}: (6, {})} | custom-call | tf_op jit(solution)/shard_map/adjoint/pallas_call | solution.py:830
  40.3 0.1 collective-permute-start.12
  40.4 1.4 %collective-permute-start.11 = (f32[1,4224]{1,0:T(1,128)S(1)}, f32[1,4224]{1,0:T(1,128)S(1)}, u32[]{:S(2)}, u32[]{:S(2)}) collective-permute-start(f32[1,4224]{1,0:T(1,128)S(1)} %get-tuple-element.88), channel_id=1, source_target_pairs={{0,2},{1,3},{2,0},{3,1},{4,6},{5,7},{6,4},{7,5},{8,10},{9,11},{10,... | collective-permute-start | bytes 50696 | tf_op jit(solution)/shard_map/ppermute | solution.py:691
  41.8 0.3 collective-permute-start.10
  42.1 1.4 %collective-permute-done.12 = f32[1,4224]{1,0:T(1,128)S(1)} collective-permute-done((f32[1,4224]{1,0:T(1,128)S(1)}, f32[1,4224]{1,0:T(1,128)S(1)}, u32[]{:S(2)}, u32[]{:S(2)}) %collective-permute-start.12) | collective-permute-done | bytes 16928 | tf_op jit(solution)/shard_map/ppermute | solution.py:691
  43.5 0.6 %collective-permute-done.11 = f32[1,4224]{1,0:T(1,128)S(1)} collective-permute-done((f32[1,4224]{1,0:T(1,128)S(1)}, f32[1,4224]{1,0:T(1,128)S(1)}, u32[]{:S(2)}, u32[]{:S(2)}) %collective-permute-start.11) | collective-permute-done | bytes 16928 | tf_op jit(solution)/shard_map/ppermute | solution.py:691
  44.2 2.7 %collective-permute-start.15 = (f32[1,4224]{1,0:T(1,128)S(1)}, f32[1,4224]{1,0:T(1,128)S(1)}, u32[]{:S(2)}, u32[]{:S(2)}) collective-permute-start(f32[1,4224]{1,0:T(1,128)S(1)} %add_add_fusion.value), channel_id=1, source_target_pairs={{0,12},{1,13},{2,14},{3,15},{4,8},{5,9},{6,10},{7,11},{8,4},{9,5},... | collective-permute-start | bytes 50696 | tf_op jit(solution)/shard_map/ppermute | solution.py:691
  46.9 1.7 %collective-permute-start.14 = (f32[1,4224]{1,0:T(1,128)S(1)}, f32[1,4224]{1,0:T(1,128)S(1)}, u32[]{:S(2)}, u32[]{:S(2)}) collective-permute-start(f32[1,4224]{1,0:T(1,128)S(1)} %add_add_fusion.value), channel_id=1, source_target_pairs={{0,8},{1,9},{2,10},{3,11},{4,12},{5,13},{6,14},{7,15},{8,0},{9,1},... | collective-permute-start | bytes 50696 | tf_op jit(solution)/shard_map/ppermute | solution.py:691
  48.6 0.3 collective-permute-start.13
  48.9 0.9 %collective-permute-done.15.refs_2_ = f32[1,4224]{1,0:T(1,128)S(1)} collective-permute-done((f32[1,4224]{1,0:T(1,128)S(1)}, f32[1,4224]{1,0:T(1,128)S(1)}, u32[]{:S(2)}, u32[]{:S(2)}) %collective-permute-start.15) | collective-permute-done | bytes 16928 | tf_op jit(solution)/shard_map/ppermute | solution.py:691
  49.8 1.7 %collective-permute-done.14.refs_1_ = f32[1,4224]{1,0:T(1,128)S(1)} collective-permute-done((f32[1,4224]{1,0:T(1,128)S(1)}, f32[1,4224]{1,0:T(1,128)S(1)}, u32[]{:S(2)}, u32[]{:S(2)}) %collective-permute-start.14) | collective-permute-done | bytes 16928 | tf_op jit(solution)/shard_map/ppermute | solution.py:691
  51.6 0.8 %collective-permute-done.13.refs_0_ = f32[1,4224]{1,0:T(1,128)S(1)} collective-permute-done((f32[1,4224]{1,0:T(1,128)S(1)}, f32[1,4224]{1,0:T(1,128)S(1)}, u32[]{:S(2)}, u32[]{:S(2)}) %collective-permute-start.13) | collective-permute-done | bytes 16928 | tf_op jit(solution)/shard_map/ppermute | solution.py:691
  52.3 0.6 %total.1 = (f32[1,4096]{1,0:T(1,128)}, f32[1,1]{1,0:T(1,128)}) custom-call(f32[1,4224]{1,0:T(1,128)S(1)} %add_add_fusion.value, f32[1,4224]{1,0:T(1,128)S(1)} %collective-permute-done.13.refs_0_, f32[1,4224]{1,0:T(1,128)S(1)} %collective-permute-done.14.refs_1_, f32[1,4224]{1,0:T(1,128)S(1)} %collective-permute-done.15.refs_2_), custom_call_target="tpu_custom_call" | custom-call | tf_op jit(solution)/shard_map/total/pallas_call | solution.py:698
  (12 shorter events, 0.1 us)
Async XLA Ops:
  0.6 11.7 %copy-start.1 = (s32[4]{0:T(128)S(1)}, s32[4]{0:T(128)}, u32[]{:S(2)}) copy-start(s32[4]{0:T(128)} %ranking.1) | copy-start | bytes 52
  0.6 11.7 %copy-start = (f32[4096,128]{1,0:T(8,128)S(1)}, f32[4096,128]{1,0:T(8,128)}, u32[]{:S(2)}) copy-start(f32[4096,128]{1,0:T(8,128)} %profile.1) | copy-start | bytes 6291460
  2.2 17.5 %collective-permute-start = (f32[4,4,4,16,128]{4,3,2,1,0:T(8,128)S(1)}, f32[4,4,4,16,128]{4,3,2,1,0:T(8,128)S(1)}, u32[]{:S(2)}, u32[]{:S(2)}) collective-permute-start(f32[4,4,4,16,128]{4,3,2,1,0:T(8,128)S(1)} %get-tuple-element.47), channel_id=1, source_target_pairs={{4,0},{5,1},{6,2},{7,3},{0,4},{1,5},{2,6},{3,7},{12,8},{13,9},{14,... | collective-permute-start | bytes 1572872 | tf_op jit(solution)/shard_map/ppermute | solution.py:664
  5.3 14.4 %collective-permute-start.1 = (f32[4,4,4,16,128]{4,3,2,1,0:T(8,128)S(1)}, f32[4,4,4,16,128]{4,3,2,1,0:T(8,128)S(1)}, u32[]{:S(2)}, u32[]{:S(2)}) collective-permute-start(f32[4,4,4,16,128]{4,3,2,1,0:T(8,128)S(1)} %get-tuple-element.48), channel_id=1, source_target_pairs={{1,0},{0,1},{3,2},{2,3},{8,4},{9,5},{10,6},{11,7},{4,8},{5,9},{6,1... | collective-permute-start | bytes 1572872 | tf_op jit(solution)/shard_map/ppermute | solution.py:664
  7.7 12.0 %collective-permute-start.2 = (f32[16,2,8,128]{3,2,1,0:T(8,128)S(1)}, f32[16,2,8,128]{3,2,1,0:T(8,128)S(1)}, u32[]{:S(2)}, u32[]{:S(2)}) collective-permute-start(f32[16,2,8,128]{3,2,1,0:T(8,128)S(1)} %get-tuple-element.49), channel_id=1, source_target_pairs={{2,0},{3,1},{0,2},{1,3},{6,4},{7,5},{4,6},{5,7},{10,8},{11,9},{8,1... | collective-permute-start | bytes 393224 | tf_op jit(solution)/shard_map/ppermute | solution.py:670
  9.3 10.4 %collective-permute-start.3 = (f32[8,2,8,128]{3,2,1,0:T(8,128)S(1)}, f32[8,2,8,128]{3,2,1,0:T(8,128)S(1)}, u32[]{:S(2)}, u32[]{:S(2)}) collective-permute-start(f32[8,2,8,128]{3,2,1,0:T(8,128)S(1)} %get-tuple-element.50), channel_id=1, source_target_pairs={{6,0},{7,1},{4,2},{5,3},{2,4},{3,5},{0,6},{1,7},{14,8},{15,9},{12,... | collective-permute-start | bytes 196616 | tf_op jit(solution)/shard_map/ppermute | solution.py:670
  12.4 7.3 %collective-permute-start.4 = (f32[8,2,8,128]{3,2,1,0:T(8,128)S(1)}, f32[8,2,8,128]{3,2,1,0:T(8,128)S(1)}, u32[]{:S(2)}, u32[]{:S(2)}) collective-permute-start(f32[8,2,8,128]{3,2,1,0:T(8,128)S(1)} %get-tuple-element.51), channel_id=1, source_target_pairs={{1,0},{0,1},{3,2},{2,3},{10,4},{11,5},{8,6},{9,7},{6,8},{7,9},{4,1... | collective-permute-start | bytes 196616 | tf_op jit(solution)/shard_map/ppermute | solution.py:670
  26.0 8.0 %collective-permute-start.5 = (f32[16,2,8,128]{3,2,1,0:T(8,128)S(1)}, f32[16,2,8,128]{3,2,1,0:T(8,128)S(1)}, u32[]{:S(2)}, u32[]{:S(2)}) collective-permute-start(f32[16,2,8,128]{3,2,1,0:T(8,128)S(1)} %get-tuple-element.73), channel_id=1, source_target_pairs={{4,0},{5,1},{6,2},{7,3},{0,4},{1,5},{2,6},{3,7},{12,8},{13,9},{14,... | collective-permute-start | bytes 393224 | tf_op jit(solution)/shard_map/ppermute | solution.py:664
  28.7 5.2 %collective-permute-start.6 = (f32[16,2,8,128]{3,2,1,0:T(8,128)S(1)}, f32[16,2,8,128]{3,2,1,0:T(8,128)S(1)}, u32[]{:S(2)}, u32[]{:S(2)}) collective-permute-start(f32[16,2,8,128]{3,2,1,0:T(8,128)S(1)} %get-tuple-element.74), channel_id=1, source_target_pairs={{1,0},{0,1},{3,2},{2,3},{8,4},{9,5},{10,6},{11,7},{4,8},{5,9},{6,1... | collective-permute-start | bytes 393224 | tf_op jit(solution)/shard_map/ppermute | solution.py:664
  28.7 5.2 %collective-permute-start.7 = (f32[8,8,128]{2,1,0:T(8,128)S(1)}, f32[8,8,128]{2,1,0:T(8,128)S(1)}, u32[]{:S(2)}, u32[]{:S(2)}) collective-permute-start(f32[8,8,128]{2,1,0:T(8,128)S(1)} %get-tuple-element.75), channel_id=1, source_target_pairs={{2,0},{3,1},{0,2},{1,3},{6,4},{7,5},{4,6},{5,7},{10,8},{11,9},{8,1... | collective-permute-start | bytes 98312 | tf_op jit(solution)/shard_map/ppermute | solution.py:670
  29.3 4.7 %collective-permute-start.8 = (f32[4,8,128]{2,1,0:T(8,128)S(1)}, f32[4,8,128]{2,1,0:T(8,128)S(1)}, u32[]{:S(2)}, u32[]{:S(2)}) collective-permute-start(f32[4,8,128]{2,1,0:T(8,128)S(1)} %get-tuple-element.76), channel_id=1, source_target_pairs={{6,0},{7,1},{4,2},{5,3},{2,4},{3,5},{0,6},{1,7},{14,8},{15,9},{12,... | collective-permute-start | bytes 49160 | tf_op jit(solution)/shard_map/ppermute | solution.py:670
  32.2 1.7 %collective-permute-start.9 = (f32[4,8,128]{2,1,0:T(8,128)S(1)}, f32[4,8,128]{2,1,0:T(8,128)S(1)}, u32[]{:S(2)}, u32[]{:S(2)}) collective-permute-start(f32[4,8,128]{2,1,0:T(8,128)S(1)} %get-tuple-element.77), channel_id=1, source_target_pairs={{1,0},{0,1},{3,2},{2,3},{10,4},{11,5},{8,6},{9,7},{6,8},{7,9},{4,1... | collective-permute-start | bytes 49160 | tf_op jit(solution)/shard_map/ppermute | solution.py:670
  40.3 3.3 %collective-permute-start.12 = (f32[1,4224]{1,0:T(1,128)S(1)}, f32[1,4224]{1,0:T(1,128)S(1)}, u32[]{:S(2)}, u32[]{:S(2)}) collective-permute-start(f32[1,4224]{1,0:T(1,128)S(1)} %get-tuple-element.88), channel_id=1, source_target_pairs={{0,3},{1,2},{2,1},{3,0},{4,7},{5,6},{6,5},{7,4},{8,11},{9,10},{10,... | collective-permute-start | bytes 50696 | tf_op jit(solution)/shard_map/ppermute | solution.py:691
  40.4 3.7 %collective-permute-start.11 = (f32[1,4224]{1,0:T(1,128)S(1)}, f32[1,4224]{1,0:T(1,128)S(1)}, u32[]{:S(2)}, u32[]{:S(2)}) collective-permute-start(f32[1,4224]{1,0:T(1,128)S(1)} %get-tuple-element.88), channel_id=1, source_target_pairs={{0,2},{1,3},{2,0},{3,1},{4,6},{5,7},{6,4},{7,5},{8,10},{9,11},{10,... | collective-permute-start | bytes 50696 | tf_op jit(solution)/shard_map/ppermute | solution.py:691
  41.8 2.3 %collective-permute-start.10 = (f32[1,4224]{1,0:T(1,128)S(1)}, f32[1,4224]{1,0:T(1,128)S(1)}, u32[]{:S(2)}, u32[]{:S(2)}) collective-permute-start(f32[1,4224]{1,0:T(1,128)S(1)} %get-tuple-element.88), channel_id=1, source_target_pairs={{0,1},{1,0},{2,3},{3,2},{4,5},{5,4},{6,7},{7,6},{8,9},{9,8},{10,11... | collective-permute-start | bytes 50696 | tf_op jit(solution)/shard_map/ppermute | solution.py:691
  44.2 5.6 %collective-permute-start.15 = (f32[1,4224]{1,0:T(1,128)S(1)}, f32[1,4224]{1,0:T(1,128)S(1)}, u32[]{:S(2)}, u32[]{:S(2)}) collective-permute-start(f32[1,4224]{1,0:T(1,128)S(1)} %add_add_fusion.value), channel_id=1, source_target_pairs={{0,12},{1,13},{2,14},{3,15},{4,8},{5,9},{6,10},{7,11},{8,4},{9,5},... | collective-permute-start | bytes 50696 | tf_op jit(solution)/shard_map/ppermute | solution.py:691
  46.9 4.6 %collective-permute-start.14 = (f32[1,4224]{1,0:T(1,128)S(1)}, f32[1,4224]{1,0:T(1,128)S(1)}, u32[]{:S(2)}, u32[]{:S(2)}) collective-permute-start(f32[1,4224]{1,0:T(1,128)S(1)} %add_add_fusion.value), channel_id=1, source_target_pairs={{0,8},{1,9},{2,10},{3,11},{4,12},{5,13},{6,14},{7,15},{8,0},{9,1},... | collective-permute-start | bytes 50696 | tf_op jit(solution)/shard_map/ppermute | solution.py:691
  48.6 3.7 %collective-permute-start.13 = (f32[1,4224]{1,0:T(1,128)S(1)}, f32[1,4224]{1,0:T(1,128)S(1)}, u32[]{:S(2)}, u32[]{:S(2)}) collective-permute-start(f32[1,4224]{1,0:T(1,128)S(1)} %add_add_fusion.value), channel_id=1, source_target_pairs={{0,4},{1,5},{2,6},{3,7},{4,0},{5,1},{6,2},{7,3},{8,12},{9,13},{10,... | collective-permute-start | bytes 50696 | tf_op jit(solution)/shard_map/ppermute | solution.py:691

commit v7 on v6

--- a/solution.py
+++ b/solution.py
@@ -19,7 +19,7 @@
 GROUPS = LANES // WIDE
 INNER = EXT // GROUPS
 JOIN = ITERS // 2
-CHUNK = 2048
+CHUNK = 4096
 VMEM_LIMIT = 24 * 1024 * 1024
 
 
@@ -148,9 +148,9 @@
         ref[row, half] = value
 
 
-def source_kernel(kinds, tail_count, wells, controls, profile, own, monitor, ranking, *refs):
+def source_kernel(kinds, wells, controls, profile, own, *refs):
     n = len(kinds)
-    sources, tile, edges, (saved, weights, split), (acc, acc_low) = split_refs(refs, 1 + n, 5, 1, 3, 2)
+    sources, tile, edges, (saved, split), (acc, acc_low) = split_refs(refs, 1 + n, 5, 1, 2, 2)
     for x in range(OWN):
         for half in range(2):
             raw = [planes(own.at[field], x, half, OWN) for field in range(4)]
@@ -222,16 +222,9 @@
                     moved = lane_roll(mixed, WIDE * j + DEPTH)
                     packed = moved if packed is None else jnp.where(group == j, moved, packed)
                 sources[1 + number][i, half] = packed
-    sample = sub_id() // 2
-    tail = jnp.zeros((SUBLANES, LANES), jnp.float32)
-    for s in range(4):
-        tail = jnp.where(sample == s, jnp.where(ranking[s] < tail_count, 1.0, 0.0), tail)
     for x in range(OWN):
         for half in range(2):
             tile[0][DEPTH + x, half] += sources[0][DEPTH + x, half]
-            low = jnp.broadcast_to(monitor[pl.ds(half * OWN + x, 1), :], (SUBLANES, LANES))
-            high = jnp.broadcast_to(monitor[pl.ds((2 + half) * OWN + x, 1), :], (SUBLANES, LANES))
-            weights[x, half] = tail * jnp.where(upper, high, low)
     ahead(functools.partial(forward_step, masks, (*tile, sources[0]), sourced=True), tile[0], saved)
 
 
@@ -418,10 +411,10 @@
 
 def forward_kernel(kinds, tail_count, *refs):
     n = len(kinds)
-    ins, got_strips, sources, tile, (edges, saved, weights), outs, strips, out_strips, states = split_refs(
-        refs, 2, 3 * n, 1 + n, 5, 3, 5 + 5, 4 * n, 3 * n, n
+    ins, got_strips, sources, tile, (edges, saved), outs, strips, out_strips, states = split_refs(
+        refs, 4, 3 * n, 1 + n, 5, 2, 5 + 5, 4 * n, 3 * n, n
     )
-    got_a, got_b = ins
+    monitor, ranking, got_a, got_b = ins
     final, start_a, start_b, objective, start, *tile = outs
     odd = odd_tile()
     masks = Masks(kinds)
@@ -478,12 +471,19 @@
         saved,
     )
 
+    sample = sub_id() // 2
+    tail = jnp.zeros((SUBLANES, LANES), jnp.float32)
+    for s in range(4):
+        tail = jnp.where(sample == s, jnp.where(ranking[s] < tail_count, 1.0, 0.0), tail)
+    upper = sub_id() % 2 == 1
     sums = [jnp.zeros((SUBLANES, LANES), jnp.float32) for _ in range(4)]
     for x in range(OWN):
         for h in range(2):
             fresh = masks.outer_from(strip_states, DEPTH + x, h, state[DEPTH + x, h])
             final[pl.ds(h * OWN + x, SUBLANES, stride=2 * OWN), :] = fresh
-            weighted = weights[x, h] * fresh
+            low = jnp.broadcast_to(monitor[pl.ds(h * OWN + x, 1), :], (SUBLANES, LANES))
+            high = jnp.broadcast_to(monitor[pl.ds((2 + h) * OWN + x, 1), :], (SUBLANES, LANES))
+            weighted = tail * jnp.where(upper, high, low) * fresh
             start[DEPTH + x, h] = weighted * (1.0 / (tail_count * ITERS))
             sums[x % 4] = sums[x % 4] + weighted * fresh
     objective[...] = (sums[0] + sums[1]) + (sums[2] + sums[3])
@@ -762,28 +762,27 @@
     saved_shape = shape(JOIN, 4, SUBLANES, LANES)
     blocks = (1 + n) * EXT * layers
     *prepared, split = pl.pallas_call(
-        functools.partial(source_kernel, kinds, tail_count),
+        functools.partial(source_kernel, kinds),
         out_shape=(tile_shape,)
         + (strip_shape,) * n
         + (tile_shape,) * 5
         + (
             shape(4, INNER, 2, SUBLANES, LANES),
             saved_shape,
-            shape(OWN, 2, SUBLANES, LANES),
             jax.ShapeDtypeStruct((number, 2 * LANES), jnp.bfloat16),
         ),
-        in_specs=[vmem()] * 5 + [smem],
-        out_specs=(vmem(),) * (1 + n + 5 + 4),
+        in_specs=[vmem()] * 4,
+        out_specs=(vmem(),) * (1 + n + 5 + 3),
         scratch_shapes=[
             pltpu.VMEM((blocks, 2 * LANES), jnp.float32),
             pltpu.VMEM((blocks, LANES), jnp.float32),
         ],
         compiler_params=params(),
         name="source",
-    )(wells, controls, profile, own, monitor, ranking)
+    )(wells, controls, profile, own)
     got = [part.reshape(4, -1, LANES) for part in got]
     half_start = shape(DEPTH, 2, SUBLANES, LANES)
-    first_tile = 2 + 3 * n + 1 + n
+    first_tile = 4 + 3 * n + 1 + n
     final, start_a, start_b, objective, start, *rest = pl.pallas_call(
         functools.partial(forward_kernel, kinds, tail_count),
         out_shape=(
@@ -801,13 +800,13 @@
             shape(INNER // 4, SUBLANES, LANES),
         )
         * n,
-        in_specs=[vmem()] * (2 + 3 * n + 1 + n + 5 + 3),
+        in_specs=[vmem(), smem] + [vmem()] * (2 + 3 * n + 1 + n + 5 + 2),
         out_specs=(vmem(),) * (5 + 5 + 4 * n + 3 * n),
         scratch_shapes=[pltpu.VMEM((INNER, 2, SUBLANES, LANES), jnp.float32)] * n,
         input_output_aliases={first_tile + k: 5 + k for k in range(5)},
         compiler_params=params(),
         name="forward",
-    )(*got, *got_strips, *prepared)
+    )(monitor, ranking, *got, *got_strips, *prepared)
     tile, strip_coefs, start_strips = split_refs(rest, 5, 4 * n, 3 * n)
     got_start, got_start_strips = exchange((start_a, start_b), start_strips, kinds)
     *begun, final = pl.pallas_call(

time: 53.1 us -> 52.2 us (0.983)
  Pallas kernels: 24.3 us -> 21.5 us
  waiting for transfers between devices: 7.34 us -> 9.11 us
    ppermute x6, waiting for transfers between devices: 1.85 us -> 3.62 us  [exchange(): lax.ppermute(strip, AXES, swap_pairs(partner, kind, *counts))]
    pallas_call x1, Pallas kernels: 6.06 us -> 4.37 us  [local(): pl.pallas_call(functools.partial(source_kernel, kinds), out_shape=(tile_s...]
    pallas_call x1, Pallas kernels: 6.32 us -> 5.45 us  [local(): pl.pallas_call(functools.partial(adjoint_kernel, kinds, 0.5 / (tail_count...]
  transfers between devices with their start and end apart: 16 -> 16, of which waited for: 7 -> 7; matrix products, arithmetic and copies ran while one was open for 0% -> 0% of each run, Pallas kernels for 18% -> 15%
where the time goes in v7:
time: 52.2 us; the launch traced here: 52 us
  Pallas kernels  21.5 us (41%)
  starting transfers between devices  20.6 us (39%)
  waiting for transfers between devices  9.11 us (17%)
  between operations  0.73 us (1%)
    ppermute x6, starting transfers between devices, exchange(): lax.ppermute(strip, AXES, swap_pairs(partner, kind, *counts))  8.17 us
    ppermute x6, starting transfers between devices, total_over(): lax.ppermute(value, axes, [(i, i ^ b) for i in range(count)])  6.58 us
    pallas_call x1, Pallas kernels, local(): pl.pallas_call(functools.partial(forward_kernel, kinds, tail_count), out_...  6.17 us
    ppermute x4, starting transfers between devices, exchange(): lax.ppermute(tile, AXES, swap_pairs(partner, 'tile', *counts))  5.86 us
    ppermute x6, waiting for transfers between devices, total_over(): lax.ppermute(value, axes, [(i, i ^ b) for i in range(count)])  5.49 us
    pallas_call x1, Pallas kernels, local(): pl.pallas_call(functools.partial(adjoint_kernel, kinds, 0.5 / (tail_count...  5.45 us
    pallas_call x1, Pallas kernels, local(): pl.pallas_call(functools.partial(source_kernel, kinds), out_shape=(tile_s...  4.37 us
    ppermute x6, waiting for transfers between devices, exchange(): lax.ppermute(strip, AXES, swap_pairs(partner, kind, *counts))  3.62 us
  transfers between devices with their start and end apart: 16, of which 7 were waited for; matrix products, arithmetic and copies ran while one was open for 0% of the time, Pallas kernels for 15%

profile of v7, /device:TPU:0, one launch (start us, length us, event | category | flops | bytes accessed | tf_op | source)
XLA Modules:
  0.0 52.0 jit_solution(13787042555897448777)
XLA Ops:
  0.6 1.5 %rims.1 = (f32[4,4,4,16,128]{4,3,2,1,0:T(8,128)S(1)}, f32[4,4,4,16,128]{4,3,2,1,0:T(8,128)S(1)}) custom-call(f32[4,4,32,128]{3,2,1,0:T(8,128)} %initial.1, f32[4,4,32,128]{3,2,1,0:T(8,128)} %retard.1, f32[4,4,32,128]{3,2,1,0:T(8,128)} %velx.1, f32[4,4,32,128]{3,2,1,0:T(8,128)} %vely.1), custom_call_target="tpu_custom_call" | custom-call | tf_op jit(solution)/shard_map/rims/pallas_call | solution.py:727
  2.2 3.1 %collective-permute-start = (f32[4,4,4,16,128]{4,3,2,1,0:T(8,128)S(1)}, f32[4,4,4,16,128]{4,3,2,1,0:T(8,128)S(1)}, u32[]{:S(2)}, u32[]{:S(2)}) collective-permute-start(f32[4,4,4,16,128]{4,3,2,1,0:T(8,128)S(1)} %get-tuple-element.47), channel_id=1, source_target_pairs={{4,0},{5,1},{6,2},{7,3},{0,4},{1,5},{2,6},{3,7},{12,8},{13,9},{14,... | collective-permute-start | bytes 1572872 | tf_op jit(solution)/shard_map/ppermute | solution.py:664
  5.2 0.0 collective-permute-start.1
  5.2 2.4 %strips.1 = (f32[4,512,128]{2,1,0:T(8,128)S(1)}, f32[128,128]{1,0:T(8,128)S(1)}, f32[1,4096]{1,0:T(1,128)S(1)}, s32[1,4096]{1,0:T(1,128)S(1)}, f32[16,2,8,128]{3...) custom-call(f32[512,128]{1,0:T(8,128)} %bitcast.14, f32[512,128]{1,0:T(8,128)} %bitcast.15, ...), custom_call_target="tpu_custom_call" | custom-call | tf_op jit(solution)/shard_map/strips/pallas_call | solution.py:736
  7.7 1.6 %collective-permute-start.2 = (f32[16,2,8,128]{3,2,1,0:T(8,128)S(1)}, f32[16,2,8,128]{3,2,1,0:T(8,128)S(1)}, u32[]{:S(2)}, u32[]{:S(2)}) collective-permute-start(f32[16,2,8,128]{3,2,1,0:T(8,128)S(1)} %get-tuple-element.49), channel_id=1, source_target_pairs={{2,0},{3,1},{0,2},{1,3},{6,4},{7,5},{4,6},{5,7},{10,8},{11,9},{8,1... | collective-permute-start | bytes 393224 | tf_op jit(solution)/shard_map/ppermute | solution.py:670
  9.3 3.1 %collective-permute-start.3 = (f32[8,2,8,128]{3,2,1,0:T(8,128)S(1)}, f32[8,2,8,128]{3,2,1,0:T(8,128)S(1)}, u32[]{:S(2)}, u32[]{:S(2)}) collective-permute-start(f32[8,2,8,128]{3,2,1,0:T(8,128)S(1)} %get-tuple-element.50), channel_id=1, source_target_pairs={{6,0},{7,1},{4,2},{5,3},{2,4},{3,5},{0,6},{1,7},{14,8},{15,9},{12,... | collective-permute-start | bytes 196616 | tf_op jit(solution)/shard_map/ppermute | solution.py:670
  12.4 4.4 %source.1 = (f32[64,2,8,128]{3,2,1,0:T(8,128)S(1)}, f32[16,2,8,128]{3,2,1,0:T(8,128)S(1)}, f32[64,2,8,128]{3,2,1,0:T(8,128)S(1)}, f32[64,2,8,128]{3,2,1,0:T(8,12...) custom-call(s32[1,4096]{1,0:T(1,128)S(1)} %get-tuple-element.52.well, ...), custom_call_target="tpu_custom_call" | custom-call | tf_op jit(solution)/shard_map/source/pallas_call | solution.py:764
  16.8 2.9 %collective-permute-done.3.refs_5_ = f32[8,2,8,128]{3,2,1,0:T(8,128)S(1)} collective-permute-done((f32[8,2,8,128]{3,2,1,0:T(8,128)S(1)}, f32[8,2,8,128]{3,2,1,0:T(8,128)S(1)}, u32[]{:S(2)}, u32[]{:S(2)}) %collective-permute-start.3) | collective-permute-done | bytes 65568 | tf_op jit(solution)/shard_map/ppermute | solution.py:670
  19.7 0.0 collective-permute-done.2.refs_4_
  19.7 0.0 collective-permute-done
  19.7 0.0 collective-permute-done.1
  19.7 6.2 %forward.1 = (f32[512,128]{1,0:T(8,128)S(1)}, f32[16,2,8,128]{3,2,1,0:T(8,128)S(1)}, f32[16,2,8,128]{3,2,1,0:T(8,128)S(1)}, f32[8,128]{1,0:T(8,128)S(1)}, f32[64...) custom-call(f32[128,128]{1,0:T(8,128)S(1)} %get-tuple-element.46.ref, ...), custom_call_target="tpu_custom_call", output_to_operand_aliasing={{5}: (9, {}), {6}: (10, {}), {7}: (11, {}), {8}: (12, {}), ... | custom-call | tf_op jit(solution)/shard_map/forward/pallas_call | solution.py:786
  25.9 2.8 %collective-permute-start.5 = (f32[16,2,8,128]{3,2,1,0:T(8,128)S(1)}, f32[16,2,8,128]{3,2,1,0:T(8,128)S(1)}, u32[]{:S(2)}, u32[]{:S(2)}) collective-permute-start(f32[16,2,8,128]{3,2,1,0:T(8,128)S(1)} %get-tuple-element.71), channel_id=1, source_target_pairs={{4,0},{5,1},{6,2},{7,3},{0,4},{1,5},{2,6},{3,7},{12,8},{13,9},{14,... | collective-permute-start | bytes 393224 | tf_op jit(solution)/shard_map/ppermute | solution.py:664
  28.6 0.0 collective-permute-start.6
  28.6 0.5 %collective-permute-start.7 = (f32[8,8,128]{2,1,0:T(8,128)S(1)}, f32[8,8,128]{2,1,0:T(8,128)S(1)}, u32[]{:S(2)}, u32[]{:S(2)}) collective-permute-start(f32[8,8,128]{2,1,0:T(8,128)S(1)} %get-tuple-element.73), channel_id=1, source_target_pairs={{2,0},{3,1},{0,2},{1,3},{6,4},{7,5},{4,6},{5,7},{10,8},{11,9},{8,1... | collective-permute-start | bytes 98312 | tf_op jit(solution)/shard_map/ppermute | solution.py:670
  29.2 3.0 %collective-permute-start.8 = (f32[4,8,128]{2,1,0:T(8,128)S(1)}, f32[4,8,128]{2,1,0:T(8,128)S(1)}, u32[]{:S(2)}, u32[]{:S(2)}) collective-permute-start(f32[4,8,128]{2,1,0:T(8,128)S(1)} %get-tuple-element.74), channel_id=1, source_target_pairs={{6,0},{7,1},{4,2},{5,3},{2,4},{3,5},{0,6},{1,7},{14,8},{15,9},{12,... | collective-permute-start | bytes 49160 | tf_op jit(solution)/shard_map/ppermute | solution.py:670
  32.1 1.0 %ahead.1 = (f32[64,2,8,128]{3,2,1,0:T(8,128)S(1)}, f32[32,2,8,128]{3,2,1,0:T(8,128)S(1)}, f32[8,4,8,128]{3,2,1,0:T(8,128)S(1)}, f32[16,2,8,128]{3,2,1,0:T(8,128)S(1)}, f32[512,128]{1,0:T(8,128)}) custom-call(f32[64,2,8,128]{3,2,1,0:T(8,128)S(1)} %get-tuple-element.64.refs_0_, ...), custom_call_target="tpu_custom_call", output_to_operand_aliasing={{0}: (0, {})} | custom-call | tf_op jit(solution)/shard_map/ahead/pallas_call | solution.py:812
  33.1 0.7 %collective-permute-done.8.refs_3_ = f32[4,8,128]{2,1,0:T(8,128)S(1)} collective-permute-done((f32[4,8,128]{2,1,0:T(8,128)S(1)}, f32[4,8,128]{2,1,0:T(8,128)S(1)}, u32[]{:S(2)}, u32[]{:S(2)}) %collective-permute-start.8) | collective-permute-done | bytes 16416 | tf_op jit(solution)/shard_map/ppermute | solution.py:670
  33.8 0.0 collective-permute-done.9.refs_4_
  33.9 5.4 %adjoint.1 = (f32[1,4224]{1,0:T(1,128)S(1)}, f32[64,2,8,128]{3,2,1,0:T(8,128)S(1)}, f32[32,2,8,128]{3,2,1,0:T(8,128)S(1)}) custom-call(f32[16,2,8,128]{3,2,1,0:T(8,128)S(1)} %collective-permute-done.5.refs_0_, f32[16,2,8,128]{3,2,1,0:T(8,128)S(1)} %collective-permute-done.6.refs_1_, ...), custom_call_target="tpu_custom_call", output_to_operand_aliasing={{1}: (5, {}), {2}: (6, {})} | custom-call | tf_op jit(solution)/shard_map/adjoint/pallas_call | solution.py:829
  39.3 0.2 collective-permute-start.12
  39.5 1.4 %collective-permute-start.11 = (f32[1,4224]{1,0:T(1,128)S(1)}, f32[1,4224]{1,0:T(1,128)S(1)}, u32[]{:S(2)}, u32[]{:S(2)}) collective-permute-start(f32[1,4224]{1,0:T(1,128)S(1)} %get-tuple-element.86), channel_id=1, source_target_pairs={{0,2},{1,3},{2,0},{3,1},{4,6},{5,7},{6,4},{7,5},{8,10},{9,11},{10,... | collective-permute-start | bytes 50696 | tf_op jit(solution)/shard_map/ppermute | solution.py:691
  40.9 0.3 collective-permute-start.10
  41.2 1.5 %collective-permute-done.12 = f32[1,4224]{1,0:T(1,128)S(1)} collective-permute-done((f32[1,4224]{1,0:T(1,128)S(1)}, f32[1,4224]{1,0:T(1,128)S(1)}, u32[]{:S(2)}, u32[]{:S(2)}) %collective-permute-start.12) | collective-permute-done | bytes 16928 | tf_op jit(solution)/shard_map/ppermute | solution.py:691
  42.7 0.5 %collective-permute-done.11 = f32[1,4224]{1,0:T(1,128)S(1)} collective-permute-done((f32[1,4224]{1,0:T(1,128)S(1)}, f32[1,4224]{1,0:T(1,128)S(1)}, u32[]{:S(2)}, u32[]{:S(2)}) %collective-permute-start.11) | collective-permute-done | bytes 16928 | tf_op jit(solution)/shard_map/ppermute | solution.py:691
  43.3 2.7 %collective-permute-start.15 = (f32[1,4224]{1,0:T(1,128)S(1)}, f32[1,4224]{1,0:T(1,128)S(1)}, u32[]{:S(2)}, u32[]{:S(2)}) collective-permute-start(f32[1,4224]{1,0:T(1,128)S(1)} %add_add_fusion.value), channel_id=1, source_target_pairs={{0,12},{1,13},{2,14},{3,15},{4,8},{5,9},{6,10},{7,11},{8,4},{9,5},... | collective-permute-start | bytes 50696 | tf_op jit(solution)/shard_map/ppermute | solution.py:691
  46.0 1.7 %collective-permute-start.14 = (f32[1,4224]{1,0:T(1,128)S(1)}, f32[1,4224]{1,0:T(1,128)S(1)}, u32[]{:S(2)}, u32[]{:S(2)}) collective-permute-start(f32[1,4224]{1,0:T(1,128)S(1)} %add_add_fusion.value), channel_id=1, source_target_pairs={{0,8},{1,9},{2,10},{3,11},{4,12},{5,13},{6,14},{7,15},{8,0},{9,1},... | collective-permute-start | bytes 50696 | tf_op jit(solution)/shard_map/ppermute | solution.py:691
  47.7 0.3 collective-permute-start.13
  48.0 1.0 %collective-permute-done.15.refs_2_ = f32[1,4224]{1,0:T(1,128)S(1)} collective-permute-done((f32[1,4224]{1,0:T(1,128)S(1)}, f32[1,4224]{1,0:T(1,128)S(1)}, u32[]{:S(2)}, u32[]{:S(2)}) %collective-permute-start.15) | collective-permute-done | bytes 16928 | tf_op jit(solution)/shard_map/ppermute | solution.py:691
  48.9 1.7 %collective-permute-done.14.refs_1_ = f32[1,4224]{1,0:T(1,128)S(1)} collective-permute-done((f32[1,4224]{1,0:T(1,128)S(1)}, f32[1,4224]{1,0:T(1,128)S(1)}, u32[]{:S(2)}, u32[]{:S(2)}) %collective-permute-start.14) | collective-permute-done | bytes 16928 | tf_op jit(solution)/shard_map/ppermute | solution.py:691
  50.7 0.8 %collective-permute-done.13.refs_0_ = f32[1,4224]{1,0:T(1,128)S(1)} collective-permute-done((f32[1,4224]{1,0:T(1,128)S(1)}, f32[1,4224]{1,0:T(1,128)S(1)}, u32[]{:S(2)}, u32[]{:S(2)}) %collective-permute-start.13) | collective-permute-done | bytes 16928 | tf_op jit(solution)/shard_map/ppermute | solution.py:691
  51.4 0.6 %total.1 = (f32[1,4096]{1,0:T(1,128)}, f32[1,1]{1,0:T(1,128)}) custom-call(f32[1,4224]{1,0:T(1,128)S(1)} %add_add_fusion.value, f32[1,4224]{1,0:T(1,128)S(1)} %collective-permute-done.13.refs_0_, f32[1,4224]{1,0:T(1,128)S(1)} %collective-permute-done.14.refs_1_, f32[1,4224]{1,0:T(1,128)S(1)} %collective-permute-done.15.refs_2_), custom_call_target="tpu_custom_call" | custom-call | tf_op jit(solution)/shard_map/total/pallas_call | solution.py:698
  (12 shorter events, 0.1 us)
Async XLA Ops:
  0.6 11.8 %copy-start = (f32[4096,128]{1,0:T(8,128)S(1)}, f32[4096,128]{1,0:T(8,128)}, u32[]{:S(2)}) copy-start(f32[4096,128]{1,0:T(8,128)} %profile.1) | copy-start | bytes 6291460
  2.2 17.5 %collective-permute-start = (f32[4,4,4,16,128]{4,3,2,1,0:T(8,128)S(1)}, f32[4,4,4,16,128]{4,3,2,1,0:T(8,128)S(1)}, u32[]{:S(2)}, u32[]{:S(2)}) collective-permute-start(f32[4,4,4,16,128]{4,3,2,1,0:T(8,128)S(1)} %get-tuple-element.47), channel_id=1, source_target_pairs={{4,0},{5,1},{6,2},{7,3},{0,4},{1,5},{2,6},{3,7},{12,8},{13,9},{14,... | collective-permute-start | bytes 1572872 | tf_op jit(solution)/shard_map/ppermute | solution.py:664
  5.2 14.4 %collective-permute-start.1 = (f32[4,4,4,16,128]{4,3,2,1,0:T(8,128)S(1)}, f32[4,4,4,16,128]{4,3,2,1,0:T(8,128)S(1)}, u32[]{:S(2)}, u32[]{:S(2)}) collective-permute-start(f32[4,4,4,16,128]{4,3,2,1,0:T(8,128)S(1)} %get-tuple-element.48), channel_id=1, source_target_pairs={{1,0},{0,1},{3,2},{2,3},{8,4},{9,5},{10,6},{11,7},{4,8},{5,9},{6,1... | collective-permute-start | bytes 1572872 | tf_op jit(solution)/shard_map/ppermute | solution.py:664
  5.2 14.4 %copy-start.1 = (s32[4]{0:T(128)S(1)}, s32[4]{0:T(128)}, u32[]{:S(2)}) copy-start(s32[4]{0:T(128)} %refs_1_.1) | copy-start | bytes 52
  7.7 12.0 %collective-permute-start.2 = (f32[16,2,8,128]{3,2,1,0:T(8,128)S(1)}, f32[16,2,8,128]{3,2,1,0:T(8,128)S(1)}, u32[]{:S(2)}, u32[]{:S(2)}) collective-permute-start(f32[16,2,8,128]{3,2,1,0:T(8,128)S(1)} %get-tuple-element.49), channel_id=1, source_target_pairs={{2,0},{3,1},{0,2},{1,3},{6,4},{7,5},{4,6},{5,7},{10,8},{11,9},{8,1... | collective-permute-start | bytes 393224 | tf_op jit(solution)/shard_map/ppermute | solution.py:670
  9.3 10.4 %collective-permute-start.3 = (f32[8,2,8,128]{3,2,1,0:T(8,128)S(1)}, f32[8,2,8,128]{3,2,1,0:T(8,128)S(1)}, u32[]{:S(2)}, u32[]{:S(2)}) collective-permute-start(f32[8,2,8,128]{3,2,1,0:T(8,128)S(1)} %get-tuple-element.50), channel_id=1, source_target_pairs={{6,0},{7,1},{4,2},{5,3},{2,4},{3,5},{0,6},{1,7},{14,8},{15,9},{12,... | collective-permute-start | bytes 196616 | tf_op jit(solution)/shard_map/ppermute | solution.py:670
  12.4 7.3 %collective-permute-start.4 = (f32[8,2,8,128]{3,2,1,0:T(8,128)S(1)}, f32[8,2,8,128]{3,2,1,0:T(8,128)S(1)}, u32[]{:S(2)}, u32[]{:S(2)}) collective-permute-start(f32[8,2,8,128]{3,2,1,0:T(8,128)S(1)} %get-tuple-element.51), channel_id=1, source_target_pairs={{1,0},{0,1},{3,2},{2,3},{10,4},{11,5},{8,6},{9,7},{6,8},{7,9},{4,1... | collective-permute-start | bytes 196616 | tf_op jit(solution)/shard_map/ppermute | solution.py:670
  25.9 8.0 %collective-permute-start.5 = (f32[16,2,8,128]{3,2,1,0:T(8,128)S(1)}, f32[16,2,8,128]{3,2,1,0:T(8,128)S(1)}, u32[]{:S(2)}, u32[]{:S(2)}) collective-permute-start(f32[16,2,8,128]{3,2,1,0:T(8,128)S(1)} %get-tuple-element.71), channel_id=1, source_target_pairs={{4,0},{5,1},{6,2},{7,3},{0,4},{1,5},{2,6},{3,7},{12,8},{13,9},{14,... | collective-permute-start | bytes 393224 | tf_op jit(solution)/shard_map/ppermute | solution.py:664
  28.6 5.2 %collective-permute-start.6 = (f32[16,2,8,128]{3,2,1,0:T(8,128)S(1)}, f32[16,2,8,128]{3,2,1,0:T(8,128)S(1)}, u32[]{:S(2)}, u32[]{:S(2)}) collective-permute-start(f32[16,2,8,128]{3,2,1,0:T(8,128)S(1)} %get-tuple-element.72), channel_id=1, source_target_pairs={{1,0},{0,1},{3,2},{2,3},{8,4},{9,5},{10,6},{11,7},{4,8},{5,9},{6,1... | collective-permute-start | bytes 393224 | tf_op jit(solution)/shard_map/ppermute | solution.py:664
  28.6 5.2 %collective-permute-start.7 = (f32[8,8,128]{2,1,0:T(8,128)S(1)}, f32[8,8,128]{2,1,0:T(8,128)S(1)}, u32[]{:S(2)}, u32[]{:S(2)}) collective-permute-start(f32[8,8,128]{2,1,0:T(8,128)S(1)} %get-tuple-element.73), channel_id=1, source_target_pairs={{2,0},{3,1},{0,2},{1,3},{6,4},{7,5},{4,6},{5,7},{10,8},{11,9},{8,1... | collective-permute-start | bytes 98312 | tf_op jit(solution)/shard_map/ppermute | solution.py:670
  29.2 4.7 %collective-permute-start.8 = (f32[4,8,128]{2,1,0:T(8,128)S(1)}, f32[4,8,128]{2,1,0:T(8,128)S(1)}, u32[]{:S(2)}, u32[]{:S(2)}) collective-permute-start(f32[4,8,128]{2,1,0:T(8,128)S(1)} %get-tuple-element.74), channel_id=1, source_target_pairs={{6,0},{7,1},{4,2},{5,3},{2,4},{3,5},{0,6},{1,7},{14,8},{15,9},{12,... | collective-permute-start | bytes 49160 | tf_op jit(solution)/shard_map/ppermute | solution.py:670
  32.1 1.7 %collective-permute-start.9 = (f32[4,8,128]{2,1,0:T(8,128)S(1)}, f32[4,8,128]{2,1,0:T(8,128)S(1)}, u32[]{:S(2)}, u32[]{:S(2)}) collective-permute-start(f32[4,8,128]{2,1,0:T(8,128)S(1)} %get-tuple-element.75), channel_id=1, source_target_pairs={{1,0},{0,1},{3,2},{2,3},{10,4},{11,5},{8,6},{9,7},{6,8},{7,9},{4,1... | collective-permute-start | bytes 49160 | tf_op jit(solution)/shard_map/ppermute | solution.py:670
  39.3 3.4 %collective-permute-start.12 = (f32[1,4224]{1,0:T(1,128)S(1)}, f32[1,4224]{1,0:T(1,128)S(1)}, u32[]{:S(2)}, u32[]{:S(2)}) collective-permute-start(f32[1,4224]{1,0:T(1,128)S(1)} %get-tuple-element.86), channel_id=1, source_target_pairs={{0,3},{1,2},{2,1},{3,0},{4,7},{5,6},{6,5},{7,4},{8,11},{9,10},{10,... | collective-permute-start | bytes 50696 | tf_op jit(solution)/shard_map/ppermute | solution.py:691
  39.5 3.7 %collective-permute-start.11 = (f32[1,4224]{1,0:T(1,128)S(1)}, f32[1,4224]{1,0:T(1,128)S(1)}, u32[]{:S(2)}, u32[]{:S(2)}) collective-permute-start(f32[1,4224]{1,0:T(1,128)S(1)} %get-tuple-element.86), channel_id=1, source_target_pairs={{0,2},{1,3},{2,0},{3,1},{4,6},{5,7},{6,4},{7,5},{8,10},{9,11},{10,... | collective-permute-start | bytes 50696 | tf_op jit(solution)/shard_map/ppermute | solution.py:691
  40.9 2.4 %collective-permute-start.10 = (f32[1,4224]{1,0:T(1,128)S(1)}, f32[1,4224]{1,0:T(1,128)S(1)}, u32[]{:S(2)}, u32[]{:S(2)}) collective-permute-start(f32[1,4224]{1,0:T(1,128)S(1)} %get-tuple-element.86), channel_id=1, source_target_pairs={{0,1},{1,0},{2,3},{3,2},{4,5},{5,4},{6,7},{7,6},{8,9},{9,8},{10,11... | collective-permute-start | bytes 50696 | tf_op jit(solution)/shard_map/ppermute | solution.py:691
  43.3 5.6 %collective-permute-start.15 = (f32[1,4224]{1,0:T(1,128)S(1)}, f32[1,4224]{1,0:T(1,128)S(1)}, u32[]{:S(2)}, u32[]{:S(2)}) collective-permute-start(f32[1,4224]{1,0:T(1,128)S(1)} %add_add_fusion.value), channel_id=1, source_target_pairs={{0,12},{1,13},{2,14},{3,15},{4,8},{5,9},{6,10},{7,11},{8,4},{9,5},... | collective-permute-start | bytes 50696 | tf_op jit(solution)/shard_map/ppermute | solution.py:691
  46.0 4.6 %collective-permute-start.14 = (f32[1,4224]{1,0:T(1,128)S(1)}, f32[1,4224]{1,0:T(1,128)S(1)}, u32[]{:S(2)}, u32[]{:S(2)}) collective-permute-start(f32[1,4224]{1,0:T(1,128)S(1)} %add_add_fusion.value), channel_id=1, source_target_pairs={{0,8},{1,9},{2,10},{3,11},{4,12},{5,13},{6,14},{7,15},{8,0},{9,1},... | collective-permute-start | bytes 50696 | tf_op jit(solution)/shard_map/ppermute | solution.py:691
  47.7 3.7 %collective-permute-start.13 = (f32[1,4224]{1,0:T(1,128)S(1)}, f32[1,4224]{1,0:T(1,128)S(1)}, u32[]{:S(2)}, u32[]{:S(2)}) collective-permute-start(f32[1,4224]{1,0:T(1,128)S(1)} %add_add_fusion.value), channel_id=1, source_target_pairs={{0,4},{1,5},{2,6},{3,7},{4,0},{5,1},{6,2},{7,3},{8,12},{9,13},{10,... | collective-permute-start | bytes 50696 | tf_op jit(solution)/shard_map/ppermute | solution.py:691

commit v8 on v7

--- a/solution.py
+++ b/solution.py
@@ -132,6 +132,13 @@
                     out[i, half] = packed
 
 
+def over_chunks(number, chunk):
+    if number == CHUNK:
+        chunk(0, 0)
+    else:
+        lax.fori_loop(0, number // CHUNK, chunk, 0)
+
+
 def coefficients(retard, velx, vely):
     spread = KAPPA * retard
     from_x = retard * velx + spread
@@ -182,7 +189,7 @@
     acc_low[...] = jnp.zeros_like(acc_low)
 
     def chunk(c, carry):
-        span = pl.ds(pl.multiple_of(c * CHUNK, CHUNK), CHUNK)
+        span = pl.ds(c * CHUNK if isinstance(c, int) else pl.multiple_of(c * CHUNK, CHUNK), CHUNK)
         part = profile[span, :]
         high = part.astype(jnp.bfloat16)
         low = (part - high.astype(jnp.float32)).astype(jnp.bfloat16)
@@ -197,7 +204,7 @@
         acc_low[...] += jnp.dot(hot_low, high, preferred_element_type=jnp.float32)
         return carry
 
-    lax.fori_loop(0, wells.shape[1] // CHUNK, chunk, 0)
+    over_chunks(wells.shape[1], chunk)
     acc_low[...] += acc[:, :LANES] + acc[:, LANES:]
     upper = sub_id() % 2 == 1
     group = lane_id() // WIDE
@@ -547,6 +554,8 @@
     out, state, total = outs
     odd = odd_tile()
     masks = Masks(kinds)
+    whole = jnp.sum(jnp.sum(objective[...], axis=0, keepdims=True), axis=1, keepdims=True)
+    out[:, wells.shape[1] :] = jnp.broadcast_to(whole * scale, (1, LANES))
     at = places(odd)[2:]
     for part, first in zip(parts, at):
         for x in range(DEPTH):
@@ -608,7 +617,7 @@
     controls = wells.shape[1]
 
     def chunk(c, carry):
-        span = pl.ds(pl.multiple_of(c * CHUNK, CHUNK), CHUNK)
+        span = pl.ds(c * CHUNK if isinstance(c, int) else pl.multiple_of(c * CHUNK, CHUNK), CHUNK)
         share_high, share_low = profile[span, :LANES], profile[span, LANES:]
         first = lax.dot_general(both, share_high, contract, preferred_element_type=jnp.float32)
         second = lax.dot_general(high, share_low, contract, preferred_element_type=jnp.float32)
@@ -617,9 +626,7 @@
         out[:, span] = jnp.sum(chosen, axis=0, keepdims=True)
         return carry
 
-    lax.fori_loop(0, controls // CHUNK, chunk, 0)
-    whole = jnp.sum(jnp.sum(objective[...], axis=0, keepdims=True), axis=1, keepdims=True)
-    out[:, controls:] = jnp.broadcast_to(whole * scale, (1, LANES))
+    over_chunks(controls, chunk)
 
 
 def shape(*dims):

time: 52.2 us -> 52.2 us (level)
  no operation moved by 1% of the time
where the time goes in v8:
time: 52.2 us; the launch traced here: 52.1 us
  Pallas kernels  21.6 us (41%)
  starting transfers between devices  20.6 us (39%)
  waiting for transfers between devices  9.11 us (17%)
  between operations  0.73 us (1%)
    ppermute x6, starting transfers between devices, exchange(): lax.ppermute(strip, AXES, swap_pairs(partner, kind, *counts))  8.17 us
    ppermute x6, starting transfers between devices, total_over(): lax.ppermute(value, axes, [(i, i ^ b) for i in range(count)])  6.58 us
    pallas_call x1, Pallas kernels, local(): pl.pallas_call(functools.partial(forward_kernel, kinds, tail_count), out_...  6.17 us
    ppermute x4, starting transfers between devices, exchange(): lax.ppermute(tile, AXES, swap_pairs(partner, 'tile', *counts))  5.86 us
    ppermute x6, waiting for transfers between devices, total_over(): lax.ppermute(value, axes, [(i, i ^ b) for i in range(count)])  5.49 us
    pallas_call x1, Pallas kernels, local(): pl.pallas_call(functools.partial(adjoint_kernel, kinds, 0.5 / (tail_count...  5.48 us
    pallas_call x1, Pallas kernels, local(): pl.pallas_call(functools.partial(source_kernel, kinds), out_shape=(tile_s...  4.37 us
    ppermute x6, waiting for transfers between devices, exchange(): lax.ppermute(strip, AXES, swap_pairs(partner, kind, *counts))  3.62 us
  transfers between devices with their start and end apart: 16, of which 7 were waited for; matrix products, arithmetic and copies ran while one was open for 0% of the time, Pallas kernels for 15%

profile of v8, /device:TPU:0, one launch (start us, length us, event | category | flops | bytes accessed | tf_op | source)
XLA Modules:
  0.0 52.1 jit_solution(4264782271772588425)
XLA Ops:
  0.6 1.5 %rims.1 = (f32[4,4,4,16,128]{4,3,2,1,0:T(8,128)S(1)}, f32[4,4,4,16,128]{4,3,2,1,0:T(8,128)S(1)}) custom-call(f32[4,4,32,128]{3,2,1,0:T(8,128)} %initial.1, f32[4,4,32,128]{3,2,1,0:T(8,128)} %retard.1, f32[4,4,32,128]{3,2,1,0:T(8,128)} %velx.1, f32[4,4,32,128]{3,2,1,0:T(8,128)} %vely.1), custom_call_target="tpu_custom_call" | custom-call | tf_op jit(solution)/shard_map/rims/pallas_call | solution.py:734
  2.2 3.1 %collective-permute-start = (f32[4,4,4,16,128]{4,3,2,1,0:T(8,128)S(1)}, f32[4,4,4,16,128]{4,3,2,1,0:T(8,128)S(1)}, u32[]{:S(2)}, u32[]{:S(2)}) collective-permute-start(f32[4,4,4,16,128]{4,3,2,1,0:T(8,128)S(1)} %get-tuple-element.47), channel_id=1, source_target_pairs={{4,0},{5,1},{6,2},{7,3},{0,4},{1,5},{2,6},{3,7},{12,8},{13,9},{14,... | collective-permute-start | bytes 1572872 | tf_op jit(solution)/shard_map/ppermute | solution.py:671
  5.2 0.0 collective-permute-start.1
  5.2 2.4 %strips.1 = (f32[4,512,128]{2,1,0:T(8,128)S(1)}, f32[128,128]{1,0:T(8,128)S(1)}, f32[1,4096]{1,0:T(1,128)S(1)}, s32[1,4096]{1,0:T(1,128)S(1)}, f32[16,2,8,128]{3...) custom-call(f32[512,128]{1,0:T(8,128)} %bitcast.14, f32[512,128]{1,0:T(8,128)} %bitcast.15, ...), custom_call_target="tpu_custom_call" | custom-call | tf_op jit(solution)/shard_map/strips/pallas_call | solution.py:743
  7.7 1.6 %collective-permute-start.2 = (f32[16,2,8,128]{3,2,1,0:T(8,128)S(1)}, f32[16,2,8,128]{3,2,1,0:T(8,128)S(1)}, u32[]{:S(2)}, u32[]{:S(2)}) collective-permute-start(f32[16,2,8,128]{3,2,1,0:T(8,128)S(1)} %get-tuple-element.49), channel_id=1, source_target_pairs={{2,0},{3,1},{0,2},{1,3},{6,4},{7,5},{4,6},{5,7},{10,8},{11,9},{8,1... | collective-permute-start | bytes 393224 | tf_op jit(solution)/shard_map/ppermute | solution.py:677
  9.3 3.1 %collective-permute-start.3 = (f32[8,2,8,128]{3,2,1,0:T(8,128)S(1)}, f32[8,2,8,128]{3,2,1,0:T(8,128)S(1)}, u32[]{:S(2)}, u32[]{:S(2)}) collective-permute-start(f32[8,2,8,128]{3,2,1,0:T(8,128)S(1)} %get-tuple-element.50), channel_id=1, source_target_pairs={{6,0},{7,1},{4,2},{5,3},{2,4},{3,5},{0,6},{1,7},{14,8},{15,9},{12,... | collective-permute-start | bytes 196616 | tf_op jit(solution)/shard_map/ppermute | solution.py:677
  12.4 4.4 %source.1 = (f32[64,2,8,128]{3,2,1,0:T(8,128)S(1)}, f32[16,2,8,128]{3,2,1,0:T(8,128)S(1)}, f32[64,2,8,128]{3,2,1,0:T(8,128)S(1)}, f32[64,2,8,128]{3,2,1,0:T(8,12...) custom-call(s32[1,4096]{1,0:T(1,128)S(1)} %get-tuple-element.52.well, ...), custom_call_target="tpu_custom_call" | custom-call | tf_op jit(solution)/shard_map/source/pallas_call | solution.py:771
  16.8 2.9 %collective-permute-done.3.refs_5_ = f32[8,2,8,128]{3,2,1,0:T(8,128)S(1)} collective-permute-done((f32[8,2,8,128]{3,2,1,0:T(8,128)S(1)}, f32[8,2,8,128]{3,2,1,0:T(8,128)S(1)}, u32[]{:S(2)}, u32[]{:S(2)}) %collective-permute-start.3) | collective-permute-done | bytes 65568 | tf_op jit(solution)/shard_map/ppermute | solution.py:677
  19.7 0.0 collective-permute-done.4.refs_6_
  19.7 0.0 collective-permute-done.2.refs_4_
  19.7 0.0 collective-permute-done
  19.7 0.0 collective-permute-done.1
  19.7 6.2 %forward.1 = (f32[512,128]{1,0:T(8,128)S(1)}, f32[16,2,8,128]{3,2,1,0:T(8,128)S(1)}, f32[16,2,8,128]{3,2,1,0:T(8,128)S(1)}, f32[8,128]{1,0:T(8,128)S(1)}, f32[64...) custom-call(f32[128,128]{1,0:T(8,128)S(1)} %get-tuple-element.46.ref, ...), custom_call_target="tpu_custom_call", output_to_operand_aliasing={{5}: (9, {}), {6}: (10, {}), {7}: (11, {}), {8}: (12, {}), ... | custom-call | tf_op jit(solution)/shard_map/forward/pallas_call | solution.py:793
  25.9 2.8 %collective-permute-start.5 = (f32[16,2,8,128]{3,2,1,0:T(8,128)S(1)}, f32[16,2,8,128]{3,2,1,0:T(8,128)S(1)}, u32[]{:S(2)}, u32[]{:S(2)}) collective-permute-start(f32[16,2,8,128]{3,2,1,0:T(8,128)S(1)} %get-tuple-element.71), channel_id=1, source_target_pairs={{4,0},{5,1},{6,2},{7,3},{0,4},{1,5},{2,6},{3,7},{12,8},{13,9},{14,... | collective-permute-start | bytes 393224 | tf_op jit(solution)/shard_map/ppermute | solution.py:671
  28.6 0.0 collective-permute-start.6
  28.6 0.5 %collective-permute-start.7 = (f32[8,8,128]{2,1,0:T(8,128)S(1)}, f32[8,8,128]{2,1,0:T(8,128)S(1)}, u32[]{:S(2)}, u32[]{:S(2)}) collective-permute-start(f32[8,8,128]{2,1,0:T(8,128)S(1)} %get-tuple-element.73), channel_id=1, source_target_pairs={{2,0},{3,1},{0,2},{1,3},{6,4},{7,5},{4,6},{5,7},{10,8},{11,9},{8,1... | collective-permute-start | bytes 98312 | tf_op jit(solution)/shard_map/ppermute | solution.py:677
  29.2 3.0 %collective-permute-start.8 = (f32[4,8,128]{2,1,0:T(8,128)S(1)}, f32[4,8,128]{2,1,0:T(8,128)S(1)}, u32[]{:S(2)}, u32[]{:S(2)}) collective-permute-start(f32[4,8,128]{2,1,0:T(8,128)S(1)} %get-tuple-element.74), channel_id=1, source_target_pairs={{6,0},{7,1},{4,2},{5,3},{2,4},{3,5},{0,6},{1,7},{14,8},{15,9},{12,... | collective-permute-start | bytes 49160 | tf_op jit(solution)/shard_map/ppermute | solution.py:677
  32.1 1.0 %ahead.1 = (f32[64,2,8,128]{3,2,1,0:T(8,128)S(1)}, f32[32,2,8,128]{3,2,1,0:T(8,128)S(1)}, f32[8,4,8,128]{3,2,1,0:T(8,128)S(1)}, f32[16,2,8,128]{3,2,1,0:T(8,128)S(1)}, f32[512,128]{1,0:T(8,128)}) custom-call(f32[64,2,8,128]{3,2,1,0:T(8,128)S(1)} %get-tuple-element.64.refs_0_, ...), custom_call_target="tpu_custom_call", output_to_operand_aliasing={{0}: (0, {})} | custom-call | tf_op jit(solution)/shard_map/ahead/pallas_call | solution.py:819
  33.1 0.7 %collective-permute-done.8.refs_3_ = f32[4,8,128]{2,1,0:T(8,128)S(1)} collective-permute-done((f32[4,8,128]{2,1,0:T(8,128)S(1)}, f32[4,8,128]{2,1,0:T(8,128)S(1)}, u32[]{:S(2)}, u32[]{:S(2)}) %collective-permute-start.8) | collective-permute-done | bytes 16416 | tf_op jit(solution)/shard_map/ppermute | solution.py:677
  33.9 5.5 %adjoint.1 = (f32[1,4224]{1,0:T(1,128)S(1)}, f32[64,2,8,128]{3,2,1,0:T(8,128)S(1)}, f32[32,2,8,128]{3,2,1,0:T(8,128)S(1)}) custom-call(f32[16,2,8,128]{3,2,1,0:T(8,128)S(1)} %collective-permute-done.5.refs_0_, f32[16,2,8,128]{3,2,1,0:T(8,128)S(1)} %collective-permute-done.6.refs_1_, ...), custom_call_target="tpu_custom_call", output_to_operand_aliasing={{1}: (5, {}), {2}: (6, {})} | custom-call | tf_op jit(solution)/shard_map/adjoint/pallas_call | solution.py:836
  39.4 0.2 collective-permute-start.12
  39.6 1.4 %collective-permute-start.11 = (f32[1,4224]{1,0:T(1,128)S(1)}, f32[1,4224]{1,0:T(1,128)S(1)}, u32[]{:S(2)}, u32[]{:S(2)}) collective-permute-start(f32[1,4224]{1,0:T(1,128)S(1)} %get-tuple-element.86), channel_id=1, source_target_pairs={{0,2},{1,3},{2,0},{3,1},{4,6},{5,7},{6,4},{7,5},{8,10},{9,11},{10,... | collective-permute-start | bytes 50696 | tf_op jit(solution)/shard_map/ppermute | solution.py:698
  41.0 0.3 collective-permute-start.10
  41.3 1.5 %collective-permute-done.12 = f32[1,4224]{1,0:T(1,128)S(1)} collective-permute-done((f32[1,4224]{1,0:T(1,128)S(1)}, f32[1,4224]{1,0:T(1,128)S(1)}, u32[]{:S(2)}, u32[]{:S(2)}) %collective-permute-start.12) | collective-permute-done | bytes 16928 | tf_op jit(solution)/shard_map/ppermute | solution.py:698
  42.8 0.5 %collective-permute-done.11 = f32[1,4224]{1,0:T(1,128)S(1)} collective-permute-done((f32[1,4224]{1,0:T(1,128)S(1)}, f32[1,4224]{1,0:T(1,128)S(1)}, u32[]{:S(2)}, u32[]{:S(2)}) %collective-permute-start.11) | collective-permute-done | bytes 16928 | tf_op jit(solution)/shard_map/ppermute | solution.py:698
  43.3 2.7 %collective-permute-start.15 = (f32[1,4224]{1,0:T(1,128)S(1)}, f32[1,4224]{1,0:T(1,128)S(1)}, u32[]{:S(2)}, u32[]{:S(2)}) collective-permute-start(f32[1,4224]{1,0:T(1,128)S(1)} %add_add_fusion.value), channel_id=1, source_target_pairs={{0,12},{1,13},{2,14},{3,15},{4,8},{5,9},{6,10},{7,11},{8,4},{9,5},... | collective-permute-start | bytes 50696 | tf_op jit(solution)/shard_map/ppermute | solution.py:698
  46.0 1.7 %collective-permute-start.14 = (f32[1,4224]{1,0:T(1,128)S(1)}, f32[1,4224]{1,0:T(1,128)S(1)}, u32[]{:S(2)}, u32[]{:S(2)}) collective-permute-start(f32[1,4224]{1,0:T(1,128)S(1)} %add_add_fusion.value), channel_id=1, source_target_pairs={{0,8},{1,9},{2,10},{3,11},{4,12},{5,13},{6,14},{7,15},{8,0},{9,1},... | collective-permute-start | bytes 50696 | tf_op jit(solution)/shard_map/ppermute | solution.py:698
  47.7 0.3 collective-permute-start.13
  48.0 1.0 %collective-permute-done.15.refs_2_ = f32[1,4224]{1,0:T(1,128)S(1)} collective-permute-done((f32[1,4224]{1,0:T(1,128)S(1)}, f32[1,4224]{1,0:T(1,128)S(1)}, u32[]{:S(2)}, u32[]{:S(2)}) %collective-permute-start.15) | collective-permute-done | bytes 16928 | tf_op jit(solution)/shard_map/ppermute | solution.py:698
  48.9 1.7 %collective-permute-done.14.refs_1_ = f32[1,4224]{1,0:T(1,128)S(1)} collective-permute-done((f32[1,4224]{1,0:T(1,128)S(1)}, f32[1,4224]{1,0:T(1,128)S(1)}, u32[]{:S(2)}, u32[]{:S(2)}) %collective-permute-start.14) | collective-permute-done | bytes 16928 | tf_op jit(solution)/shard_map/ppermute | solution.py:698
  50.7 0.8 %collective-permute-done.13.refs_0_ = f32[1,4224]{1,0:T(1,128)S(1)} collective-permute-done((f32[1,4224]{1,0:T(1,128)S(1)}, f32[1,4224]{1,0:T(1,128)S(1)}, u32[]{:S(2)}, u32[]{:S(2)}) %collective-permute-start.13) | collective-permute-done | bytes 16928 | tf_op jit(solution)/shard_map/ppermute | solution.py:698
  51.5 0.6 %total.1 = (f32[1,4096]{1,0:T(1,128)}, f32[1,1]{1,0:T(1,128)}) custom-call(f32[1,4224]{1,0:T(1,128)S(1)} %add_add_fusion.value, f32[1,4224]{1,0:T(1,128)S(1)} %collective-permute-done.13.refs_0_, f32[1,4224]{1,0:T(1,128)S(1)} %collective-permute-done.14.refs_1_, f32[1,4224]{1,0:T(1,128)S(1)} %collective-permute-done.15.refs_2_), custom_call_target="tpu_custom_call" | custom-call | tf_op jit(solution)/shard_map/total/pallas_call | solution.py:705
  (12 shorter events, 0.1 us)
Async XLA Ops:
  0.6 11.8 %copy-start = (f32[4096,128]{1,0:T(8,128)S(1)}, f32[4096,128]{1,0:T(8,128)}, u32[]{:S(2)}) copy-start(f32[4096,128]{1,0:T(8,128)} %profile.1) | copy-start | bytes 6291460
  2.2 17.5 %collective-permute-start = (f32[4,4,4,16,128]{4,3,2,1,0:T(8,128)S(1)}, f32[4,4,4,16,128]{4,3,2,1,0:T(8,128)S(1)}, u32[]{:S(2)}, u32[]{:S(2)}) collective-permute-start(f32[4,4,4,16,128]{4,3,2,1,0:T(8,128)S(1)} %get-tuple-element.47), channel_id=1, source_target_pairs={{4,0},{5,1},{6,2},{7,3},{0,4},{1,5},{2,6},{3,7},{12,8},{13,9},{14,... | collective-permute-start | bytes 1572872 | tf_op jit(solution)/shard_map/ppermute | solution.py:671
  5.2 14.4 %collective-permute-start.1 = (f32[4,4,4,16,128]{4,3,2,1,0:T(8,128)S(1)}, f32[4,4,4,16,128]{4,3,2,1,0:T(8,128)S(1)}, u32[]{:S(2)}, u32[]{:S(2)}) collective-permute-start(f32[4,4,4,16,128]{4,3,2,1,0:T(8,128)S(1)} %get-tuple-element.48), channel_id=1, source_target_pairs={{1,0},{0,1},{3,2},{2,3},{8,4},{9,5},{10,6},{11,7},{4,8},{5,9},{6,1... | collective-permute-start | bytes 1572872 | tf_op jit(solution)/shard_map/ppermute | solution.py:671
  5.2 14.4 %copy-start.1 = (s32[4]{0:T(128)S(1)}, s32[4]{0:T(128)}, u32[]{:S(2)}) copy-start(s32[4]{0:T(128)} %refs_1_.1) | copy-start | bytes 52
  7.7 12.0 %collective-permute-start.2 = (f32[16,2,8,128]{3,2,1,0:T(8,128)S(1)}, f32[16,2,8,128]{3,2,1,0:T(8,128)S(1)}, u32[]{:S(2)}, u32[]{:S(2)}) collective-permute-start(f32[16,2,8,128]{3,2,1,0:T(8,128)S(1)} %get-tuple-element.49), channel_id=1, source_target_pairs={{2,0},{3,1},{0,2},{1,3},{6,4},{7,5},{4,6},{5,7},{10,8},{11,9},{8,1... | collective-permute-start | bytes 393224 | tf_op jit(solution)/shard_map/ppermute | solution.py:677
  9.3 10.4 %collective-permute-start.3 = (f32[8,2,8,128]{3,2,1,0:T(8,128)S(1)}, f32[8,2,8,128]{3,2,1,0:T(8,128)S(1)}, u32[]{:S(2)}, u32[]{:S(2)}) collective-permute-start(f32[8,2,8,128]{3,2,1,0:T(8,128)S(1)} %get-tuple-element.50), channel_id=1, source_target_pairs={{6,0},{7,1},{4,2},{5,3},{2,4},{3,5},{0,6},{1,7},{14,8},{15,9},{12,... | collective-permute-start | bytes 196616 | tf_op jit(solution)/shard_map/ppermute | solution.py:677
  12.4 7.3 %collective-permute-start.4 = (f32[8,2,8,128]{3,2,1,0:T(8,128)S(1)}, f32[8,2,8,128]{3,2,1,0:T(8,128)S(1)}, u32[]{:S(2)}, u32[]{:S(2)}) collective-permute-start(f32[8,2,8,128]{3,2,1,0:T(8,128)S(1)} %get-tuple-element.51), channel_id=1, source_target_pairs={{1,0},{0,1},{3,2},{2,3},{10,4},{11,5},{8,6},{9,7},{6,8},{7,9},{4,1... | collective-permute-start | bytes 196616 | tf_op jit(solution)/shard_map/ppermute | solution.py:677
  25.9 8.0 %collective-permute-start.5 = (f32[16,2,8,128]{3,2,1,0:T(8,128)S(1)}, f32[16,2,8,128]{3,2,1,0:T(8,128)S(1)}, u32[]{:S(2)}, u32[]{:S(2)}) collective-permute-start(f32[16,2,8,128]{3,2,1,0:T(8,128)S(1)} %get-tuple-element.71), channel_id=1, source_target_pairs={{4,0},{5,1},{6,2},{7,3},{0,4},{1,5},{2,6},{3,7},{12,8},{13,9},{14,... | collective-permute-start | bytes 393224 | tf_op jit(solution)/shard_map/ppermute | solution.py:671
  28.6 5.2 %collective-permute-start.6 = (f32[16,2,8,128]{3,2,1,0:T(8,128)S(1)}, f32[16,2,8,128]{3,2,1,0:T(8,128)S(1)}, u32[]{:S(2)}, u32[]{:S(2)}) collective-permute-start(f32[16,2,8,128]{3,2,1,0:T(8,128)S(1)} %get-tuple-element.72), channel_id=1, source_target_pairs={{1,0},{0,1},{3,2},{2,3},{8,4},{9,5},{10,6},{11,7},{4,8},{5,9},{6,1... | collective-permute-start | bytes 393224 | tf_op jit(solution)/shard_map/ppermute | solution.py:671
  28.6 5.2 %collective-permute-start.7 = (f32[8,8,128]{2,1,0:T(8,128)S(1)}, f32[8,8,128]{2,1,0:T(8,128)S(1)}, u32[]{:S(2)}, u32[]{:S(2)}) collective-permute-start(f32[8,8,128]{2,1,0:T(8,128)S(1)} %get-tuple-element.73), channel_id=1, source_target_pairs={{2,0},{3,1},{0,2},{1,3},{6,4},{7,5},{4,6},{5,7},{10,8},{11,9},{8,1... | collective-permute-start | bytes 98312 | tf_op jit(solution)/shard_map/ppermute | solution.py:677
  29.2 4.7 %collective-permute-start.8 = (f32[4,8,128]{2,1,0:T(8,128)S(1)}, f32[4,8,128]{2,1,0:T(8,128)S(1)}, u32[]{:S(2)}, u32[]{:S(2)}) collective-permute-start(f32[4,8,128]{2,1,0:T(8,128)S(1)} %get-tuple-element.74), channel_id=1, source_target_pairs={{6,0},{7,1},{4,2},{5,3},{2,4},{3,5},{0,6},{1,7},{14,8},{15,9},{12,... | collective-permute-start | bytes 49160 | tf_op jit(solution)/shard_map/ppermute | solution.py:677
  32.1 1.7 %collective-permute-start.9 = (f32[4,8,128]{2,1,0:T(8,128)S(1)}, f32[4,8,128]{2,1,0:T(8,128)S(1)}, u32[]{:S(2)}, u32[]{:S(2)}) collective-permute-start(f32[4,8,128]{2,1,0:T(8,128)S(1)} %get-tuple-element.75), channel_id=1, source_target_pairs={{1,0},{0,1},{3,2},{2,3},{10,4},{11,5},{8,6},{9,7},{6,8},{7,9},{4,1... | collective-permute-start | bytes 49160 | tf_op jit(solution)/shard_map/ppermute | solution.py:677
  39.4 3.4 %collective-permute-start.12 = (f32[1,4224]{1,0:T(1,128)S(1)}, f32[1,4224]{1,0:T(1,128)S(1)}, u32[]{:S(2)}, u32[]{:S(2)}) collective-permute-start(f32[1,4224]{1,0:T(1,128)S(1)} %get-tuple-element.86), channel_id=1, source_target_pairs={{0,3},{1,2},{2,1},{3,0},{4,7},{5,6},{6,5},{7,4},{8,11},{9,10},{10,... | collective-permute-start | bytes 50696 | tf_op jit(solution)/shard_map/ppermute | solution.py:698
  39.6 3.7 %collective-permute-start.11 = (f32[1,4224]{1,0:T(1,128)S(1)}, f32[1,4224]{1,0:T(1,128)S(1)}, u32[]{:S(2)}, u32[]{:S(2)}) collective-permute-start(f32[1,4224]{1,0:T(1,128)S(1)} %get-tuple-element.86), channel_id=1, source_target_pairs={{0,2},{1,3},{2,0},{3,1},{4,6},{5,7},{6,4},{7,5},{8,10},{9,11},{10,... | collective-permute-start | bytes 50696 | tf_op jit(solution)/shard_map/ppermute | solution.py:698
  41.0 2.4 %collective-permute-start.10 = (f32[1,4224]{1,0:T(1,128)S(1)}, f32[1,4224]{1,0:T(1,128)S(1)}, u32[]{:S(2)}, u32[]{:S(2)}) collective-permute-start(f32[1,4224]{1,0:T(1,128)S(1)} %get-tuple-element.86), channel_id=1, source_target_pairs={{0,1},{1,0},{2,3},{3,2},{4,5},{5,4},{6,7},{7,6},{8,9},{9,8},{10,11... | collective-permute-start | bytes 50696 | tf_op jit(solution)/shard_map/ppermute | solution.py:698
  43.3 5.6 %collective-permute-start.15 = (f32[1,4224]{1,0:T(1,128)S(1)}, f32[1,4224]{1,0:T(1,128)S(1)}, u32[]{:S(2)}, u32[]{:S(2)}) collective-permute-start(f32[1,4224]{1,0:T(1,128)S(1)} %add_add_fusion.value), channel_id=1, source_target_pairs={{0,12},{1,13},{2,14},{3,15},{4,8},{5,9},{6,10},{7,11},{8,4},{9,5},... | collective-permute-start | bytes 50696 | tf_op jit(solution)/shard_map/ppermute | solution.py:698
  46.0 4.6 %collective-permute-start.14 = (f32[1,4224]{1,0:T(1,128)S(1)}, f32[1,4224]{1,0:T(1,128)S(1)}, u32[]{:S(2)}, u32[]{:S(2)}) collective-permute-start(f32[1,4224]{1,0:T(1,128)S(1)} %add_add_fusion.value), channel_id=1, source_target_pairs={{0,8},{1,9},{2,10},{3,11},{4,12},{5,13},{6,14},{7,15},{8,0},{9,1},... | collective-permute-start | bytes 50696 | tf_op jit(solution)/shard_map/ppermute | solution.py:698
  47.7 3.7 %collective-permute-start.13 = (f32[1,4224]{1,0:T(1,128)S(1)}, f32[1,4224]{1,0:T(1,128)S(1)}, u32[]{:S(2)}, u32[]{:S(2)}) collective-permute-start(f32[1,4224]{1,0:T(1,128)S(1)} %add_add_fusion.value), channel_id=1, source_target_pairs={{0,4},{1,5},{2,6},{3,7},{4,0},{5,1},{6,2},{7,3},{8,12},{9,13},{10,... | collective-permute-start | bytes 50696 | tf_op jit(solution)/shard_map/ppermute | solution.py:698
